TPU v7x, 32 devices: a whole 2x2x4 slice. The times are simulated.
32 devices in a mesh: row: 4 (over z), col: 8 (over y, x, core).
Axes of the slice: x: 2, y: 2, z: 4, core: 2. Of those that a mesh axis runs over, the one named last changes fastest.
Arguments:
- inverse_first: float32 [512, 512], P('row'), may hold values from -0.4 to 2
- inverse_second: float32 [512, 512], P('row'), may hold values from -0.4 to 2
- coupling: float32 [512, 512], P('row'), may hold values from -0.25 to 0.25
- panel_first: float32 [16384, 512], P('row', 'col'), may hold values from -0.1875 to 0.1875
- panel_second: float32 [16384, 512], P('row', 'col'), may hold values from -0.1875 to 0.1875
- rhs_first: float32 [512, 2048], P('row', 'col'), may hold values from -6 to 6
- rhs_second: float32 [512, 2048], P('row', 'col'), may hold values from -6 to 6
- rhs_rest: float32 [16384, 2048], P('row', 'col'), may hold values from -6 to 6
Outputs:
- solved_first: float32 [512, 2048], P('row', 'col')
- solved_second: float32 [512, 2048], P('row', 'col')
- updated: float32 [16384, 2048], P('row', 'col')
All inputs are finite; a program needn't handle non-finite values.
Results may differ from a plain program's by a relative error of at most 0.00011.
Values sent between devices are 32-bit elements; how exact they have to be, the bound alone decides.
No kernel may reach another device: no remote copies, remote signals or barrier semaphores. Data moves between devices by JAX's collectives and lax.ppermute only.
A program may use at most 64 MiB of HBM per device.

v0:
```python
import jax
import jax.numpy as jnp
from jax import lax
from jax.sharding import PartitionSpec as P


def product(left, right):
    return jnp.dot(left, right, precision=lax.Precision.HIGHEST, preferred_element_type=jnp.float32)


def per_device(
    inverse_first,
    inverse_second,
    coupling,
    panel_first,
    panel_second,
    rhs_first,
    rhs_second,
    rhs_rest,
):

    def apply_inverse(matrix, piece):
        return product(matrix, piece)

    solved_first = apply_inverse(
        inverse_first, lax.all_gather(rhs_first, "row", axis=0, tiled=True)
    )
    first_full = lax.all_gather(solved_first, "row", axis=0, tiled=True)
    reduced = rhs_second - product(coupling, first_full)
    solved_second = apply_inverse(
        inverse_second, lax.all_gather(reduced, "row", axis=0, tiled=True)
    )
    second_full = lax.all_gather(solved_second, "row", axis=0, tiled=True)
    updated = (
        rhs_rest
        - product(lax.all_gather(panel_first, "col", axis=1, tiled=True), first_full)
        - product(lax.all_gather(panel_second, "col", axis=1, tiled=True), second_full)
    )
    return (solved_first, solved_second, updated)


def solution(mesh):
    in_specs = (
        P("row", None),
        P("row", None),
        P("row", None),
        P("row", "col"),
        P("row", "col"),
        P("row", "col"),
        P("row", "col"),
        P("row", "col"),
    )
    out_specs = (P("row", "col"), P("row", "col"), P("row", "col"))
    return jax.shard_map(
        per_device, mesh=mesh, in_specs=in_specs, out_specs=out_specs, check_vma=False
    )
```

profile of v0, /device:TPU:0, one launch (start us, length us, event | category | flops | bytes accessed | tf_op | source)
XLA Modules:
  0.0 147.5 jit_solution(327663597991277486)
XLA Ops:
  7.2 0.0 copy-start
  7.2 0.0 copy-start.4
  7.2 0.0 copy-start.3
  7.2 0.0 copy-start.2
  7.2 0.0 all-gather.3.cloned.1.call-start
  7.3 0.7 all-gather.3.cloned.1.call-update
  7.9 0.0 all-gather.5.cloned.1.call-start
  8.0 0.7 all-gather.5.cloned.1.call-update
  8.7 17.6 %all_gather.18 = f32[512,256]{1,0:T(8,128)S(1)} all-gather(f32[128,256]{1,0:T(8,128)} %param.13), channel_id=1, replica_groups=mesh['row'=4,'col'=8] {'row'}, dimensions={0}, use_global_device_ids=true | all-gather | bytes 655360 | tf_op jit(solution)/shard_map/all_gather | solution.py:26
  26.3 0.0 copy-done
  26.3 0.4 fusion.3
  26.7 0.0 copy-start.1
  26.7 16.3 %all_gather.19 = f32[512,256]{1,0:T(8,128)S(1)} all-gather(f32[128,256]{1,0:T(8,128)S(1)} %fusion.3), channel_id=1, replica_groups=mesh['row'=4,'col'=8] {'row'}, dimensions={0}, use_global_device_ids=true | all-gather | bytes 655360 | tf_op jit(solution)/shard_map/all_gather | solution.py:28
  43.0 0.0 copy-done.4
  43.0 0.0 copy-done.3
  43.0 0.4 fusion.2
  43.4 15.5 %all_gather.20 = f32[512,256]{1,0:T(8,128)S(1)} all-gather(f32[128,256]{1,0:T(8,128)S(1)} %fusion.2), channel_id=1, replica_groups=mesh['row'=4,'col'=8] {'row'}, dimensions={0}, use_global_device_ids=true | all-gather | bytes 655360 | tf_op jit(solution)/shard_map/all_gather | solution.py:31
  58.9 0.0 copy-done.2
  58.9 1.0 convolution_bitcast_fusion.2
  59.9 0.8 copy.12
  60.7 5.6 %copy.11 = f32[4096,256]{0,1:T(8,128)} copy(f32[4096,256]{1,0:T(8,128)} %param.15) | data formatting | bytes 8388608 | tf_op args[7]
  66.3 0.0 copy-done.1
  66.3 14.8 %all_gather.22 = f32[512,256]{0,1:T(8,128)S(1)} all-gather(f32[128,256]{0,1:T(8,128)S(1)} %convolution_bitcast_fusion.2), channel_id=1, replica_groups=mesh['row'=4,'col'=8] {'row'}, dimensions={0}, use_global_device_ids=true | all-gather | bytes 655360 | tf_op jit(solution)/shard_map/all_gather | solution.py:33
  81.1 0.0 all-gather.3.cloned.1.call-done
  81.1 11.5 %fusion.1 = f32[4096,256]{0,1:T(8,128)} fusion(f32[4096,256]{0,1:T(8,128)} %copy.11, f32[512,256]{1,0:T(8,128)S(1)} %all_gather.19, f32[4096,512]{0,1:T(8,128)} %all-gather.3.cloned.1.call-done), kind=kOutput, calls=%fused_computation.3 | convolution fusion | flops 6443499520 | bytes 17301504 | tf_op jit(solution)/shard_map/dot_general | solution.py:8
  92.6 30.8 %all-gather.5.cloned.1.call-done = f32[4096,512]{0,1:T(8,128)} async-done(((f32[4096,64]{0,1:T(8,128)}), f32[4096,512]{0,1:T(8,128)}) %all-gather.5.cloned.1.call-update) | async-done | bytes 8388624 | tf_op jit(solution)/shard_map/all_gather | solution.py:37
  123.4 11.7 %fusion = f32[4096,256]{0,1:T(8,128)} fusion(f32[4096,256]{0,1:T(8,128)} %fusion.1, f32[512,256]{0,1:T(8,128)S(1)} %all_gather.22, f32[4096,512]{0,1:T(8,128)} %all-gather.5.cloned.1.call-done), kind=kOutput, calls=%fused_computation.1 | convolution fusion | flops 6443499520 | bytes 17301504 | tf_op jit(solution)/shard_map/dot_general | solution.py:8
  135.0 5.6 %copy.13 = f32[4096,256]{1,0:T(8,128)} copy(f32[4096,256]{0,1:T(8,128)} %fusion) | data formatting | bytes 8388608
Async XLA Ops:
  7.2 19.1 %copy-start = (f32[128,512]{1,0:T(8,128)S(1)}, f32[128,512]{1,0:T(8,128)}, u32[]{:S(2)}) copy-start(f32[128,512]{1,0:T(8,128)} %param.8) | copy-start | bytes 786436
  7.2 35.8 %copy-start.4 = (f32[128,256]{1,0:T(8,128)S(1)}, f32[128,256]{1,0:T(8,128)}, u32[]{:S(2)}) copy-start(f32[128,256]{1,0:T(8,128)} %param.14) | copy-start | bytes 393220
  7.2 35.8 %copy-start.3 = (f32[128,512]{1,0:T(8,128)S(1)}, f32[128,512]{1,0:T(8,128)}, u32[]{:S(2)}) copy-start(f32[128,512]{1,0:T(8,128)} %param.10) | copy-start | bytes 786436
  7.2 51.7 %copy-start.2 = (f32[128,512]{1,0:T(8,128)S(1)}, f32[128,512]{1,0:T(8,128)}, u32[]{:S(2)}) copy-start(f32[128,512]{1,0:T(8,128)} %param.9) | copy-start | bytes 786436
  7.2 73.9 %all-gather.3.cloned.1.call-start = ((), (), s32[]{:S(2)}) async-start(), calls=%async_computation | async-start | bytes 9437184 | tf_op jit(solution)/shard_map/all_gather | solution.py:36
  7.9 115.4 %all-gather.5.cloned.1.call-start = ((), (), s32[]{:S(2)}) async-start(), calls=%async_computation.1 | async-start | bytes 9437184 | tf_op jit(solution)/shard_map/all_gather | solution.py:37
  26.7 39.6 %copy-start.1 = (f32[128,256]{1,0:T(8,128)}, f32[128,256]{1,0:T(8,128)S(1)}, u32[]{:S(2)}) copy-start(f32[128,256]{1,0:T(8,128)S(1)} %fusion.3) | copy-start | bytes 393220
Sparse Core Ops, SparseCore 0:
  9.9 57.0 all-gather.2
  68.9 54.3 all-gather.4
where the time goes:
time: 148 us; the launch traced here: 147 us
  blocking collectives  64.1 us (43%)
  waiting for transfers between devices  32.1 us (22%)
  matrix products  25 us (17%)
  between operations  14.1 us (10%)
  local copies, waits for them, and re-layouts  12 us (8%)
    all_gather x1, waiting for transfers between devices, per_device(): lax.all_gather(panel_second, 'col', axis=1, tiled=True)  30.8 us
    dot_general x5, matrix products, product(): jnp.dot(left, right, precision=lax.Precision.HIGHEST, preferred_element_t...  25 us
    all_gather x1, blocking collectives, per_device(): lax.all_gather(rhs_first, 'row', axis=0, tiled=True)  17.6 us
    all_gather x1, blocking collectives, per_device(): first_full = lax.all_gather(solved_first, 'row', axis=0, tiled=True)  16.3 us
    all_gather x1, blocking collectives, per_device(): lax.all_gather(reduced, 'row', axis=0, tiled=True)  15.5 us
    all_gather x1, blocking collectives, per_device(): second_full = lax.all_gather(solved_second, 'row', axis=0, tiled=True)  14.8 us
    unnamed x13, local copies, waits for them, and re-layouts  12 us
  transfers between devices with their start and end apart: 2, of which 1 were waited for; matrix products, arithmetic and copies ran while one was open for 13% of the time, Pallas kernels for 0%

commit v1 on v0

v1 whole, which is shorter than its diff:
```python
import functools

import jax
import jax.numpy as jnp
from jax import lax
from jax.experimental import pallas as pl
from jax.experimental.pallas import tpu as pltpu
from jax.sharding import PartitionSpec as P

VMEM_BYTES = 24 * 2**20
INNER = 8
CORE, ACROSS, UP = 1, 2, 4
FIRST, SECOND = 0, 1
GROUPS = (
    (
        (FIRST, 0), (FIRST, CORE), (SECOND, 0), (SECOND, CORE),
        (FIRST, UP), (FIRST, UP | CORE), (SECOND, ACROSS), (SECOND, ACROSS | CORE),
    ),
    ((FIRST, ACROSS), (FIRST, ACROSS | CORE), (SECOND, UP), (SECOND, UP | CORE)),
    (
        (FIRST, ACROSS | UP), (FIRST, ACROSS | UP | CORE),
        (SECOND, ACROSS | UP), (SECOND, ACROSS | UP | CORE),
    ),
)


def split(value):
    high = value.astype(jnp.bfloat16)
    return high, (value - high.astype(jnp.float32)).astype(jnp.bfloat16)


def product(left, right, contract=1):
    def one(a, b):
        return lax.dot_general(
            a, b, (((contract,), (0,)), ((), ())), preferred_element_type=jnp.float32
        )

    return one(left[0], right[0]) + one(left[0], right[1]) + one(left[1], right[0])


def pack_kernel(*refs):
    (*matrices, first, second), out = refs[:-1], refs[-1]
    rows, width = first.shape
    even = lax.rem(lax.axis_index("col"), 2) == 0
    for k, ref in enumerate(matrices):
        out[k * rows : (k + 1) * rows, :] = jnp.where(even, ref[:, :width], ref[:, width:])
    out[3 * rows : 4 * rows, :] = first[...]
    out[4 * rows :, :] = second[...]


def pack_rows(own):
    rows, width = own[3].shape
    whole = pl.BlockSpec(memory_space=pltpu.VMEM)
    return pl.pallas_call(
        pack_kernel,
        out_shape=jax.ShapeDtypeStruct((5 * rows, width), jnp.float32),
        in_specs=[whole] * 5,
        out_specs=whole,
        cost_estimate=pl.CostEstimate(flops=0, bytes_accessed=0, transcendentals=0),
    )(*own)


def solve_kernel(steps, block, *refs):
    own, refs = refs[:5], refs[5:]
    pieces, (others, *refs) = refs[: steps - 1], refs[steps - 1 :]
    outs, (first_out, second_out, *scratch) = refs[: 2 * len(GROUPS)], refs[2 * len(GROUPS) :]
    matrices, right_first, right_second, solved = scratch
    here = lax.axis_index("row")
    lane = lax.axis_index("col")
    even = lax.rem(lane, 2) == 0
    rows, width = own[3].shape[0], matrices.shape[2] // 2

    def at(step):
        return pl.ds(pl.multiple_of(lax.rem(here + steps - step, steps) * rows, rows), rows)

    for k in range(3):
        matrices[k, at(0), :] = own[k][...]
    right_first[at(0), :] = own[3][...]
    right_second[at(0), :] = own[4][...]
    for j, piece in enumerate(pieces):
        right_first[at(j + 1), :] = piece[3 * rows : 4 * rows, :]
        right_second[at(j + 1), :] = piece[4 * rows :, :]
        for k in range(3):
            mine = piece[k * rows : (k + 1) * rows, :]
            other = others[(3 * j + k) * rows : (3 * j + k + 1) * rows, :]
            matrices[k, at(j + 1), :width] = jnp.where(even, mine, other)
            matrices[k, at(j + 1), width:] = jnp.where(even, other, mine)
    solved[0] = product(split(matrices[0]), split(right_first[...]))
    reduced = right_second[...] - product(split(matrices[2]), split(solved[0]))
    solved[1] = product(split(matrices[1]), split(reduced))
    first_out[...] = solved[0, at(0), :]
    second_out[...] = solved[1, at(0), :]

    inner = lax.rem(lane, INNER)
    outer = solved.shape[1] // (INNER * block)
    for group, (high_out, low_out) in zip(GROUPS, zip(outs[::2], outs[1::2])):
        to = 0
        for part, m in group:
            which = lax.bitwise_xor(inner, m)
            for o in range(outer):
                start = pl.multiple_of((o * INNER + which) * block, block)
                high, low = split(solved[part, pl.ds(start, block), :])
                high_out[to : to + block, :] = high
                low_out[to : to + block, :] = low
                to += block


def solve(steps, block, own, pieces, others):
    rows, width = own[3].shape
    depth = rows * steps
    outs = [
        jax.ShapeDtypeStruct((len(group) * depth // INNER, width), jnp.bfloat16)
        for group in GROUPS
        for _ in range(2)
    ]
    outs += [jax.ShapeDtypeStruct((rows, width), jnp.float32)] * 2
    whole = pl.BlockSpec(memory_space=pltpu.VMEM)
    operands = [*own, *pieces, others]
    return pl.pallas_call(
        functools.partial(solve_kernel, steps, block),
        out_shape=outs,
        in_specs=[whole] * len(operands),
        out_specs=[whole] * len(outs),
        scratch_shapes=[
            pltpu.VMEM((3, depth, depth), jnp.float32),
            pltpu.VMEM((depth, width), jnp.float32),
            pltpu.VMEM((depth, width), jnp.float32),
            pltpu.VMEM((2, depth, width), jnp.float32),
        ],
        compiler_params=pltpu.CompilerParams(vmem_limit_bytes=VMEM_BYTES),
        cost_estimate=pl.CostEstimate(flops=0, bytes_accessed=0, transcendentals=0),
    )(*operands)


def turn_kernel(count, *refs):
    panels, (high, low) = refs[:count], refs[count:]
    high[...], low[...] = split(jnp.concatenate([ref[...] for ref in panels], axis=0).T)


def turn(panels):
    rows, depth = panels[0].shape[1], sum(p.shape[0] for p in panels)
    tile = min(rows, 1024)
    return pl.pallas_call(
        functools.partial(turn_kernel, len(panels)),
        grid=(rows // tile,),
        out_shape=[jax.ShapeDtypeStruct((rows, depth), jnp.bfloat16)] * 2,
        in_specs=[pl.BlockSpec((p.shape[0], tile), lambda i: (0, i)) for p in panels],
        out_specs=[pl.BlockSpec((tile, depth), lambda i: (i, 0))] * 2,
        compiler_params=pltpu.CompilerParams(vmem_limit_bytes=VMEM_BYTES),
        cost_estimate=pl.CostEstimate(flops=0, bytes_accessed=0, transcendentals=0),
    )(*panels)


def update_kernel(count, *refs):
    before, after = refs[4 * count :]
    total = before[...]
    for j in range(count):
        a, b, c, d = (ref[...] for ref in refs[4 * j : 4 * j + 4])
        total = total - product((a, b), (c, d))
    after[...] = total


def update(pairs, before, in_place=False):
    rows, width = pairs[0][0][0].shape[0], before.shape[1]
    tile = min(rows, 512)
    panel = [pl.BlockSpec((tile, left[0].shape[1]), lambda i: (i, 0)) for left, _ in pairs]
    factor = [pl.BlockSpec(right[0].shape, lambda i: (0, 0)) for _, right in pairs]
    depth = sum(left[0].shape[1] for left, _ in pairs)
    return pl.pallas_call(
        functools.partial(update_kernel, len(pairs)),
        grid=(rows // tile,),
        out_shape=jax.ShapeDtypeStruct(before.shape, jnp.float32),
        in_specs=[x for p, f in zip(panel, factor) for x in (p, p, f, f)]
        + [pl.BlockSpec((tile, width), lambda i: (i, 0))],
        out_specs=pl.BlockSpec((tile, width), lambda i: (i, 0)),
        input_output_aliases={4 * len(pairs): 0} if in_place else {},
        compiler_params=pltpu.CompilerParams(vmem_limit_bytes=VMEM_BYTES),
        cost_estimate=pl.CostEstimate(flops=0, bytes_accessed=0, transcendentals=0),
    )(*[x for left, right in pairs for x in (*left, *right)], before)


def finish_kernel(count, *refs):
    panels, (high, low, before, after) = refs[:count], refs[count:]
    panel = jnp.concatenate([ref[...] for ref in panels], axis=0)
    after[...] = before[...] - product(split(panel), (high[...], low[...]), contract=0)


def finish(panels, factor, before, start):
    count, rows, depth = len(panels), panels[0].shape[1], sum(p.shape[0] for p in panels)
    width = before.shape[1]
    tile = min(rows, 512)
    first = start // tile
    return pl.pallas_call(
        functools.partial(finish_kernel, count),
        grid=(rows // tile,),
        out_shape=jax.ShapeDtypeStruct(before.shape, jnp.float32),
        in_specs=[pl.BlockSpec((p.shape[0], tile), lambda i: (0, i)) for p in panels]
        + [pl.BlockSpec(f.shape, lambda i: (0, 0)) for f in factor]
        + [pl.BlockSpec((tile, width), lambda i: (i + first, 0))],
        out_specs=pl.BlockSpec((tile, width), lambda i: (i + first, 0)),
        input_output_aliases={count + 2: 0},
        compiler_params=pltpu.CompilerParams(vmem_limit_bytes=VMEM_BYTES),
        cost_estimate=pl.CostEstimate(flops=0, bytes_accessed=0, transcendentals=0),
    )(*panels, *factor, before)


def solution(mesh):
    row_count, col_count = mesh.shape["row"], mesh.shape["col"]

    def swap(value, bit):
        return lax.ppermute(value, "col", [(i, i ^ bit) for i in range(col_count)])

    def shift(value, by):
        return lax.ppermute(value, "row", [(i, (i + by) % row_count) for i in range(row_count)])

    def per_device(
        inverse_first, inverse_second, coupling, panel_first, panel_second,
        rhs_first, rhs_second, rhs_rest,
    ):
        first, second = panel_first.T, panel_second.T
        block = first.shape[0]
        if col_count > INNER:
            groups = [list(range(i, col_count, INNER)) for i in range(INNER)]
            first, second = (
                lax.all_gather(p, "col", axis=0, tiled=True, axis_index_groups=groups)
                for p in (first, second)
            )
        rest = first.shape[1]

        own = (inverse_first, inverse_second, coupling, rhs_first, rhs_second)
        def both(pair, bits=(ACROSS, UP)):
            return tuple(swap(x, bit) for x, bit in zip(pair, bits))

        def beside(pair):
            return both(pair, (CORE, CORE))

        def after(values, *tokens):
            return lax.optimization_barrier((values, tokens))[0]

        near_0 = both((second, first))
        near_1 = both((first, second))
        own_beside = beside((first, second))
        pack = pack_rows(own)
        packs = {1: shift(pack, 1)}
        for j in range(2, row_count // 2 + 1):
            packs[j] = shift(packs[j - 1], 1)
        for j in range(row_count - 1, row_count // 2, -1):
            packs[j] = shift(packs[j + 1] if j < row_count - 1 else after(pack, packs[1]), -1)
        packs = [packs[j] for j in range(1, row_count)]
        beside_0 = beside(after(near_0, own_beside))
        beside_1 = beside(after(near_1, beside_0))
        cuts = [0, 5 * rest // 8, rest]
        far = [
            both(after((near_0[1][:, a:b], near_0[0][:, a:b]), near_1))
            for a, b in zip(cuts[:-1], cuts[1:])
        ]
        turned_0 = turn(
            [first, own_beside[0], second, own_beside[1], near_0[1], beside_0[1], near_0[0], beside_0[0]]
        )
        turned_1 = turn([near_1[0], beside_1[0], near_1[1], beside_1[1]])

        matrix_rows = 3 * rhs_first.shape[0]
        others = swap(jnp.concatenate([p[:matrix_rows] for p in packs], axis=0), CORE)
        *factors, solved_first, solved_second = solve(row_count, block, own, packs, others)
        factors = list(zip(factors[::2], factors[1::2]))
        updated = update([(turned_0, factors[0]), (turned_1, factors[1])], rhs_rest)
        for start, pair in zip(cuts, far):
            pair = after(pair, updated)
            other = beside(pair)
            updated = finish([pair[0], other[0], pair[1], other[1]], factors[2], updated, start)
        return solved_first, solved_second, updated

    in_specs = (P("row", None),) * 3 + (P("row", "col"),) * 5
    return jax.shard_map(
        per_device, mesh=mesh, in_specs=in_specs, out_specs=(P("row", "col"),) * 3, check_vma=False
    )
```

time: 148 us -> 95.2 us (0.64)
  blocking collectives: 64.1 us -> 0 us
  Pallas kernels: 0 us -> 27 us
  matrix products: 25 us -> 0 us
  starting transfers between devices: 0.08 us -> 19.2 us
  waiting for transfers between devices: 32.1 us -> 47.1 us
  between operations: 14.1 us -> 0.85 us
  local copies, waits for them, and re-layouts: 12 us -> 0.7 us
    all_gather x4 -> x0, blocking collectives: 64.1 us -> none  [the longest x1 17.6 us: per_device(): lax.all_gather(rhs_first, 'row', axis=0, tiled=True)]
    ppermute x0 -> x22, waiting for transfers between devices: none -> 47.1 us  [the longest x3 31.2 us: shift(): lax.ppermute(value, 'row', [(i, (i + by) % row_count) for i in range(row_...]
    all_gather x2 -> x0, waiting for transfers between devices: 30.8 us -> none  [the longest x1 30.8 us: per_device(): lax.all_gather(panel_second, 'col', axis=1, tiled=True)]
    pallas_call x0 -> x7, Pallas kernels: none -> 27 us  [the longest x2 9.57 us: finish(): pl.pallas_call(functools.partial(finish_kernel, count), grid=(rows // til...]
    dot_general x5 -> x0, matrix products: 25 us -> none  [product(): jnp.dot(left, right, precision=lax.Precision.HIGHEST, preferred_element_t...]
    ppermute x0 -> x22, starting transfers between devices: none -> 19.2 us  [the longest x19 12.8 us: swap(): return lax.ppermute(value, 'col', [(i, i ^ bit) for i in range(col_count)])]
    unnamed x13 -> x16, local copies, waits for them, and re-layouts: 12 us -> 0.48 us
  transfers between devices with their start and end apart: 2 -> 22, of which waited for: 1 -> 10; matrix products, arithmetic and copies ran while one was open for 13% -> 0% of each run, Pallas kernels for 0% -> 22%
where the time goes in v1:
time: 95.2 us; the launch traced here: 94.9 us
  waiting for transfers between devices  47.1 us (49%)
  Pallas kernels  27 us (28%)
  starting transfers between devices  19.2 us (20%)
    ppermute x3, waiting for transfers between devices, shift(): lax.ppermute(value, 'row', [(i, (i + by) % row_count) for i in range(row_...  31.2 us
    ppermute x19, waiting for transfers between devices, swap(): return lax.ppermute(value, 'col', [(i, i ^ bit) for i in range(col_count)])  15.9 us
    ppermute x19, starting transfers between devices, swap(): return lax.ppermute(value, 'col', [(i, i ^ bit) for i in range(col_count)])  12.8 us
    pallas_call x2, Pallas kernels, finish(): pl.pallas_call(functools.partial(finish_kernel, count), grid=(rows // til...  9.57 us
    pallas_call x1, Pallas kernels, update(): pl.pallas_call(functools.partial(update_kernel, len(pairs)), grid=(rows /...  7.12 us
    ppermute x3, starting transfers between devices, shift(): lax.ppermute(value, 'row', [(i, (i + by) % row_count) for i in range(row_...  6.34 us
    pallas_call x2, Pallas kernels, turn(): pl.pallas_call(functools.partial(turn_kernel, len(panels)), grid=(rows //...  4.84 us
    pallas_call x1, Pallas kernels, solve(): pl.pallas_call(functools.partial(solve_kernel, steps, block), out_shape=o...  3.41 us
  transfers between devices with their start and end apart: 22, of which 10 were waited for; matrix products, arithmetic and copies ran while one was open for 0% of the time, Pallas kernels for 22%

profile of v1, /device:TPU:0, one launch (start us, length us, event | category | flops | bytes accessed | tf_op | source)
XLA Modules:
  0.0 94.9 jit_solution(2974466719981719857)
XLA Ops:
  0.6 2.1 %shard_map.103 = f32[640,256]{1,0:T(8,128)} custom-call(f32[128,512]{1,0:T(8,128)} %refs_0_.3, f32[128,512]{1,0:T(8,128)} %refs_1_.3, f32[128,512]{1,0:T(8,128)} %refs_2_.3, f32[128,256]{1,0:T(8,128)} %refs_3_.3, f32[128,256]{1,0:T(8,128)} %refs_4_.3), custom_call_target="tpu_custom_call" | custom-call | tf_op jit(solution)/shard_map/pallas_call | solution.py:54
  2.7 3.0 %collective-permute-start = (f32[640,256]{1,0:T(8,128)}, f32[640,256]{1,0:T(8,128)S(1)}, u32[]{:S(2)}, u32[]{:S(2)}) collective-permute-start(f32[640,256]{1,0:T(8,128)} %shard_map.103), channel_id=1, source_target_pairs={{0,8},{8,16},{16,24},{24,0},{1,9},{9,17},{17,25},{25,1},{2,10},{10... | collective-permute-start | bytes 1966088 | tf_op jit(solution)/shard_map/ppermute | solution.py:214
  5.8 1.5 %collective-permute-start.4 = (f32[64,4096]{1,0:T(8,128)}, f32[64,4096]{1,0:T(8,128)S(1)}, u32[]{:S(2)}, u32[]{:S(2)}) collective-permute-start(f32[64,4096]{1,0:T(8,128)} %bitcast.2), channel_id=1, source_target_pairs={{0,4},{1,5},{2,6},{3,7},{4,0},{5,1},{6,2},{7,3},{8,12},{9,13},{10,... | collective-permute-start | bytes 3145736 | tf_op jit(solution)/shard_map/ppermute | solution.py:211
  7.3 1.5 %collective-permute-start.5 = (f32[64,4096]{1,0:T(8,128)}, f32[64,4096]{1,0:T(8,128)S(1)}, u32[]{:S(2)}, u32[]{:S(2)}) collective-permute-start(f32[64,4096]{1,0:T(8,128)} %bitcast.6), channel_id=1, source_target_pairs={{0,2},{1,3},{2,0},{3,1},{4,6},{5,7},{6,4},{7,5},{8,10},{9,11},{10,... | collective-permute-start | bytes 3145736 | tf_op jit(solution)/shard_map/ppermute | solution.py:211
  8.8 0.0 collective-permute-start.12
  8.8 0.5 collective-permute-start.13
  9.3 13.4 %collective-permute-done.refs_5_ = f32[640,256]{1,0:T(8,128)S(1)} collective-permute-done((f32[640,256]{1,0:T(8,128)}, f32[640,256]{1,0:T(8,128)S(1)}, u32[]{:S(2)}, u32[]{:S(2)}) %collective-permute-start) | collective-permute-done | bytes 655392 | tf_op jit(solution)/shard_map/ppermute | solution.py:214
  22.7 1.7 %collective-permute-start.2 = (f32[640,256]{1,0:T(8,128)}, f32[640,256]{1,0:T(8,128)S(1)}, u32[]{:S(2)}, u32[]{:S(2)}) collective-permute-start(f32[640,256]{1,0:T(8,128)} %shard_map.103), channel_id=1, source_target_pairs={{0,24},{8,0},{16,8},{24,16},{1,25},{9,1},{17,9},{25,17},{2,26},{10... | collective-permute-start | bytes 1966088 | tf_op jit(solution)/shard_map/ppermute | solution.py:214
  24.5 6.1 %collective-permute-done.4.refs_4_ = f32[64,4096]{1,0:T(8,128)S(1)} collective-permute-done((f32[64,4096]{1,0:T(8,128)}, f32[64,4096]{1,0:T(8,128)S(1)}, u32[]{:S(2)}, u32[]{:S(2)}) %collective-permute-start.4) | collective-permute-done | bytes 1048608 | tf_op jit(solution)/shard_map/ppermute | solution.py:211
  30.6 1.6 %collective-permute-start.1 = (f32[640,256]{1,0:T(8,128)S(1)}, f32[640,256]{1,0:T(8,128)S(1)}, u32[]{:S(2)}, u32[]{:S(2)}) collective-permute-start(f32[640,256]{1,0:T(8,128)S(1)} %collective-permute-done.refs_5_), channel_id=1, source_target_pairs={{0,8},{8,16},{16,24},{24,0},{1,9},{9,17},{17,25},{25,1},{2,10},{10... | collective-permute-start | bytes 1966088 | tf_op jit(solution)/shard_map/ppermute | solution.py:214
  32.2 0.0 collective-permute-done.5.refs_6_
  32.2 1.5 %collective-permute-start.6 = (f32[64,4096]{1,0:T(8,128)}, f32[64,4096]{1,0:T(8,128)S(1)}, u32[]{:S(2)}, u32[]{:S(2)}) collective-permute-start(f32[64,4096]{1,0:T(8,128)} %bitcast.4), channel_id=1, source_target_pairs={{0,2},{1,3},{2,0},{3,1},{4,6},{5,7},{6,4},{7,5},{8,10},{9,11},{10,... | collective-permute-start | bytes 3145736 | tf_op jit(solution)/shard_map/ppermute | solution.py:211
  33.7 0.0 collective-permute-done.12.refs_1_
  33.7 1.5 %collective-permute-start.7 = (f32[64,4096]{1,0:T(8,128)}, f32[64,4096]{1,0:T(8,128)S(1)}, u32[]{:S(2)}, u32[]{:S(2)}) collective-permute-start(f32[64,4096]{1,0:T(8,128)} %bitcast.8), channel_id=1, source_target_pairs={{0,4},{1,5},{2,6},{3,7},{4,0},{5,1},{6,2},{7,3},{8,12},{9,13},{10,... | collective-permute-start | bytes 3145736 | tf_op jit(solution)/shard_map/ppermute | solution.py:211
  35.2 0.0 collective-permute-done.13.refs_3_
  35.2 0.0 collective-permute-start.14
  35.2 17.7 %collective-permute-done.2.refs_7_ = f32[640,256]{1,0:T(8,128)S(1)} collective-permute-done((f32[640,256]{1,0:T(8,128)}, f32[640,256]{1,0:T(8,128)S(1)}, u32[]{:S(2)}, u32[]{:S(2)}) %collective-permute-start.2) | collective-permute-done | bytes 655392 | tf_op jit(solution)/shard_map/ppermute | solution.py:214
  52.9 0.0 collective-permute-start.15
  53.0 0.0 collective-permute-done.1.refs_6_
  53.0 0.0 copy-start.4
  53.0 0.0 copy-start.5
  53.0 0.1 pad_maximum_fusion
  53.1 0.6 collective-permute-start.3
  53.7 2.1 %collective-permute-done.6.refs_0_ = f32[64,4096]{1,0:T(8,128)S(1)} collective-permute-done((f32[64,4096]{1,0:T(8,128)}, f32[64,4096]{1,0:T(8,128)S(1)}, u32[]{:S(2)}, u32[]{:S(2)}) %collective-permute-start.6) | collective-permute-done | bytes 1048608 | tf_op jit(solution)/shard_map/ppermute | solution.py:211
  55.8 1.2 %collective-permute-done.7.refs_2_ = f32[64,4096]{1,0:T(8,128)S(1)} collective-permute-done((f32[64,4096]{1,0:T(8,128)}, f32[64,4096]{1,0:T(8,128)S(1)}, u32[]{:S(2)}, u32[]{:S(2)}) %collective-permute-start.7) | collective-permute-done | bytes 1048608 | tf_op jit(solution)/shard_map/ppermute | solution.py:211
  57.0 0.0 collective-permute-done.14.refs_5_
  57.0 0.0 collective-permute-done.15.refs_7_
  57.0 0.0 collective-permute-start.16
  57.0 0.5 collective-permute-start.17
  57.6 0.0 copy-start.1
  57.7 0.0 copy-start.2
  57.7 0.0 copy-start.3
  57.7 0.0 copy-start.6
  57.7 0.0 copy-start.7
  57.7 0.6 collective-permute-start.10
  58.3 1.5 %collective-permute-start.11 = (f32[64,2560]{1,0:T(8,128)S(1)}, f32[64,2560]{1,0:T(8,128)S(1)}, u32[]{:S(2)}, u32[]{:S(2)}) collective-permute-start(f32[64,2560]{1,0:T(8,128)S(1)} %slice.34), channel_id=1, source_target_pairs={{0,4},{1,5},{2,6},{3,7},{4,0},{5,1},{6,2},{7,3},{8,12},{9,13},{10,... | collective-permute-start | bytes 1966088 | tf_op jit(solution)/shard_map/ppermute | solution.py:211
  59.8 0.0 copy-done.4
  59.8 3.1 %shard_map.105 = (bf16[4096,512]{1,0:T(8,128)(2,1)S(1)}, bf16[4096,512]{1,0:T(8,128)(2,1)S(1)}) custom-call(f32[64,4096]{1,0:T(8,128)S(1)} %bitcast.5, f32[64,4096]{1,0:T(8,128)S(1)} %collective-permute-done.12.refs_1_, f32[64,4096]{1,0:T(8,128)S(1)} %bitcast.9, f32[64,4096]{1,0:T(8,128)S(1)} %collective-permute-done.13.refs_3_, ...), custom_call_target="tpu_custom_call" | custom-call | tf_op jit(solution)/shard_map/pallas_call | solution.py:143
  62.9 0.0 collective-permute-done.3.refs_8_
  62.9 0.0 copy-done.1
  63.0 0.0 copy-done.2
  63.0 0.0 copy-done.3
  63.0 3.4 %shard_map.104 = (bf16[512,256]{1,0:T(8,128)(2,1)S(1)}, bf16[512,256]{1,0:T(8,128)(2,1)S(1)}, bf16[256,256]{1,0:T(8,128)(2,1)S(1)}, bf16[256,256]{1,0:T(8,128)(2...) custom-call(f32[128,512]{1,0:T(8,128)S(1)} %copy-done.1, ...), custom_call_target="tpu_custom_call" | custom-call | tf_op jit(solution)/shard_map/pallas_call | solution.py:119
  66.4 0.0 collective-permute-done.16.refs_1_
  66.4 0.0 collective-permute-done.17.refs_3_
  66.4 1.7 %shard_map.106 = (bf16[4096,256]{1,0:T(8,128)(2,1)S(1)}, bf16[4096,256]{1,0:T(8,128)(2,1)S(1)}) custom-call(f32[64,4096]{1,0:T(8,128)S(1)} %collective-permute-done.6.refs_0_, f32[64,4096]{1,0:T(8,128)S(1)} %collective-permute-done.16.refs_1_, f32[64,4096]{1,0:T(8,128)S(1)} %collective-permute-done.7.refs_2_, f32[64,4096]{1,0:T(8,128)S(1)} %collective-permute-done.17.refs_3_), custom_call_target="tpu_custom_call" | custom-call | tf_op jit(solution)/shard_map/pallas_call | solution.py:143
  68.2 0.4 copy-done
  68.6 7.1 %shard_map.107.refs_6_ = f32[4096,256]{1,0:T(8,128)} custom-call(bf16[4096,512]{1,0:T(8,128)(2,1)S(1)} %get-tuple-element.37.refs_0_, bf16[4096,512]{1,0:T(8,128)(2,1)S(1)} %get-tuple-element.38.refs_1_, bf16[512,256]{1,0:T(8,128)(2,1)S(1)} %get-tuple-element.39.refs_2_, bf16[512,256]{1,0:T(8,128)(2,1)S(1)} %get-tuple-element.40.refs_3_, ...), custom_call_target="tpu_custom_call" | custom-call | tf_op jit(solution)/shard_map/pallas_call | solution.py:169
  75.7 0.0 collective-permute-done.10.refs_0_
  75.7 0.0 collective-permute-done.11.refs_2_
  75.7 0.0 collective-permute-start.18
  75.7 0.5 collective-permute-start.19
  76.3 1.6 %collective-permute-start.8 = (f32[64,1536]{1,0:T(8,128)S(1)}, f32[64,1536]{1,0:T(8,128)S(1)}, u32[]{:S(2)}, u32[]{:S(2)}) collective-permute-start(f32[64,1536]{1,0:T(8,128)S(1)} %slice.31), channel_id=1, source_target_pairs={{0,2},{1,3},{2,0},{3,1},{4,6},{5,7},{6,4},{7,5},{8,10},{9,11},{10,... | collective-permute-start | bytes 1179656 | tf_op jit(solution)/shard_map/ppermute | solution.py:211
  77.9 0.5 collective-permute-start.9
  78.4 0.0 collective-permute-done.18.refs_1_
  78.4 0.4 collective-permute-done.19.refs_3_
  78.8 5.6 %shard_map.108.refs_6_ = f32[4096,256]{1,0:T(8,128)} custom-call(f32[64,2560]{1,0:T(8,128)S(1)} %collective-permute-done.10.refs_0_, f32[64,2560]{1,0:T(8,128)S(1)} %collective-permute-done.18.refs_1_, f32[64,2560]{1,0:T(8,128)S(1)} %collective-permute-done.11.refs_2_, ...), custom_call_target="tpu_custom_call", output_to_operand_aliasing={{}: (6, {})} | custom-call | tf_op jit(solution)/shard_map/pallas_call | solution.py:193
  84.4 3.1 %collective-permute-done.8.refs_0_ = f32[64,1536]{1,0:T(8,128)S(1)} collective-permute-done((f32[64,1536]{1,0:T(8,128)S(1)}, f32[64,1536]{1,0:T(8,128)S(1)}, u32[]{:S(2)}, u32[]{:S(2)}) %collective-permute-start.8) | collective-permute-done | bytes 393248 | tf_op jit(solution)/shard_map/ppermute | solution.py:211
  87.5 1.2 %collective-permute-done.9.refs_2_ = f32[64,1536]{1,0:T(8,128)S(1)} collective-permute-done((f32[64,1536]{1,0:T(8,128)S(1)}, f32[64,1536]{1,0:T(8,128)S(1)}, u32[]{:S(2)}, u32[]{:S(2)}) %collective-permute-start.9) | collective-permute-done | bytes 393248 | tf_op jit(solution)/shard_map/ppermute | solution.py:211
  88.7 0.0 collective-permute-start.20
  88.7 0.5 collective-permute-start.21
  89.2 1.2 %collective-permute-done.20.refs_1_ = f32[64,1536]{1,0:T(8,128)S(1)} collective-permute-done((f32[64,1536]{1,0:T(8,128)S(1)}, f32[64,1536]{1,0:T(8,128)S(1)}, u32[]{:S(2)}, u32[]{:S(2)}) %collective-permute-start.20) | collective-permute-done | bytes 393248 | tf_op jit(solution)/shard_map/ppermute | solution.py:211
  90.4 0.6 collective-permute-done.21.refs_3_
  91.0 3.9 %shard_map.109 = f32[4096,256]{1,0:T(8,128)} custom-call(f32[64,1536]{1,0:T(8,128)S(1)} %collective-permute-done.8.refs_0_, f32[64,1536]{1,0:T(8,128)S(1)} %collective-permute-done.20.refs_1_, f32[64,1536]{1,0:T(8,128)S(1)} %collective-permute-done.9.refs_2_, f32[64,1536]{1,0:T(8,128)S(1)} %collective-permute-done.21.refs_3_, ...), custom_call_target="tpu_custom_call", output_to_operand_aliasing={{}: (6, {})} | custom-call | tf_op jit(solution)/shard_map/pallas_call | solution.py:193
  (11 shorter events, 0.2 us)
Async XLA Ops:
  2.7 20.0 %collective-permute-start = (f32[640,256]{1,0:T(8,128)}, f32[640,256]{1,0:T(8,128)S(1)}, u32[]{:S(2)}, u32[]{:S(2)}) collective-permute-start(f32[640,256]{1,0:T(8,128)} %shard_map.103), channel_id=1, source_target_pairs={{0,8},{8,16},{16,24},{24,0},{1,9},{9,17},{17,25},{25,1},{2,10},{10... | collective-permute-start | bytes 1966088 | tf_op jit(solution)/shard_map/ppermute | solution.py:214
  5.8 24.8 %collective-permute-start.4 = (f32[64,4096]{1,0:T(8,128)}, f32[64,4096]{1,0:T(8,128)S(1)}, u32[]{:S(2)}, u32[]{:S(2)}) collective-permute-start(f32[64,4096]{1,0:T(8,128)} %bitcast.2), channel_id=1, source_target_pairs={{0,4},{1,5},{2,6},{3,7},{4,0},{5,1},{6,2},{7,3},{8,12},{9,13},{10,... | collective-permute-start | bytes 3145736 | tf_op jit(solution)/shard_map/ppermute | solution.py:211
  7.3 24.9 %collective-permute-start.5 = (f32[64,4096]{1,0:T(8,128)}, f32[64,4096]{1,0:T(8,128)S(1)}, u32[]{:S(2)}, u32[]{:S(2)}) collective-permute-start(f32[64,4096]{1,0:T(8,128)} %bitcast.6), channel_id=1, source_target_pairs={{0,2},{1,3},{2,0},{3,1},{4,6},{5,7},{6,4},{7,5},{8,10},{9,11},{10,... | collective-permute-start | bytes 3145736 | tf_op jit(solution)/shard_map/ppermute | solution.py:211
  8.8 24.9 %collective-permute-start.12 = (f32[64,4096]{1,0:T(8,128)}, f32[64,4096]{1,0:T(8,128)S(1)}, u32[]{:S(2)}, u32[]{:S(2)}) collective-permute-start(f32[64,4096]{1,0:T(8,128)} %bitcast.3), channel_id=1, source_target_pairs={{0,1},{1,0},{2,3},{3,2},{4,5},{5,4},{6,7},{7,6},{8,9},{9,8},{10,11... | collective-permute-start | bytes 3145736 | tf_op jit(solution)/shard_map/ppermute | solution.py:211
  8.8 26.4 %collective-permute-start.13 = (f32[64,4096]{1,0:T(8,128)}, f32[64,4096]{1,0:T(8,128)S(1)}, u32[]{:S(2)}, u32[]{:S(2)}) collective-permute-start(f32[64,4096]{1,0:T(8,128)} %bitcast.7), channel_id=1, source_target_pairs={{0,1},{1,0},{2,3},{3,2},{4,5},{5,4},{6,7},{7,6},{8,9},{9,8},{10,11... | collective-permute-start | bytes 3145736 | tf_op jit(solution)/shard_map/ppermute | solution.py:211
  22.7 30.2 %collective-permute-start.2 = (f32[640,256]{1,0:T(8,128)}, f32[640,256]{1,0:T(8,128)S(1)}, u32[]{:S(2)}, u32[]{:S(2)}) collective-permute-start(f32[640,256]{1,0:T(8,128)} %shard_map.103), channel_id=1, source_target_pairs={{0,24},{8,0},{16,8},{24,16},{1,25},{9,1},{17,9},{25,17},{2,26},{10... | collective-permute-start | bytes 1966088 | tf_op jit(solution)/shard_map/ppermute | solution.py:214
  30.6 22.4 %collective-permute-start.1 = (f32[640,256]{1,0:T(8,128)S(1)}, f32[640,256]{1,0:T(8,128)S(1)}, u32[]{:S(2)}, u32[]{:S(2)}) collective-permute-start(f32[640,256]{1,0:T(8,128)S(1)} %collective-permute-done.refs_5_), channel_id=1, source_target_pairs={{0,8},{8,16},{16,24},{24,0},{1,9},{9,17},{17,25},{25,1},{2,10},{10... | collective-permute-start | bytes 1966088 | tf_op jit(solution)/shard_map/ppermute | solution.py:214
  32.2 23.6 %collective-permute-start.6 = (f32[64,4096]{1,0:T(8,128)}, f32[64,4096]{1,0:T(8,128)S(1)}, u32[]{:S(2)}, u32[]{:S(2)}) collective-permute-start(f32[64,4096]{1,0:T(8,128)} %bitcast.4), channel_id=1, source_target_pairs={{0,2},{1,3},{2,0},{3,1},{4,6},{5,7},{6,4},{7,5},{8,10},{9,11},{10,... | collective-permute-start | bytes 3145736 | tf_op jit(solution)/shard_map/ppermute | solution.py:211
  33.7 23.4 %collective-permute-start.7 = (f32[64,4096]{1,0:T(8,128)}, f32[64,4096]{1,0:T(8,128)S(1)}, u32[]{:S(2)}, u32[]{:S(2)}) collective-permute-start(f32[64,4096]{1,0:T(8,128)} %bitcast.8), channel_id=1, source_target_pairs={{0,4},{1,5},{2,6},{3,7},{4,0},{5,1},{6,2},{7,3},{8,12},{9,13},{10,... | collective-permute-start | bytes 3145736 | tf_op jit(solution)/shard_map/ppermute | solution.py:211
  35.2 21.8 %collective-permute-start.14 = (f32[64,4096]{1,0:T(8,128)S(1)}, f32[64,4096]{1,0:T(8,128)S(1)}, u32[]{:S(2)}, u32[]{:S(2)}) collective-permute-start(f32[64,4096]{1,0:T(8,128)S(1)} %collective-permute-done.4.refs_4_), channel_id=1, source_target_pairs={{0,1},{1,0},{2,3},{3,2},{4,5},{5,4},{6,7},{7,6},{8,9},{9,8},{10,11... | collective-permute-start | bytes 3145736 | tf_op jit(solution)/shard_map/ppermute | solution.py:211
  52.9 4.1 %collective-permute-start.15 = (f32[64,4096]{1,0:T(8,128)S(1)}, f32[64,4096]{1,0:T(8,128)S(1)}, u32[]{:S(2)}, u32[]{:S(2)}) collective-permute-start(f32[64,4096]{1,0:T(8,128)S(1)} %collective-permute-done.5.refs_6_), channel_id=1, source_target_pairs={{0,1},{1,0},{2,3},{3,2},{4,5},{5,4},{6,7},{7,6},{8,9},{9,8},{10,11... | collective-permute-start | bytes 3145736 | tf_op jit(solution)/shard_map/ppermute | solution.py:211
  53.0 6.8 %copy-start.4 = (f32[4096,64]{0,1:T(8,128)S(1)}, f32[4096,64]{0,1:T(8,128)}, u32[]{:S(2)}) copy-start(f32[4096,64]{0,1:T(8,128)} %param.11) | copy-start | bytes 3145732
  53.0 6.8 %copy-start.5 = (f32[4096,64]{0,1:T(8,128)S(1)}, f32[4096,64]{0,1:T(8,128)}, u32[]{:S(2)}) copy-start(f32[4096,64]{0,1:T(8,128)} %param.12) | copy-start | bytes 3145732
  53.1 9.8 %collective-permute-start.3 = (f32[1152,256]{1,0:T(8,128)S(1)}, f32[1152,256]{1,0:T(8,128)S(1)}, u32[]{:S(2)}, u32[]{:S(2)}) collective-permute-start(f32[1152,256]{1,0:T(8,128)S(1)} %pad_maximum_fusion), channel_id=1, source_target_pairs={{0,1},{1,0},{2,3},{3,2},{4,5},{5,4},{6,7},{7,6},{8,9},{9,8},{10,11... | collective-permute-start | bytes 3538952 | tf_op jit(solution)/shard_map/ppermute | solution.py:211
  57.0 9.4 %collective-permute-start.16 = (f32[64,4096]{1,0:T(8,128)S(1)}, f32[64,4096]{1,0:T(8,128)S(1)}, u32[]{:S(2)}, u32[]{:S(2)}) collective-permute-start(f32[64,4096]{1,0:T(8,128)S(1)} %collective-permute-done.6.refs_0_), channel_id=1, source_target_pairs={{0,1},{1,0},{2,3},{3,2},{4,5},{5,4},{6,7},{7,6},{8,9},{9,8},{10,11... | collective-permute-start | bytes 3145736 | tf_op jit(solution)/shard_map/ppermute | solution.py:211
  57.0 9.4 %collective-permute-start.17 = (f32[64,4096]{1,0:T(8,128)S(1)}, f32[64,4096]{1,0:T(8,128)S(1)}, u32[]{:S(2)}, u32[]{:S(2)}) collective-permute-start(f32[64,4096]{1,0:T(8,128)S(1)} %collective-permute-done.7.refs_2_), channel_id=1, source_target_pairs={{0,1},{1,0},{2,3},{3,2},{4,5},{5,4},{6,7},{7,6},{8,9},{9,8},{10,11... | collective-permute-start | bytes 3145736 | tf_op jit(solution)/shard_map/ppermute | solution.py:211
  57.6 5.3 %copy-start.1 = (f32[128,512]{1,0:T(8,128)S(1)}, f32[128,512]{1,0:T(8,128)}, u32[]{:S(2)}) copy-start(f32[128,512]{1,0:T(8,128)} %refs_0_.3) | copy-start | bytes 786436
  57.7 5.3 %copy-start.2 = (f32[128,512]{1,0:T(8,128)S(1)}, f32[128,512]{1,0:T(8,128)}, u32[]{:S(2)}) copy-start(f32[128,512]{1,0:T(8,128)} %refs_1_.3) | copy-start | bytes 786436
  57.7 5.3 %copy-start.3 = (f32[128,512]{1,0:T(8,128)S(1)}, f32[128,512]{1,0:T(8,128)}, u32[]{:S(2)}) copy-start(f32[128,512]{1,0:T(8,128)} %refs_2_.3) | copy-start | bytes 786436
  57.7 5.3 %copy-start.6 = (f32[128,256]{1,0:T(8,128)S(1)}, f32[128,256]{1,0:T(8,128)}, u32[]{:S(2)}) copy-start(f32[128,256]{1,0:T(8,128)} %refs_3_.3) | copy-start | bytes 393220
  57.7 5.3 %copy-start.7 = (f32[128,256]{1,0:T(8,128)S(1)}, f32[128,256]{1,0:T(8,128)}, u32[]{:S(2)}) copy-start(f32[128,256]{1,0:T(8,128)} %refs_4_.3) | copy-start | bytes 393220
  57.7 18.0 %collective-permute-start.10 = (f32[64,2560]{1,0:T(8,128)S(1)}, f32[64,2560]{1,0:T(8,128)S(1)}, u32[]{:S(2)}, u32[]{:S(2)}) collective-permute-start(f32[64,2560]{1,0:T(8,128)S(1)} %slice.33), channel_id=1, source_target_pairs={{0,2},{1,3},{2,0},{3,1},{4,6},{5,7},{6,4},{7,5},{8,10},{9,11},{10,... | collective-permute-start | bytes 1966088 | tf_op jit(solution)/shard_map/ppermute | solution.py:211
  58.3 17.4 %collective-permute-start.11 = (f32[64,2560]{1,0:T(8,128)S(1)}, f32[64,2560]{1,0:T(8,128)S(1)}, u32[]{:S(2)}, u32[]{:S(2)}) collective-permute-start(f32[64,2560]{1,0:T(8,128)S(1)} %slice.34), channel_id=1, source_target_pairs={{0,4},{1,5},{2,6},{3,7},{4,0},{5,1},{6,2},{7,3},{8,12},{9,13},{10,... | collective-permute-start | bytes 1966088 | tf_op jit(solution)/shard_map/ppermute | solution.py:211
  66.4 2.2 %copy-start = (f32[4096,256]{1,0:T(8,128)S(1)}, f32[4096,256]{1,0:T(8,128)}, u32[]{:S(2)}) copy-start(f32[4096,256]{1,0:T(8,128)} %refs_8_.1) | copy-start | bytes 12582916
  75.7 2.7 %collective-permute-start.18 = (f32[64,2560]{1,0:T(8,128)S(1)}, f32[64,2560]{1,0:T(8,128)S(1)}, u32[]{:S(2)}, u32[]{:S(2)}) collective-permute-start(f32[64,2560]{1,0:T(8,128)S(1)} %collective-permute-done.10.refs_0_), channel_id=1, source_target_pairs={{0,1},{1,0},{2,3},{3,2},{4,5},{5,4},{6,7},{7,6},{8,9},{9,8},{10,11... | collective-permute-start | bytes 1966088 | tf_op jit(solution)/shard_map/ppermute | solution.py:211
  75.7 3.0 %collective-permute-start.19 = (f32[64,2560]{1,0:T(8,128)S(1)}, f32[64,2560]{1,0:T(8,128)S(1)}, u32[]{:S(2)}, u32[]{:S(2)}) collective-permute-start(f32[64,2560]{1,0:T(8,128)S(1)} %collective-permute-done.11.refs_2_), channel_id=1, source_target_pairs={{0,1},{1,0},{2,3},{3,2},{4,5},{5,4},{6,7},{7,6},{8,9},{9,8},{10,11... | collective-permute-start | bytes 1966088 | tf_op jit(solution)/shard_map/ppermute | solution.py:211
  76.3 11.2 %collective-permute-start.8 = (f32[64,1536]{1,0:T(8,128)S(1)}, f32[64,1536]{1,0:T(8,128)S(1)}, u32[]{:S(2)}, u32[]{:S(2)}) collective-permute-start(f32[64,1536]{1,0:T(8,128)S(1)} %slice.31), channel_id=1, source_target_pairs={{0,2},{1,3},{2,0},{3,1},{4,6},{5,7},{6,4},{7,5},{8,10},{9,11},{10,... | collective-permute-start | bytes 1179656 | tf_op jit(solution)/shard_map/ppermute | solution.py:211
  77.9 10.8 %collective-permute-start.9 = (f32[64,1536]{1,0:T(8,128)S(1)}, f32[64,1536]{1,0:T(8,128)S(1)}, u32[]{:S(2)}, u32[]{:S(2)}) collective-permute-start(f32[64,1536]{1,0:T(8,128)S(1)} %slice.32), channel_id=1, source_target_pairs={{0,4},{1,5},{2,6},{3,7},{4,0},{5,1},{6,2},{7,3},{8,12},{9,13},{10,... | collective-permute-start | bytes 1179656 | tf_op jit(solution)/shard_map/ppermute | solution.py:211
  88.7 1.7 %collective-permute-start.20 = (f32[64,1536]{1,0:T(8,128)S(1)}, f32[64,1536]{1,0:T(8,128)S(1)}, u32[]{:S(2)}, u32[]{:S(2)}) collective-permute-start(f32[64,1536]{1,0:T(8,128)S(1)} %collective-permute-done.8.refs_0_), channel_id=1, source_target_pairs={{0,1},{1,0},{2,3},{3,2},{4,5},{5,4},{6,7},{7,6},{8,9},{9,8},{10,11... | collective-permute-start | bytes 1179656 | tf_op jit(solution)/shard_map/ppermute | solution.py:211
  88.7 2.3 %collective-permute-start.21 = (f32[64,1536]{1,0:T(8,128)S(1)}, f32[64,1536]{1,0:T(8,128)S(1)}, u32[]{:S(2)}, u32[]{:S(2)}) collective-permute-start(f32[64,1536]{1,0:T(8,128)S(1)} %collective-permute-done.9.refs_2_), channel_id=1, source_target_pairs={{0,1},{1,0},{2,3},{3,2},{4,5},{5,4},{6,7},{7,6},{8,9},{9,8},{10,11... | collective-permute-start | bytes 1179656 | tf_op jit(solution)/shard_map/ppermute | solution.py:211

commit v2 on v1

v2 whole, which is shorter than its diff:
```python
import functools

import jax
import jax.numpy as jnp
from jax import lax
from jax.experimental import pallas as pl
from jax.experimental.pallas import tpu as pltpu
from jax.sharding import PartitionSpec as P

VMEM_BYTES = 24 * 2**20
UPDATE_BYTES = 32 * 2**20
COST = pl.CostEstimate(flops=1024, bytes_accessed=1024, transcendentals=0)
INNER = 8
CORE, ACROSS, UP = 1, 2, 4
FIRST, SECOND = 0, 1
ONE, OTHER = (ACROSS, UP), (UP, ACROSS)


def beyond(masks):
    return masks[1] | CORE, masks[0] | CORE


BOTH = (ACROSS | UP, ACROSS | UP)
GROUPS = tuple(
    tuple((panel, masks) for who in block for masks in (who, beyond(who)) for panel in (FIRST, SECOND))
    for block in (((0, 0), ONE, OTHER), (BOTH,))
)


def split(value):
    high = value.astype(jnp.bfloat16)
    return high, (value - high.astype(jnp.float32)).astype(jnp.bfloat16)


def product(left, right, contract=1):
    def one(a, b):
        return lax.dot_general(
            a, b, (((contract,), (0,)), ((), ())), preferred_element_type=jnp.float32
        )

    return one(left[0], right[0]) + one(left[0], right[1]) + one(left[1], right[0])


def pack_kernel(*refs):
    (*matrices, first, second), out = refs[:-1], refs[-1]
    rows, width = first.shape
    even = lax.rem(lax.axis_index("col"), 2) == 0
    for k, ref in enumerate(matrices):
        out[k * rows : (k + 1) * rows, :] = jnp.where(even, ref[:, :width], ref[:, width:])
    out[3 * rows : 4 * rows, :] = first[...]
    out[4 * rows :, :] = second[...]


def pack_rows(own):
    rows, width = own[3].shape
    whole = pl.BlockSpec(memory_space=pltpu.VMEM)
    return pl.pallas_call(
        pack_kernel,
        out_shape=jax.ShapeDtypeStruct((5 * rows, width), jnp.float32),
        in_specs=[whole] * 5,
        out_specs=whole,
        cost_estimate=COST,
    )(*own)


def solve_kernel(steps, block, *refs):
    own, refs = refs[:5], refs[5:]
    pieces, (early, late, *refs) = refs[: steps - 1], refs[steps - 1 :]
    outs, (first_out, second_out, *scratch) = refs[: 2 * len(GROUPS)], refs[2 * len(GROUPS) :]
    matrices, right_first, right_second, solved = scratch
    here = lax.axis_index("row")
    lane = lax.axis_index("col")
    even = lax.rem(lane, 2) == 0
    rows, width = own[3].shape[0], matrices.shape[2] // 2

    def at(step):
        return pl.ds(pl.multiple_of(lax.rem(here + steps - step, steps) * rows, rows), rows)

    for k in range(3):
        matrices[k, at(0), :] = own[k][...]
    right_first[at(0), :] = own[3][...]
    right_second[at(0), :] = own[4][...]
    for j, piece in enumerate(pieces):
        right_first[at(j + 1), :] = piece[3 * rows : 4 * rows, :]
        right_second[at(j + 1), :] = piece[4 * rows :, :]
        for k in range(3):
            mine = piece[k * rows : (k + 1) * rows, :]
            others, at_row = (late, 3 * (j - 1) + k) if j else (early, k)
            other = others[at_row * rows : (at_row + 1) * rows, :]
            matrices[k, at(j + 1), :width] = jnp.where(even, mine, other)
            matrices[k, at(j + 1), width:] = jnp.where(even, other, mine)
    solved[0] = product(split(matrices[0]), split(right_first[...]))
    reduced = right_second[...] - product(split(matrices[2]), split(solved[0]))
    solved[1] = product(split(matrices[1]), split(reduced))
    first_out[...] = solved[0, at(0), :]
    second_out[...] = solved[1, at(0), :]

    inner = lax.rem(lane, INNER)
    outer = solved.shape[1] // (INNER * block)
    for group, (high_out, low_out) in zip(GROUPS, zip(outs[::2], outs[1::2])):
        to = 0
        for part, (mask, odd_mask) in group:
            which = lax.bitwise_xor(inner, jnp.where(even, mask, odd_mask))
            for o in range(outer):
                start = pl.multiple_of((o * INNER + which) * block, block)
                high, low = split(solved[part, pl.ds(start, block), :])
                high_out[to : to + block, :] = high
                low_out[to : to + block, :] = low
                to += block


def solve(steps, block, own, pieces, others):
    rows, width = own[3].shape
    depth = rows * steps
    outs = [
        jax.ShapeDtypeStruct((len(group) * depth // INNER, width), jnp.bfloat16)
        for group in GROUPS
        for _ in range(2)
    ]
    outs += [jax.ShapeDtypeStruct((rows, width), jnp.float32)] * 2
    whole = pl.BlockSpec(memory_space=pltpu.VMEM)
    operands = [*own, *pieces, *others]
    return pl.pallas_call(
        functools.partial(solve_kernel, steps, block),
        out_shape=outs,
        in_specs=[whole] * len(operands),
        out_specs=[whole] * len(outs),
        scratch_shapes=[
            pltpu.VMEM((3, depth, depth), jnp.float32),
            pltpu.VMEM((depth, width), jnp.float32),
            pltpu.VMEM((depth, width), jnp.float32),
            pltpu.VMEM((2, depth, width), jnp.float32),
        ],
        compiler_params=pltpu.CompilerParams(vmem_limit_bytes=VMEM_BYTES),
        cost_estimate=COST,
    )(*operands)


def update_kernel(near_count, far_count, start, tile, *refs):
    near, refs = refs[:near_count], refs[near_count:]
    far, refs = refs[:far_count], refs[far_count:]
    near_factor, refs = (refs[:2], refs[2:]) if near else (None, refs)
    far_factor, refs = (refs[:2], refs[2:]) if far else (None, refs)
    before, after, work, arrived, left = refs
    tiles = work.shape[0] // tile
    full = far[0].shape[1] // tile if far else 0

    def rows_of(t, first=0):
        return pl.ds(pl.multiple_of(first + t * tile, tile), tile)

    def bring(t):
        return pltpu.make_async_copy(before.at[rows_of(t, start)], work.at[rows_of(t)], arrived.at[t])

    def take(t):
        return pltpu.make_async_copy(work.at[rows_of(t)], after.at[rows_of(t, start)], left.at[t])

    def part(panels, factor, t):
        panel = jnp.concatenate([ref[:, rows_of(t)] for ref in panels], axis=0)
        return product(split(panel), (factor[0][...], factor[1][...]), contract=0)

    def step(t, with_far):
        total = part(near, near_factor, t) if near else 0.0
        if with_far:
            total = total + part(far, far_factor, t)
        bring(t).wait()
        work[rows_of(t), :] = work[rows_of(t), :] - total
        take(t).start()

    for t in range(tiles):
        bring(t).start()
    pl.loop(0, full)(lambda t: step(t, True))
    if full < tiles:
        pl.loop(full, tiles)(lambda t: step(t, False))
    for t in range(tiles):
        take(t).wait()


def update(near, near_factor, far, far_factor, before, start, tile, in_place):
    rows, width = (near or far)[0].shape[1], before.shape[1]
    tile = min(tile, rows)
    operands = [*near, *far, *(near_factor if near else ()), *(far_factor if far else ())]
    anywhere = pl.BlockSpec(memory_space=pl.ANY)
    return pl.pallas_call(
        functools.partial(update_kernel, len(near), len(far), start, tile),
        out_shape=jax.ShapeDtypeStruct(before.shape, jnp.float32),
        in_specs=[pl.BlockSpec(memory_space=pltpu.VMEM)] * len(operands) + [anywhere],
        out_specs=anywhere,
        input_output_aliases={len(operands): 0} if in_place else {},
        scratch_shapes=[
            pltpu.VMEM((rows, width), jnp.float32),
            pltpu.SemaphoreType.DMA((rows // tile,)),
            pltpu.SemaphoreType.DMA((rows // tile,)),
        ],
        compiler_params=pltpu.CompilerParams(vmem_limit_bytes=UPDATE_BYTES),
        cost_estimate=COST,
    )(*operands, before)


def solution(mesh):
    row_count, col_count = mesh.shape["row"], mesh.shape["col"]

    def swap(value, bit):
        return lax.ppermute(value, "col", [(i, i ^ bit) for i in range(col_count)])

    def shift(value, by):
        return lax.ppermute(value, "row", [(i, (i + by) % row_count) for i in range(row_count)])

    def per_device(
        inverse_first, inverse_second, coupling, panel_first, panel_second,
        rhs_first, rhs_second, rhs_rest,
    ):
        first, second = panel_first.T, panel_second.T
        block = first.shape[0]
        if col_count > INNER:
            groups = [list(range(i, col_count, INNER)) for i in range(INNER)]
            first, second = (
                lax.all_gather(p, "col", axis=0, tiled=True, axis_index_groups=groups)
                for p in (first, second)
            )
        rest = first.shape[1]

        own = (inverse_first, inverse_second, coupling, rhs_first, rhs_second)
        def cross(value, masks):
            return lax.ppermute(value, "col", [(i, i ^ masks[i % 2]) for i in range(col_count)])

        def beside(pair):
            return tuple(swap(x, CORE) for x in pair)

        def after(values, *tokens):
            return lax.optimization_barrier((values, tokens))[0]

        near_0 = tuple(cross(x, ONE) for x in (first, second))
        own_beside = beside((first, second))
        matrix_rows = 3 * rhs_first.shape[0]
        packs = [shift(pack_rows(own), 1)]
        near_1 = tuple(cross(x, OTHER) for x in after((first, second), own_beside, packs[0]))
        for _ in range(row_count - 2):
            packs.append(shift(packs[-1], 1))
        beside_0 = swap(near_0[0], CORE)
        beside_0 = beside_0, swap(after(near_0[1], beside_0), CORE)
        early = swap(after(packs[0][:matrix_rows], near_1, beside_0), CORE)
        late = swap(after(jnp.concatenate([p[:matrix_rows] for p in packs[1:]], axis=0), early), CORE)
        others = [early, late]
        cuts = [0, rest // 4, rest // 2, rest]
        far = [
            cross(jnp.concatenate([x[:, a:b] for x in after(near_0, near_1)], axis=0), OTHER)
            for a, b in zip(cuts[:-1], cuts[1:])
        ]
        beside_1 = beside(near_1)
        near = [
            panel
            for pair in ((first, second), own_beside, near_0, beside_0, near_1, beside_1)
            for panel in pair
        ]
        *factors, solved_first, solved_second = solve(row_count, block, own, packs, after(others, beside_1))
        near_factor, far_factor = factors[:2], factors[2:]
        lead = [jnp.concatenate(x, axis=1) for x in (far[:2], [swap(panel, CORE) for panel in far[:2]])]
        updated = update(near, near_factor, lead, far_factor, rhs_rest, 0, 1024, False)
        for start, panel in zip(cuts[2:], far[2:]):
            panel = after(panel, updated)
            updated = update([], None, [panel, swap(panel, CORE)], far_factor, updated, start, 512, True)
        return solved_first, solved_second, updated

    in_specs = (P("row", None),) * 3 + (P("row", "col"),) * 5
    return jax.shard_map(
        per_device, mesh=mesh, in_specs=in_specs, out_specs=(P("row", "col"),) * 3, check_vma=False
    )
```

time: 95.2 us -> 87.4 us (0.918)
  Pallas kernels: 27 us -> 17.2 us
  waiting for transfers between devices: 47.1 us -> 55.2 us
  starting transfers between devices: 19.2 us -> 13.3 us
    ppermute x0 -> x7, waiting for transfers between devices: none -> 26.5 us  [cross(): lax.ppermute(value, 'col', [(i, i ^ masks[i % 2]) for i in range(col_coun...]
    ppermute x19 -> x11, waiting for transfers between devices: 15.9 us -> 4.97 us  [swap(): return lax.ppermute(value, 'col', [(i, i ^ bit) for i in range(col_count)])]
    ppermute x19 -> x11, starting transfers between devices: 12.8 us -> 1.96 us  [swap(): return lax.ppermute(value, 'col', [(i, i ^ bit) for i in range(col_count)])]
    pallas_call x5 -> x2, Pallas kernels: 21.5 us -> 11.6 us  [update(): pl.pallas_call(functools.partial(update_kernel, len(near), len(far), star...]
    ppermute x0 -> x7, starting transfers between devices: none -> 9.79 us  [cross(): lax.ppermute(value, 'col', [(i, i ^ masks[i % 2]) for i in range(col_coun...]
    ppermute x3, waiting for transfers between devices: 31.2 us -> 23.7 us  [shift(): lax.ppermute(value, 'row', [(i, (i + by) % row_count) for i in range(row_...]
    ppermute x3, starting transfers between devices: 6.34 us -> 1.58 us  [shift(): lax.ppermute(value, 'row', [(i, (i + by) % row_count) for i in range(row_...]
  transfers between devices with their start and end apart: 22 -> 21, of which waited for: 10 -> 9; matrix products, arithmetic and copies ran while one was open for 0% -> 1% of each run, Pallas kernels for 22% -> 16%
where the time goes in v2:
time: 87.4 us; the launch traced here: 87.3 us
  waiting for transfers between devices  55.2 us (63%)
  Pallas kernels  17.2 us (20%)
  starting transfers between devices  13.3 us (15%)
  between operations  0.9 us (1%)
    ppermute x7, waiting for transfers between devices, cross(): lax.ppermute(value, 'col', [(i, i ^ masks[i % 2]) for i in range(col_coun...  26.5 us
    ppermute x3, waiting for transfers between devices, shift(): lax.ppermute(value, 'row', [(i, (i + by) % row_count) for i in range(row_...  23.7 us
    pallas_call x2, Pallas kernels, update(): pl.pallas_call(functools.partial(update_kernel, len(near), len(far), star...  11.6 us
    ppermute x7, starting transfers between devices, cross(): lax.ppermute(value, 'col', [(i, i ^ masks[i % 2]) for i in range(col_coun...  9.79 us
    ppermute x11, waiting for transfers between devices, swap(): return lax.ppermute(value, 'col', [(i, i ^ bit) for i in range(col_count)])  4.97 us
    pallas_call x1, Pallas kernels, solve(): pl.pallas_call(functools.partial(solve_kernel, steps, block), out_shape=o...  3.47 us
    pallas_call x1, Pallas kernels, pack_rows(): pl.pallas_call(pack_kernel, out_shape=jax.ShapeDtypeStruct((5 * rows, wid...  2.1 us
    ppermute x11, starting transfers between devices, swap(): return lax.ppermute(value, 'col', [(i, i ^ bit) for i in range(col_count)])  1.96 us
  transfers between devices with their start and end apart: 21, of which 9 were waited for; matrix products, arithmetic and copies ran while one was open for 1% of the time, Pallas kernels for 16%

profile of v2, /device:TPU:0, one launch (start us, length us, event | category | flops | bytes accessed | tf_op | source)
XLA Modules:
  0.0 87.3 jit_solution(9315772766204343229)
XLA Ops:
  0.6 3.0 %collective-permute-start.7 = (f32[64,4096]{1,0:T(8,128)}, f32[64,4096]{1,0:T(8,128)S(1)}, u32[]{:S(2)}, u32[]{:S(2)}) collective-permute-start(f32[64,4096]{1,0:T(8,128)} %bitcast.6), channel_id=1, source_target_pairs={{0,2},{1,5},{2,0},{3,7},{4,6},{5,1},{6,4},{7,3},{8,10},{9,13},{10,... | collective-permute-start | bytes 3145736 | tf_op jit(solution)/shard_map/ppermute | solution.py:224
  3.6 0.0 collective-permute-start.3
  3.6 0.5 collective-permute-start.4
  4.1 2.1 %shard_map.103 = f32[640,256]{1,0:T(8,128)} custom-call(f32[128,512]{1,0:T(8,128)} %refs_0_.3, f32[128,512]{1,0:T(8,128)} %refs_1_.3, f32[128,512]{1,0:T(8,128)} %refs_2_.3, f32[128,256]{1,0:T(8,128)} %refs_3_.3, f32[128,256]{1,0:T(8,128)} %refs_4_.3), custom_call_target="tpu_custom_call" | custom-call | flops 1024 | bytes 1024 | tf_op jit(solution)/shard_map/pallas_call | solution.py:57
  6.2 1.6 %collective-permute-start = (f32[640,256]{1,0:T(8,128)}, f32[640,256]{1,0:T(8,128)S(1)}, u32[]{:S(2)}, u32[]{:S(2)}) collective-permute-start(f32[640,256]{1,0:T(8,128)} %shard_map.103), channel_id=1, source_target_pairs={{0,8},{8,16},{16,24},{24,0},{1,9},{9,17},{17,25},{25,1},{2,10},{10... | collective-permute-start | bytes 1966088 | tf_op jit(solution)/shard_map/ppermute | solution.py:206
  7.8 0.6 collective-permute-start.9
  8.4 8.2 %collective-permute-done.7.refs_4_ = f32[64,4096]{1,0:T(8,128)S(1)} collective-permute-done((f32[64,4096]{1,0:T(8,128)}, f32[64,4096]{1,0:T(8,128)S(1)}, u32[]{:S(2)}, u32[]{:S(2)}) %collective-permute-start.7) | collective-permute-done | bytes 1048608 | tf_op jit(solution)/shard_map/ppermute | solution.py:224
  16.6 0.0 collective-permute-start.8
  16.6 8.3 %collective-permute-done.refs_5_ = f32[640,256]{1,0:T(8,128)S(1)} collective-permute-done((f32[640,256]{1,0:T(8,128)}, f32[640,256]{1,0:T(8,128)S(1)}, u32[]{:S(2)}, u32[]{:S(2)}) %collective-permute-start) | collective-permute-done | bytes 655392 | tf_op jit(solution)/shard_map/ppermute | solution.py:206
  25.0 0.0 collective-permute-done.3.refs_2_
  25.0 0.0 collective-permute-done.4.refs_3_
  25.0 1.5 %collective-permute-start.5 = (f32[64,4096]{1,0:T(8,128)}, f32[64,4096]{1,0:T(8,128)S(1)}, u32[]{:S(2)}, u32[]{:S(2)}) collective-permute-start(f32[64,4096]{1,0:T(8,128)} %bitcast.8), channel_id=1, source_target_pairs={{0,4},{1,3},{2,6},{3,1},{4,0},{5,7},{6,2},{7,5},{8,12},{9,11},{10,... | collective-permute-start | bytes 3145736 | tf_op jit(solution)/shard_map/ppermute | solution.py:224
  26.5 0.5 collective-permute-start.6
  27.0 0.0 collective-permute-start.1
  27.0 1.7 %collective-permute-done.9.refs_5_ = f32[64,4096]{1,0:T(8,128)S(1)} collective-permute-done((f32[64,4096]{1,0:T(8,128)}, f32[64,4096]{1,0:T(8,128)S(1)}, u32[]{:S(2)}, u32[]{:S(2)}) %collective-permute-start.9) | collective-permute-done | bytes 1048608 | tf_op jit(solution)/shard_map/ppermute | solution.py:224
  28.7 0.0 collective-permute-done.8.refs_6_
  28.7 0.0 collective-permute-start.10
  28.7 15.4 %collective-permute-done.1.refs_6_ = f32[640,256]{1,0:T(8,128)S(1)} collective-permute-done((f32[640,256]{1,0:T(8,128)S(1)}, f32[640,256]{1,0:T(8,128)S(1)}, u32[]{:S(2)}, u32[]{:S(2)}) %collective-permute-start.1) | collective-permute-done | bytes 655392 | tf_op jit(solution)/shard_map/ppermute | solution.py:206
  44.1 0.0 collective-permute-start.2
  44.1 0.0 collective-permute-done.5.refs_8_
  44.1 7.1 %collective-permute-done.6.refs_9_ = f32[64,4096]{1,0:T(8,128)S(1)} collective-permute-done((f32[64,4096]{1,0:T(8,128)}, f32[64,4096]{1,0:T(8,128)S(1)}, u32[]{:S(2)}, u32[]{:S(2)}) %collective-permute-start.6) | collective-permute-done | bytes 1048608 | tf_op jit(solution)/shard_map/ppermute | solution.py:224
  51.2 0.1 fusion
  51.4 1.6 %collective-permute-start.16 = (f32[128,1024]{1,0:T(8,128)S(1)}, f32[128,1024]{1,0:T(8,128)S(1)}, u32[]{:S(2)}, u32[]{:S(2)}) collective-permute-start(f32[128,1024]{1,0:T(8,128)S(1)} %pad_maximum_fusion.4), channel_id=1, source_target_pairs={{0,4},{1,3},{2,6},{3,1},{4,0},{5,7},{6,2},{7,5},{8,12},{9,11},{10,... | collective-permute-start | bytes 1572872 | tf_op jit(solution)/shard_map/ppermute | solution.py:224
  53.0 0.0 collective-permute-done.10.refs_7_
  53.0 0.1 collective-permute-start.11
  53.1 1.0 %collective-permute-start.17 = (f32[128,1024]{1,0:T(8,128)S(1)}, f32[128,1024]{1,0:T(8,128)S(1)}, u32[]{:S(2)}, u32[]{:S(2)}) collective-permute-start(f32[128,1024]{1,0:T(8,128)S(1)} %pad_maximum_fusion.5), channel_id=1, source_target_pairs={{0,4},{1,3},{2,6},{3,1},{4,0},{5,7},{6,2},{7,5},{8,12},{9,11},{10,... | collective-permute-start | bytes 1572872 | tf_op jit(solution)/shard_map/ppermute | solution.py:224
  54.2 6.5 %collective-permute-done.16 = f32[128,1024]{1,0:T(8,128)S(1)} collective-permute-done((f32[128,1024]{1,0:T(8,128)S(1)}, f32[128,1024]{1,0:T(8,128)S(1)}, u32[]{:S(2)}, u32[]{:S(2)}) %collective-permute-start.16) | collective-permute-done | bytes 524320 | tf_op jit(solution)/shard_map/ppermute | solution.py:224
  60.6 0.0 collective-permute-start.18
  60.7 0.6 collective-permute-start.13
  61.3 0.0 collective-permute-done.2.refs_7_
  61.3 0.1 collective-permute-start.14
  61.4 0.1 pad_maximum_fusion
  61.5 0.0 copy-start.3
  61.5 0.0 copy-start.4
  61.5 0.0 copy-start.5
  61.5 0.0 copy-start.6
  61.5 0.0 copy-start.7
  61.5 0.0 collective-permute-done.11.refs_8_
  61.5 1.6 %collective-permute-start.15 = (f32[128,2048]{1,0:T(8,128)S(1)}, f32[128,2048]{1,0:T(8,128)S(1)}, u32[]{:S(2)}, u32[]{:S(2)}) collective-permute-start(f32[128,2048]{1,0:T(8,128)S(1)} %pad_maximum_fusion), channel_id=1, source_target_pairs={{0,4},{1,3},{2,6},{3,1},{4,0},{5,7},{6,2},{7,5},{8,12},{9,11},{10,... | collective-permute-start | bytes 3145736 | tf_op jit(solution)/shard_map/ppermute | solution.py:224
  63.2 0.1 pad_maximum_fusion.3
  63.2 0.0 copy-start
  63.3 0.0 copy-start.1
  63.3 0.0 copy-start.2
  63.3 3.0 %collective-permute-done.17 = f32[128,1024]{1,0:T(8,128)S(1)} collective-permute-done((f32[128,1024]{1,0:T(8,128)S(1)}, f32[128,1024]{1,0:T(8,128)S(1)}, u32[]{:S(2)}, u32[]{:S(2)}) %collective-permute-start.17) | collective-permute-done | bytes 524320 | tf_op jit(solution)/shard_map/ppermute | solution.py:224
  66.2 0.0 collective-permute-start.12
  66.2 0.0 collective-permute-done.18
  66.2 0.5 collective-permute-start.19
  66.7 0.1 pad_maximum_fusion.1.refs_12_
  66.8 2.4 %collective-permute-done.19 = f32[128,1024]{1,0:T(8,128)S(1)} collective-permute-done((f32[128,1024]{1,0:T(8,128)S(1)}, f32[128,1024]{1,0:T(8,128)S(1)}, u32[]{:S(2)}, u32[]{:S(2)}) %collective-permute-start.19) | collective-permute-done | bytes 524320 | tf_op jit(solution)/shard_map/ppermute | solution.py:203
  69.3 0.1 pad_maximum_fusion.2.refs_13_
  69.4 0.0 collective-permute-done.13.refs_10_
  69.4 0.0 collective-permute-done.14.refs_11_
  69.4 0.0 collective-permute-done.12.refs_9_
  69.4 0.0 copy-done.3
  69.4 0.0 copy-done.4
  69.4 0.0 copy-done.5
  69.4 0.0 copy-done.6
  69.4 0.0 copy-done.7
  69.4 3.5 %shard_map.104 = (bf16[768,256]{1,0:T(8,128)(2,1)S(1)}, bf16[768,256]{1,0:T(8,128)(2,1)S(1)}, bf16[256,256]{1,0:T(8,128)(2,1)S(1)}, bf16[256,256]{1,0:T(8,128)(2...) custom-call(f32[128,512]{1,0:T(8,128)S(1)} %copy-done.3, f32[128,512]{1,0:T(8,128)S(1)} %copy-done.4, ...), custom_call_target="tpu_custom_call" | custom-call | flops 1024 | bytes 1024 | tf_op jit(solution)/shard_map/pallas_call | solution.py:123
  72.9 8.3 %shard_map.105.refs_4_ = f32[4096,256]{1,0:T(8,128)} custom-call(f32[64,4096]{1,0:T(8,128)S(1)} %bitcast.9, f32[64,4096]{1,0:T(8,128)S(1)} %bitcast.5, f32[64,4096]{1,0:T(8,128)S(1)} %collective-permute-done.3.refs_2_, f32[64,4096]{1,0:T(8,128)S(1)} %collective-permute-done.4.refs_3_, f32[64,4096]{1,0:T(8,128)S(1)} %collective-permute-done.7.refs_4_, ...), custom_call_target="tpu_custom_call" | custom-call | flops 1024 | bytes 1024 | tf_op jit(solution)/shard_map/pallas_call | solution.py:183
  81.2 0.0 collective-permute-done.15.refs_0_
  81.2 0.2 collective-permute-start.20
  81.5 2.5 %collective-permute-done.20.refs_1_ = f32[128,2048]{1,0:T(8,128)S(1)} collective-permute-done((f32[128,2048]{1,0:T(8,128)S(1)}, f32[128,2048]{1,0:T(8,128)S(1)}, u32[]{:S(2)}, u32[]{:S(2)}) %collective-permute-start.20) | collective-permute-done | bytes 1048608 | tf_op jit(solution)/shard_map/ppermute | solution.py:203
  84.0 3.3 %shard_map.106 = f32[4096,256]{1,0:T(8,128)} custom-call(f32[128,2048]{1,0:T(8,128)S(1)} %collective-permute-done.15.refs_0_, f32[128,2048]{1,0:T(8,128)S(1)} %collective-permute-done.20.refs_1_, bf16[256,256]{1,0:T(8,128)(2,1)S(1)} %get-tuple-element.32.refs_16_.refs_2_, ...), custom_call_target="tpu_custom_call", output_to_operand_aliasing={{}: (4, {})} | custom-call | flops 1024 | bytes 1024 | tf_op jit(solution)/shard_map/pallas_call | solution.py:183
  (10 shorter events, 0.2 us)
Async XLA Ops:
  0.6 16.0 %collective-permute-start.7 = (f32[64,4096]{1,0:T(8,128)}, f32[64,4096]{1,0:T(8,128)S(1)}, u32[]{:S(2)}, u32[]{:S(2)}) collective-permute-start(f32[64,4096]{1,0:T(8,128)} %bitcast.6), channel_id=1, source_target_pairs={{0,2},{1,5},{2,0},{3,7},{4,6},{5,1},{6,4},{7,3},{8,10},{9,13},{10,... | collective-permute-start | bytes 3145736 | tf_op jit(solution)/shard_map/ppermute | solution.py:224
  3.6 21.3 %collective-permute-start.3 = (f32[64,4096]{1,0:T(8,128)}, f32[64,4096]{1,0:T(8,128)S(1)}, u32[]{:S(2)}, u32[]{:S(2)}) collective-permute-start(f32[64,4096]{1,0:T(8,128)} %bitcast.7), channel_id=1, source_target_pairs={{0,1},{1,0},{2,3},{3,2},{4,5},{5,4},{6,7},{7,6},{8,9},{9,8},{10,11... | collective-permute-start | bytes 3145736 | tf_op jit(solution)/shard_map/ppermute | solution.py:203
  3.6 21.3 %collective-permute-start.4 = (f32[64,4096]{1,0:T(8,128)}, f32[64,4096]{1,0:T(8,128)S(1)}, u32[]{:S(2)}, u32[]{:S(2)}) collective-permute-start(f32[64,4096]{1,0:T(8,128)} %bitcast.2), channel_id=1, source_target_pairs={{0,1},{1,0},{2,3},{3,2},{4,5},{5,4},{6,7},{7,6},{8,9},{9,8},{10,11... | collective-permute-start | bytes 3145736 | tf_op jit(solution)/shard_map/ppermute | solution.py:203
  6.2 18.7 %collective-permute-start = (f32[640,256]{1,0:T(8,128)}, f32[640,256]{1,0:T(8,128)S(1)}, u32[]{:S(2)}, u32[]{:S(2)}) collective-permute-start(f32[640,256]{1,0:T(8,128)} %shard_map.103), channel_id=1, source_target_pairs={{0,8},{8,16},{16,24},{24,0},{1,9},{9,17},{17,25},{25,1},{2,10},{10... | collective-permute-start | bytes 1966088 | tf_op jit(solution)/shard_map/ppermute | solution.py:206
  7.8 20.9 %collective-permute-start.9 = (f32[64,4096]{1,0:T(8,128)}, f32[64,4096]{1,0:T(8,128)S(1)}, u32[]{:S(2)}, u32[]{:S(2)}) collective-permute-start(f32[64,4096]{1,0:T(8,128)} %bitcast.3), channel_id=1, source_target_pairs={{0,2},{1,5},{2,0},{3,7},{4,6},{5,1},{6,4},{7,3},{8,10},{9,13},{10,... | collective-permute-start | bytes 3145736 | tf_op jit(solution)/shard_map/ppermute | solution.py:224
  16.6 12.1 %collective-permute-start.8 = (f32[64,4096]{1,0:T(8,128)S(1)}, f32[64,4096]{1,0:T(8,128)S(1)}, u32[]{:S(2)}, u32[]{:S(2)}) collective-permute-start(f32[64,4096]{1,0:T(8,128)S(1)} %collective-permute-done.7.refs_4_), channel_id=1, source_target_pairs={{0,1},{1,0},{2,3},{3,2},{4,5},{5,4},{6,7},{7,6},{8,9},{9,8},{10,11... | collective-permute-start | bytes 3145736 | tf_op jit(solution)/shard_map/ppermute | solution.py:203
  25.0 19.1 %collective-permute-start.5 = (f32[64,4096]{1,0:T(8,128)}, f32[64,4096]{1,0:T(8,128)S(1)}, u32[]{:S(2)}, u32[]{:S(2)}) collective-permute-start(f32[64,4096]{1,0:T(8,128)} %bitcast.8), channel_id=1, source_target_pairs={{0,4},{1,3},{2,6},{3,1},{4,0},{5,7},{6,2},{7,5},{8,12},{9,11},{10,... | collective-permute-start | bytes 3145736 | tf_op jit(solution)/shard_map/ppermute | solution.py:224
  26.5 24.7 %collective-permute-start.6 = (f32[64,4096]{1,0:T(8,128)}, f32[64,4096]{1,0:T(8,128)S(1)}, u32[]{:S(2)}, u32[]{:S(2)}) collective-permute-start(f32[64,4096]{1,0:T(8,128)} %bitcast.4), channel_id=1, source_target_pairs={{0,4},{1,3},{2,6},{3,1},{4,0},{5,7},{6,2},{7,5},{8,12},{9,11},{10,... | collective-permute-start | bytes 3145736 | tf_op jit(solution)/shard_map/ppermute | solution.py:224
  27.0 17.1 %collective-permute-start.1 = (f32[640,256]{1,0:T(8,128)S(1)}, f32[640,256]{1,0:T(8,128)S(1)}, u32[]{:S(2)}, u32[]{:S(2)}) collective-permute-start(f32[640,256]{1,0:T(8,128)S(1)} %collective-permute-done.refs_5_), channel_id=1, source_target_pairs={{0,8},{8,16},{16,24},{24,0},{1,9},{9,17},{17,25},{25,1},{2,10},{10... | collective-permute-start | bytes 1966088 | tf_op jit(solution)/shard_map/ppermute | solution.py:206
  28.7 24.3 %collective-permute-start.10 = (f32[64,4096]{1,0:T(8,128)S(1)}, f32[64,4096]{1,0:T(8,128)S(1)}, u32[]{:S(2)}, u32[]{:S(2)}) collective-permute-start(f32[64,4096]{1,0:T(8,128)S(1)} %collective-permute-done.9.refs_5_), channel_id=1, source_target_pairs={{0,1},{1,0},{2,3},{3,2},{4,5},{5,4},{6,7},{7,6},{8,9},{9,8},{10,11... | collective-permute-start | bytes 3145736 | tf_op jit(solution)/shard_map/ppermute | solution.py:203
  44.1 17.2 %collective-permute-start.2 = (f32[640,256]{1,0:T(8,128)S(1)}, f32[640,256]{1,0:T(8,128)S(1)}, u32[]{:S(2)}, u32[]{:S(2)}) collective-permute-start(f32[640,256]{1,0:T(8,128)S(1)} %collective-permute-done.1.refs_6_), channel_id=1, source_target_pairs={{0,8},{8,16},{16,24},{24,0},{1,9},{9,17},{17,25},{25,1},{2,10},{10... | collective-permute-start | bytes 1966088 | tf_op jit(solution)/shard_map/ppermute | solution.py:206
  51.4 9.2 %collective-permute-start.16 = (f32[128,1024]{1,0:T(8,128)S(1)}, f32[128,1024]{1,0:T(8,128)S(1)}, u32[]{:S(2)}, u32[]{:S(2)}) collective-permute-start(f32[128,1024]{1,0:T(8,128)S(1)} %pad_maximum_fusion.4), channel_id=1, source_target_pairs={{0,4},{1,3},{2,6},{3,1},{4,0},{5,7},{6,2},{7,5},{8,12},{9,11},{10,... | collective-permute-start | bytes 1572872 | tf_op jit(solution)/shard_map/ppermute | solution.py:224
  53.0 8.5 %collective-permute-start.11 = (f32[384,256]{1,0:T(8,128)S(1)}, f32[384,256]{1,0:T(8,128)S(1)}, u32[]{:S(2)}, u32[]{:S(2)}) collective-permute-start(f32[384,256]{1,0:T(8,128)S(1)} %slice.36), channel_id=1, source_target_pairs={{0,1},{1,0},{2,3},{3,2},{4,5},{5,4},{6,7},{7,6},{8,9},{9,8},{10,11... | collective-permute-start | bytes 1179656 | tf_op jit(solution)/shard_map/ppermute | solution.py:203
  53.1 13.1 %collective-permute-start.17 = (f32[128,1024]{1,0:T(8,128)S(1)}, f32[128,1024]{1,0:T(8,128)S(1)}, u32[]{:S(2)}, u32[]{:S(2)}) collective-permute-start(f32[128,1024]{1,0:T(8,128)S(1)} %pad_maximum_fusion.5), channel_id=1, source_target_pairs={{0,4},{1,3},{2,6},{3,1},{4,0},{5,7},{6,2},{7,5},{8,12},{9,11},{10,... | collective-permute-start | bytes 1572872 | tf_op jit(solution)/shard_map/ppermute | solution.py:224
  60.6 5.6 %collective-permute-start.18 = (f32[128,1024]{1,0:T(8,128)S(1)}, f32[128,1024]{1,0:T(8,128)S(1)}, u32[]{:S(2)}, u32[]{:S(2)}) collective-permute-start(f32[128,1024]{1,0:T(8,128)S(1)} %collective-permute-done.16), channel_id=1, source_target_pairs={{0,1},{1,0},{2,3},{3,2},{4,5},{5,4},{6,7},{7,6},{8,9},{9,8},{10,11... | collective-permute-start | bytes 1572872 | tf_op jit(solution)/shard_map/ppermute | solution.py:203
  60.7 8.7 %collective-permute-start.13 = (f32[64,4096]{1,0:T(8,128)S(1)}, f32[64,4096]{1,0:T(8,128)S(1)}, u32[]{:S(2)}, u32[]{:S(2)}) collective-permute-start(f32[64,4096]{1,0:T(8,128)S(1)} %collective-permute-done.5.refs_8_), channel_id=1, source_target_pairs={{0,1},{1,0},{2,3},{3,2},{4,5},{5,4},{6,7},{7,6},{8,9},{9,8},{10,11... | collective-permute-start | bytes 3145736 | tf_op jit(solution)/shard_map/ppermute | solution.py:203
  61.3 8.1 %collective-permute-start.14 = (f32[64,4096]{1,0:T(8,128)S(1)}, f32[64,4096]{1,0:T(8,128)S(1)}, u32[]{:S(2)}, u32[]{:S(2)}) collective-permute-start(f32[64,4096]{1,0:T(8,128)S(1)} %collective-permute-done.6.refs_9_), channel_id=1, source_target_pairs={{0,1},{1,0},{2,3},{3,2},{4,5},{5,4},{6,7},{7,6},{8,9},{9,8},{10,11... | collective-permute-start | bytes 3145736 | tf_op jit(solution)/shard_map/ppermute | solution.py:203
  61.5 7.9 %copy-start.3 = (f32[128,512]{1,0:T(8,128)S(1)}, f32[128,512]{1,0:T(8,128)}, u32[]{:S(2)}) copy-start(f32[128,512]{1,0:T(8,128)} %refs_0_.3) | copy-start | bytes 786436
  61.5 7.9 %copy-start.4 = (f32[128,512]{1,0:T(8,128)S(1)}, f32[128,512]{1,0:T(8,128)}, u32[]{:S(2)}) copy-start(f32[128,512]{1,0:T(8,128)} %refs_1_.3) | copy-start | bytes 786436
  61.5 7.9 %copy-start.5 = (f32[128,512]{1,0:T(8,128)S(1)}, f32[128,512]{1,0:T(8,128)}, u32[]{:S(2)}) copy-start(f32[128,512]{1,0:T(8,128)} %refs_2_.3) | copy-start | bytes 786436
  61.5 7.9 %copy-start.6 = (f32[128,256]{1,0:T(8,128)S(1)}, f32[128,256]{1,0:T(8,128)}, u32[]{:S(2)}) copy-start(f32[128,256]{1,0:T(8,128)} %refs_3_.3) | copy-start | bytes 393220
  61.5 7.9 %copy-start.7 = (f32[128,256]{1,0:T(8,128)S(1)}, f32[128,256]{1,0:T(8,128)}, u32[]{:S(2)}) copy-start(f32[128,256]{1,0:T(8,128)} %refs_4_.3) | copy-start | bytes 393220
  61.5 19.7 %collective-permute-start.15 = (f32[128,2048]{1,0:T(8,128)S(1)}, f32[128,2048]{1,0:T(8,128)S(1)}, u32[]{:S(2)}, u32[]{:S(2)}) collective-permute-start(f32[128,2048]{1,0:T(8,128)S(1)} %pad_maximum_fusion), channel_id=1, source_target_pairs={{0,4},{1,3},{2,6},{3,1},{4,0},{5,7},{6,2},{7,5},{8,12},{9,11},{10,... | collective-permute-start | bytes 3145736 | tf_op jit(solution)/shard_map/ppermute | solution.py:224
  63.2 9.7 %copy-start = (f32[4096,256]{1,0:T(8,128)S(1)}, f32[4096,256]{1,0:T(8,128)}, u32[]{:S(2)}) copy-start(f32[4096,256]{1,0:T(8,128)} %refs_18_.1) | copy-start | bytes 12582916
  63.3 9.7 %copy-start.1 = (f32[4096,64]{0,1:T(8,128)S(1)}, f32[4096,64]{0,1:T(8,128)}, u32[]{:S(2)}) copy-start(f32[4096,64]{0,1:T(8,128)} %param.12) | copy-start | bytes 3145732
  63.3 9.7 %copy-start.2 = (f32[4096,64]{0,1:T(8,128)S(1)}, f32[4096,64]{0,1:T(8,128)}, u32[]{:S(2)}) copy-start(f32[4096,64]{0,1:T(8,128)} %param.11) | copy-start | bytes 3145732
  66.2 3.2 %collective-permute-start.12 = (f32[768,256]{1,0:T(8,128)S(1)}, f32[768,256]{1,0:T(8,128)S(1)}, u32[]{:S(2)}, u32[]{:S(2)}) collective-permute-start(f32[768,256]{1,0:T(8,128)S(1)} %pad_maximum_fusion.3), channel_id=1, source_target_pairs={{0,1},{1,0},{2,3},{3,2},{4,5},{5,4},{6,7},{7,6},{8,9},{9,8},{10,11... | collective-permute-start | bytes 2359304 | tf_op jit(solution)/shard_map/ppermute | solution.py:203
  66.2 3.0 %collective-permute-start.19 = (f32[128,1024]{1,0:T(8,128)S(1)}, f32[128,1024]{1,0:T(8,128)S(1)}, u32[]{:S(2)}, u32[]{:S(2)}) collective-permute-start(f32[128,1024]{1,0:T(8,128)S(1)} %collective-permute-done.17), channel_id=1, source_target_pairs={{0,1},{1,0},{2,3},{3,2},{4,5},{5,4},{6,7},{7,6},{8,9},{9,8},{10,11... | collective-permute-start | bytes 1572872 | tf_op jit(solution)/shard_map/ppermute | solution.py:203
  81.2 2.7 %collective-permute-start.20 = (f32[128,2048]{1,0:T(8,128)S(1)}, f32[128,2048]{1,0:T(8,128)S(1)}, u32[]{:S(2)}, u32[]{:S(2)}) collective-permute-start(f32[128,2048]{1,0:T(8,128)S(1)} %collective-permute-done.15.refs_0_), channel_id=1, source_target_pairs={{0,1},{1,0},{2,3},{3,2},{4,5},{5,4},{6,7},{7,6},{8,9},{9,8},{10,11... | collective-permute-start | bytes 3145736 | tf_op jit(solution)/shard_map/ppermute | solution.py:203

commit v3 on v2

--- a/solution.py
+++ b/solution.py
@@ -73,8 +73,12 @@
     even = lax.rem(lane, 2) == 0
     rows, width = own[3].shape[0], matrices.shape[2] // 2
 
+    place = jnp.where(lax.rem(here, 2) == 0, here // 2, steps - (here + 1) // 2)
+
     def at(step):
-        return pl.ds(pl.multiple_of(lax.rem(here + steps - step, steps) * rows, rows), rows)
+        back = lax.rem(place + steps - step, steps)
+        source = jnp.where(2 * back < steps, 2 * back, 2 * steps - 1 - 2 * back)
+        return pl.ds(pl.multiple_of(source * rows, rows), rows)
 
     for k in range(3):
         matrices[k, at(0), :] = own[k][...]
@@ -85,7 +89,7 @@
         right_second[at(j + 1), :] = piece[4 * rows :, :]
         for k in range(3):
             mine = piece[k * rows : (k + 1) * rows, :]
-            others, at_row = (late, 3 * (j - 1) + k) if j else (early, k)
+            others, at_row = (early, 3 * j + k) if j < steps - 2 else (late, k)
             other = others[at_row * rows : (at_row + 1) * rows, :]
             matrices[k, at(j + 1), :width] = jnp.where(even, mine, other)
             matrices[k, at(j + 1), width:] = jnp.where(even, other, mine)
@@ -202,8 +206,10 @@
     def swap(value, bit):
         return lax.ppermute(value, "col", [(i, i ^ bit) for i in range(col_count)])
 
-    def shift(value, by):
-        return lax.ppermute(value, "row", [(i, (i + by) % row_count) for i in range(row_count)])
+    ring = [*range(0, row_count, 2), *reversed(range(1, row_count, 2))]
+
+    def onward(value):
+        return lax.ppermute(value, "row", list(zip(ring, ring[1:] + ring[:1])))
 
     def per_device(
         inverse_first, inverse_second, coupling, panel_first, panel_second,
@@ -232,31 +238,35 @@
         near_0 = tuple(cross(x, ONE) for x in (first, second))
         own_beside = beside((first, second))
         matrix_rows = 3 * rhs_first.shape[0]
-        packs = [shift(pack_rows(own), 1)]
+        packs = [onward(pack_rows(own))]
         near_1 = tuple(cross(x, OTHER) for x in after((first, second), own_beside, packs[0]))
-        for _ in range(row_count - 2):
-            packs.append(shift(packs[-1], 1))
-        beside_0 = swap(near_0[0], CORE)
-        beside_0 = beside_0, swap(after(near_0[1], beside_0), CORE)
-        early = swap(after(packs[0][:matrix_rows], near_1, beside_0), CORE)
-        late = swap(after(jnp.concatenate([p[:matrix_rows] for p in packs[1:]], axis=0), early), CORE)
-        others = [early, late]
-        cuts = [0, rest // 4, rest // 2, rest]
-        far = [
-            cross(jnp.concatenate([x[:, a:b] for x in after(near_0, near_1)], axis=0), OTHER)
-            for a, b in zip(cuts[:-1], cuts[1:])
-        ]
-        beside_1 = beside(near_1)
+        beside_0 = beside(near_0)
+        for j in range(row_count - 2):
+            packs.append(onward(after(packs[-1], beside_0[0]) if j == row_count - 3 else packs[-1]))
+        cut = first.shape[0] // 2
+        beside_1 = beside((near_1[0][:cut], near_1[0][cut:]))
+        cuts = [0, rest // 2, rest]
+
+        def far_part(pair, a, b):
+            return cross(jnp.concatenate([x[:, a:b] for x in pair], axis=0), OTHER)
+
+        far = [far_part(near_0, cuts[0], cuts[1])]
+        early = swap(jnp.concatenate([p[:matrix_rows] for p in packs[:-1]], axis=0), CORE)
+        near_0, near_1, beside_0, beside_1, packs, early = lax.optimization_barrier(
+            (near_0, near_1, beside_0, beside_1, packs, early)
+        )
+        far += [far_part(near_0, a, b) for a, b in zip(cuts[1:-1], cuts[2:])]
+        others = early, swap(packs[-1][:matrix_rows], CORE)
+        beside_1 = *beside_1, swap(near_1[1], CORE)
         near = [
             panel
             for pair in ((first, second), own_beside, near_0, beside_0, near_1, beside_1)
             for panel in pair
         ]
-        *factors, solved_first, solved_second = solve(row_count, block, own, packs, after(others, beside_1))
+        *factors, solved_first, solved_second = solve(row_count, block, own, packs, others)
         near_factor, far_factor = factors[:2], factors[2:]
-        lead = [jnp.concatenate(x, axis=1) for x in (far[:2], [swap(panel, CORE) for panel in far[:2]])]
-        updated = update(near, near_factor, lead, far_factor, rhs_rest, 0, 1024, False)
-        for start, panel in zip(cuts[2:], far[2:]):
+        updated = update(near, near_factor, [far[0], swap(after(far[0], others), CORE)], far_factor, rhs_rest, 0, 1024, False)
+        for start, panel in zip(cuts[1:], far[1:]):
             panel = after(panel, updated)
             updated = update([], None, [panel, swap(panel, CORE)], far_factor, updated, start, 512, True)
         return solved_first, solved_second, updated

time: 87.4 us -> 82.7 us (0.946)
  waiting for transfers between devices: 55.2 us -> 41.9 us
  starting transfers between devices: 13.3 us -> 22.2 us
    ppermute x7 -> x6, waiting for transfers between devices: 26.5 us -> 14.7 us  [cross(): lax.ppermute(value, 'col', [(i, i ^ masks[i % 2]) for i in range(col_coun...]
    ppermute x3, starting transfers between devices: 1.58 us -> 9.24 us  [onward(): return lax.ppermute(value, 'row', list(zip(ring, ring[1:] + ring[:1])))]
    ppermute x3, waiting for transfers between devices: 23.7 us -> 21.6 us  [onward(): return lax.ppermute(value, 'row', list(zip(ring, ring[1:] + ring[:1])))]
    ppermute x7 -> x6, starting transfers between devices: 9.79 us -> 10.3 us  [cross(): lax.ppermute(value, 'col', [(i, i ^ masks[i % 2]) for i in range(col_coun...]
  transfers between devices with their start and end apart: 21 -> 20, of which waited for: 9 -> 12; matrix products, arithmetic and copies ran while one was open for 1% -> 1% of each run, Pallas kernels for 16% -> 17%
where the time goes in v3:
time: 82.7 us; the launch traced here: 82.5 us
  waiting for transfers between devices  41.9 us (51%)
  starting transfers between devices  22.2 us (27%)
  Pallas kernels  17.1 us (21%)
  between operations  0.83 us (1%)
    ppermute x3, waiting for transfers between devices, onward(): return lax.ppermute(value, 'row', list(zip(ring, ring[1:] + ring[:1])))  21.6 us
    ppermute x6, waiting for transfers between devices, cross(): lax.ppermute(value, 'col', [(i, i ^ masks[i % 2]) for i in range(col_coun...  14.7 us
    pallas_call x2, Pallas kernels, update(): pl.pallas_call(functools.partial(update_kernel, len(near), len(far), star...  11.6 us
    ppermute x6, starting transfers between devices, cross(): lax.ppermute(value, 'col', [(i, i ^ masks[i % 2]) for i in range(col_coun...  10.3 us
    ppermute x3, starting transfers between devices, onward(): return lax.ppermute(value, 'row', list(zip(ring, ring[1:] + ring[:1])))  9.24 us
    ppermute x11, waiting for transfers between devices, swap(): return lax.ppermute(value, 'col', [(i, i ^ bit) for i in range(col_count)])  5.62 us
    pallas_call x1, Pallas kernels, solve(): pl.pallas_call(functools.partial(solve_kernel, steps, block), out_shape=o...  3.34 us
    ppermute x11, starting transfers between devices, swap(): return lax.ppermute(value, 'col', [(i, i ^ bit) for i in range(col_count)])  2.68 us
  transfers between devices with their start and end apart: 20, of which 12 were waited for; matrix products, arithmetic and copies ran while one was open for 1% of the time, Pallas kernels for 17%

profile of v3, /device:TPU:0, one launch (start us, length us, event | category | flops | bytes accessed | tf_op | source)
XLA Modules:
  0.0 82.5 jit_solution(9267158386407850646)
XLA Ops:
  0.6 3.0 %collective-permute-start = (f32[64,4096]{1,0:T(8,128)}, f32[64,4096]{1,0:T(8,128)S(1)}, u32[]{:S(2)}, u32[]{:S(2)}) collective-permute-start(f32[64,4096]{1,0:T(8,128)} %bitcast.6), channel_id=1, source_target_pairs={{0,2},{1,5},{2,0},{3,7},{4,6},{5,1},{6,4},{7,3},{8,10},{9,13},{10,... | collective-permute-start | bytes 3145736 | tf_op jit(solution)/shard_map/ppermute | solution.py:230
  3.6 0.0 collective-permute-start.2
  3.6 0.5 collective-permute-start.3
  4.1 2.1 %shard_map.103 = f32[640,256]{1,0:T(8,128)} custom-call(f32[128,512]{1,0:T(8,128)} %refs_0_.3, f32[128,512]{1,0:T(8,128)} %refs_1_.3, f32[128,512]{1,0:T(8,128)} %refs_2_.3, f32[128,256]{1,0:T(8,128)} %refs_3_.3, f32[128,256]{1,0:T(8,128)} %refs_4_.3), custom_call_target="tpu_custom_call" | custom-call | flops 1024 | bytes 1024 | tf_op jit(solution)/shard_map/pallas_call | solution.py:57
  6.2 2.6 %collective-permute-start.4 = (f32[640,256]{1,0:T(8,128)}, f32[640,256]{1,0:T(8,128)S(1)}, u32[]{:S(2)}, u32[]{:S(2)}) collective-permute-start(f32[640,256]{1,0:T(8,128)} %shard_map.103), channel_id=1, source_target_pairs={{0,16},{16,24},{24,8},{8,0},{1,17},{17,25},{25,9},{9,1},{2,18},{18... | collective-permute-start | bytes 1966088 | tf_op jit(solution)/shard_map/ppermute | solution.py:212
  8.8 0.6 collective-permute-start.1
  9.4 7.2 %collective-permute-done.refs_4_ = f32[64,4096]{1,0:T(8,128)S(1)} collective-permute-done((f32[64,4096]{1,0:T(8,128)}, f32[64,4096]{1,0:T(8,128)S(1)}, u32[]{:S(2)}, u32[]{:S(2)}) %collective-permute-start) | collective-permute-done | bytes 1048608 | tf_op jit(solution)/shard_map/ppermute | solution.py:230
  16.6 0.0 collective-permute-start.7
  16.6 6.7 %collective-permute-done.4.refs_5_ = f32[640,256]{1,0:T(8,128)S(1)} collective-permute-done((f32[640,256]{1,0:T(8,128)}, f32[640,256]{1,0:T(8,128)S(1)}, u32[]{:S(2)}, u32[]{:S(2)}) %collective-permute-start.4) | collective-permute-done | bytes 655392 | tf_op jit(solution)/shard_map/ppermute | solution.py:212
  23.3 0.0 collective-permute-done.2.refs_2_
  23.3 0.0 collective-permute-done.3.refs_3_
  23.3 1.5 %collective-permute-start.5 = (f32[64,4096]{1,0:T(8,128)}, f32[64,4096]{1,0:T(8,128)S(1)}, u32[]{:S(2)}, u32[]{:S(2)}) collective-permute-start(f32[64,4096]{1,0:T(8,128)} %bitcast.8), channel_id=1, source_target_pairs={{0,4},{1,3},{2,6},{3,1},{4,0},{5,7},{6,2},{7,5},{8,12},{9,11},{10,... | collective-permute-start | bytes 3145736 | tf_op jit(solution)/shard_map/ppermute | solution.py:230
  24.8 3.3 %collective-permute-start.11 = (f32[640,256]{1,0:T(8,128)S(1)}, f32[640,256]{1,0:T(8,128)S(1)}, u32[]{:S(2)}, u32[]{:S(2)}) collective-permute-start(f32[640,256]{1,0:T(8,128)S(1)} %collective-permute-done.4.refs_5_), channel_id=1, source_target_pairs={{0,16},{16,24},{24,8},{8,0},{1,17},{17,25},{25,9},{9,1},{2,18},{18... | collective-permute-start | bytes 1966088 | tf_op jit(solution)/shard_map/ppermute | solution.py:212
  28.1 0.6 collective-permute-start.6
  28.8 1.6 %collective-permute-done.1.refs_5_ = f32[64,4096]{1,0:T(8,128)S(1)} collective-permute-done((f32[64,4096]{1,0:T(8,128)}, f32[64,4096]{1,0:T(8,128)S(1)}, u32[]{:S(2)}, u32[]{:S(2)}) %collective-permute-start.1) | collective-permute-done | bytes 1048608 | tf_op jit(solution)/shard_map/ppermute | solution.py:230
  30.4 0.1 pad_maximum_fusion.1
  30.5 2.7 %collective-permute-start.17 = (f32[128,2048]{1,0:T(8,128)S(1)}, f32[128,2048]{1,0:T(8,128)S(1)}, u32[]{:S(2)}, u32[]{:S(2)}) collective-permute-start(f32[128,2048]{1,0:T(8,128)S(1)} %pad_maximum_fusion.1), channel_id=1, source_target_pairs={{0,4},{1,3},{2,6},{3,1},{4,0},{5,7},{6,2},{7,5},{8,12},{9,11},{10,... | collective-permute-start | bytes 3145736 | tf_op jit(solution)/shard_map/ppermute | solution.py:230
  33.2 8.0 %collective-permute-done.11.refs_6_ = f32[640,256]{1,0:T(8,128)S(1)} collective-permute-done((f32[640,256]{1,0:T(8,128)S(1)}, f32[640,256]{1,0:T(8,128)S(1)}, u32[]{:S(2)}, u32[]{:S(2)}) %collective-permute-start.11) | collective-permute-done | bytes 655392 | tf_op jit(solution)/shard_map/ppermute | solution.py:212
  41.3 0.0 collective-permute-start.8
  41.3 0.0 copy-start.3
  41.3 0.0 copy-start.4
  41.3 0.0 copy-start.5
  41.3 0.0 copy-start.6
  41.3 0.0 copy-start.7
  41.4 0.1 pad_maximum_fusion.2
  41.4 0.0 collective-permute-done.7.refs_6_
  41.4 0.6 collective-permute-start.13
  42.0 0.0 collective-permute-done.5.refs_8_
  42.0 3.4 %collective-permute-start.12 = (f32[640,256]{1,0:T(8,128)S(1)}, f32[640,256]{1,0:T(8,128)S(1)}, u32[]{:S(2)}, u32[]{:S(2)}) collective-permute-start(f32[640,256]{1,0:T(8,128)S(1)} %collective-permute-done.11.refs_6_), channel_id=1, source_target_pairs={{0,16},{16,24},{24,8},{8,0},{1,17},{17,25},{25,9},{9,1},{2,18},{18... | collective-permute-start | bytes 1966088 | tf_op jit(solution)/shard_map/ppermute | solution.py:212
  45.4 0.1 fusion
  45.5 4.1 %collective-permute-done.6.refs_9_ = f32[64,4096]{1,0:T(8,128)S(1)} collective-permute-done((f32[64,4096]{1,0:T(8,128)}, f32[64,4096]{1,0:T(8,128)S(1)}, u32[]{:S(2)}, u32[]{:S(2)}) %collective-permute-start.6) | collective-permute-done | bytes 1048608 | tf_op jit(solution)/shard_map/ppermute | solution.py:230
  49.6 0.9 %collective-permute-start.10 = (f32[32,4096]{1,0:T(8,128)S(1)}, f32[32,4096]{1,0:T(8,128)S(1)}, u32[]{:S(2)}, u32[]{:S(2)}) collective-permute-start(f32[32,4096]{1,0:T(8,128)S(1)} %get-tuple-element.49), channel_id=1, source_target_pairs={{0,1},{1,0},{2,3},{3,2},{4,5},{5,4},{6,7},{7,6},{8,9},{9,8},{10,11... | collective-permute-start | bytes 1572872 | tf_op jit(solution)/shard_map/ppermute | solution.py:207
  50.4 0.0 collective-permute-done.13.refs_8_
  50.4 0.0 collective-permute-start.9
  50.5 0.0 collective-permute-done.8.refs_7_
  50.5 1.5 %collective-permute-done.10.refs_11_ = f32[32,4096]{1,0:T(8,128)S(1)} collective-permute-done((f32[32,4096]{1,0:T(8,128)S(1)}, f32[32,4096]{1,0:T(8,128)S(1)}, u32[]{:S(2)}, u32[]{:S(2)}) %collective-permute-start.10) | collective-permute-done | bytes 524320 | tf_op jit(solution)/shard_map/ppermute | solution.py:207
  52.0 0.7 collective-permute-done.9.refs_10_
  52.7 6.9 %collective-permute-done.12.refs_7_ = f32[640,256]{1,0:T(8,128)S(1)} collective-permute-done((f32[640,256]{1,0:T(8,128)S(1)}, f32[640,256]{1,0:T(8,128)S(1)}, u32[]{:S(2)}, u32[]{:S(2)}) %collective-permute-start.12) | collective-permute-done | bytes 655392 | tf_op jit(solution)/shard_map/ppermute | solution.py:212
  59.6 0.0 copy-start
  59.7 0.0 copy-start.1
  59.7 0.0 copy-start.2
  59.7 0.1 collective-permute-start.14
  59.8 0.5 collective-permute-start.16
  60.3 0.5 collective-permute-done.17.refs_13_
  60.8 0.7 collective-permute-done.14.refs_9_
  61.5 0.1 collective-permute-start.18
  61.6 0.1 pad_maximum_fusion
  61.7 1.9 %collective-permute-start.15 = (f32[128,2048]{1,0:T(8,128)S(1)}, f32[128,2048]{1,0:T(8,128)S(1)}, u32[]{:S(2)}, u32[]{:S(2)}) collective-permute-start(f32[128,2048]{1,0:T(8,128)S(1)} %pad_maximum_fusion), channel_id=1, source_target_pairs={{0,4},{1,3},{2,6},{3,1},{4,0},{5,7},{6,2},{7,5},{8,12},{9,11},{10,... | collective-permute-start | bytes 3145736 | tf_op jit(solution)/shard_map/ppermute | solution.py:230
  63.6 0.0 copy-done.3
  63.6 0.0 copy-done.4
  63.6 0.0 copy-done.5
  63.6 0.0 copy-done.6
  63.6 0.0 copy-done.7
  63.6 3.3 %shard_map.104 = (bf16[768,256]{1,0:T(8,128)(2,1)S(1)}, bf16[768,256]{1,0:T(8,128)(2,1)S(1)}, bf16[256,256]{1,0:T(8,128)(2,1)S(1)}, bf16[256,256]{1,0:T(8,128)(2...) custom-call(f32[128,512]{1,0:T(8,128)S(1)} %copy-done.3, f32[128,512]{1,0:T(8,128)S(1)} %copy-done.4, ...), custom_call_target="tpu_custom_call" | custom-call | flops 1024 | bytes 1024 | tf_op jit(solution)/shard_map/pallas_call | solution.py:127
  67.0 0.0 collective-permute-done.16.refs_12_
  67.0 0.0 collective-permute-done.18.refs_14_
  67.0 0.0 copy-done
  67.0 0.0 copy-done.1
  67.0 0.0 copy-done.2
  67.0 8.3 %shard_map.105.refs_4_ = f32[4096,256]{1,0:T(8,128)} custom-call(f32[64,4096]{1,0:T(8,128)S(1)} %bitcast.9, f32[64,4096]{1,0:T(8,128)S(1)} %bitcast.5, f32[64,4096]{1,0:T(8,128)S(1)} %collective-permute-done.2.refs_2_, f32[64,4096]{1,0:T(8,128)S(1)} %collective-permute-done.3.refs_3_, f32[64,4096]{1,0:T(8,128)S(1)} %collective-permute-done.refs_4_, ...), custom_call_target="tpu_custom_call" | custom-call | flops 1024 | bytes 1024 | tf_op jit(solution)/shard_map/pallas_call | solution.py:187
  75.3 1.3 %collective-permute-done.15.refs_0_ = f32[128,2048]{1,0:T(8,128)S(1)} collective-permute-done((f32[128,2048]{1,0:T(8,128)S(1)}, f32[128,2048]{1,0:T(8,128)S(1)}, u32[]{:S(2)}, u32[]{:S(2)}) %collective-permute-start.15) | collective-permute-done | bytes 1048608 | tf_op jit(solution)/shard_map/ppermute | solution.py:230
  76.6 0.0 collective-permute-start.19
  76.6 2.7 %collective-permute-done.19.refs_1_ = f32[128,2048]{1,0:T(8,128)S(1)} collective-permute-done((f32[128,2048]{1,0:T(8,128)S(1)}, f32[128,2048]{1,0:T(8,128)S(1)}, u32[]{:S(2)}, u32[]{:S(2)}) %collective-permute-start.19) | collective-permute-done | bytes 1048608 | tf_op jit(solution)/shard_map/ppermute | solution.py:207
  79.2 3.3 %shard_map.106 = f32[4096,256]{1,0:T(8,128)} custom-call(f32[128,2048]{1,0:T(8,128)S(1)} %collective-permute-done.15.refs_0_, f32[128,2048]{1,0:T(8,128)S(1)} %collective-permute-done.19.refs_1_, bf16[256,256]{1,0:T(8,128)(2,1)S(1)} %get-tuple-element.46.refs_17_.refs_2_, ...), custom_call_target="tpu_custom_call", output_to_operand_aliasing={{}: (4, {})} | custom-call | flops 1024 | bytes 1024 | tf_op jit(solution)/shard_map/pallas_call | solution.py:187
  (7 shorter events, 0.2 us)
Async XLA Ops:
  0.6 16.0 %collective-permute-start = (f32[64,4096]{1,0:T(8,128)}, f32[64,4096]{1,0:T(8,128)S(1)}, u32[]{:S(2)}, u32[]{:S(2)}) collective-permute-start(f32[64,4096]{1,0:T(8,128)} %bitcast.6), channel_id=1, source_target_pairs={{0,2},{1,5},{2,0},{3,7},{4,6},{5,1},{6,4},{7,3},{8,10},{9,13},{10,... | collective-permute-start | bytes 3145736 | tf_op jit(solution)/shard_map/ppermute | solution.py:230
  3.6 19.7 %collective-permute-start.2 = (f32[64,4096]{1,0:T(8,128)}, f32[64,4096]{1,0:T(8,128)S(1)}, u32[]{:S(2)}, u32[]{:S(2)}) collective-permute-start(f32[64,4096]{1,0:T(8,128)} %bitcast.7), channel_id=1, source_target_pairs={{0,1},{1,0},{2,3},{3,2},{4,5},{5,4},{6,7},{7,6},{8,9},{9,8},{10,11... | collective-permute-start | bytes 3145736 | tf_op jit(solution)/shard_map/ppermute | solution.py:207
  3.6 19.7 %collective-permute-start.3 = (f32[64,4096]{1,0:T(8,128)}, f32[64,4096]{1,0:T(8,128)S(1)}, u32[]{:S(2)}, u32[]{:S(2)}) collective-permute-start(f32[64,4096]{1,0:T(8,128)} %bitcast.2), channel_id=1, source_target_pairs={{0,1},{1,0},{2,3},{3,2},{4,5},{5,4},{6,7},{7,6},{8,9},{9,8},{10,11... | collective-permute-start | bytes 3145736 | tf_op jit(solution)/shard_map/ppermute | solution.py:207
  6.2 17.1 %collective-permute-start.4 = (f32[640,256]{1,0:T(8,128)}, f32[640,256]{1,0:T(8,128)S(1)}, u32[]{:S(2)}, u32[]{:S(2)}) collective-permute-start(f32[640,256]{1,0:T(8,128)} %shard_map.103), channel_id=1, source_target_pairs={{0,16},{16,24},{24,8},{8,0},{1,17},{17,25},{25,9},{9,1},{2,18},{18... | collective-permute-start | bytes 1966088 | tf_op jit(solution)/shard_map/ppermute | solution.py:212
  8.8 21.6 %collective-permute-start.1 = (f32[64,4096]{1,0:T(8,128)}, f32[64,4096]{1,0:T(8,128)S(1)}, u32[]{:S(2)}, u32[]{:S(2)}) collective-permute-start(f32[64,4096]{1,0:T(8,128)} %bitcast.3), channel_id=1, source_target_pairs={{0,2},{1,5},{2,0},{3,7},{4,6},{5,1},{6,4},{7,3},{8,10},{9,13},{10,... | collective-permute-start | bytes 3145736 | tf_op jit(solution)/shard_map/ppermute | solution.py:230
  16.6 24.8 %collective-permute-start.7 = (f32[64,4096]{1,0:T(8,128)S(1)}, f32[64,4096]{1,0:T(8,128)S(1)}, u32[]{:S(2)}, u32[]{:S(2)}) collective-permute-start(f32[64,4096]{1,0:T(8,128)S(1)} %collective-permute-done.refs_4_), channel_id=1, source_target_pairs={{0,1},{1,0},{2,3},{3,2},{4,5},{5,4},{6,7},{7,6},{8,9},{9,8},{10,11... | collective-permute-start | bytes 3145736 | tf_op jit(solution)/shard_map/ppermute | solution.py:207
  23.3 18.7 %collective-permute-start.5 = (f32[64,4096]{1,0:T(8,128)}, f32[64,4096]{1,0:T(8,128)S(1)}, u32[]{:S(2)}, u32[]{:S(2)}) collective-permute-start(f32[64,4096]{1,0:T(8,128)} %bitcast.8), channel_id=1, source_target_pairs={{0,4},{1,3},{2,6},{3,1},{4,0},{5,7},{6,2},{7,5},{8,12},{9,11},{10,... | collective-permute-start | bytes 3145736 | tf_op jit(solution)/shard_map/ppermute | solution.py:230
  24.8 16.4 %collective-permute-start.11 = (f32[640,256]{1,0:T(8,128)S(1)}, f32[640,256]{1,0:T(8,128)S(1)}, u32[]{:S(2)}, u32[]{:S(2)}) collective-permute-start(f32[640,256]{1,0:T(8,128)S(1)} %collective-permute-done.4.refs_5_), channel_id=1, source_target_pairs={{0,16},{16,24},{24,8},{8,0},{1,17},{17,25},{25,9},{9,1},{2,18},{18... | collective-permute-start | bytes 1966088 | tf_op jit(solution)/shard_map/ppermute | solution.py:212
  28.1 21.4 %collective-permute-start.6 = (f32[64,4096]{1,0:T(8,128)}, f32[64,4096]{1,0:T(8,128)S(1)}, u32[]{:S(2)}, u32[]{:S(2)}) collective-permute-start(f32[64,4096]{1,0:T(8,128)} %bitcast.4), channel_id=1, source_target_pairs={{0,4},{1,3},{2,6},{3,1},{4,0},{5,7},{6,2},{7,5},{8,12},{9,11},{10,... | collective-permute-start | bytes 3145736 | tf_op jit(solution)/shard_map/ppermute | solution.py:230
  30.5 30.3 %collective-permute-start.17 = (f32[128,2048]{1,0:T(8,128)S(1)}, f32[128,2048]{1,0:T(8,128)S(1)}, u32[]{:S(2)}, u32[]{:S(2)}) collective-permute-start(f32[128,2048]{1,0:T(8,128)S(1)} %pad_maximum_fusion.1), channel_id=1, source_target_pairs={{0,4},{1,3},{2,6},{3,1},{4,0},{5,7},{6,2},{7,5},{8,12},{9,11},{10,... | collective-permute-start | bytes 3145736 | tf_op jit(solution)/shard_map/ppermute | solution.py:230
  41.3 9.2 %collective-permute-start.8 = (f32[64,4096]{1,0:T(8,128)S(1)}, f32[64,4096]{1,0:T(8,128)S(1)}, u32[]{:S(2)}, u32[]{:S(2)}) collective-permute-start(f32[64,4096]{1,0:T(8,128)S(1)} %collective-permute-done.1.refs_5_), channel_id=1, source_target_pairs={{0,1},{1,0},{2,3},{3,2},{4,5},{5,4},{6,7},{7,6},{8,9},{9,8},{10,11... | collective-permute-start | bytes 3145736 | tf_op jit(solution)/shard_map/ppermute | solution.py:207
  41.3 22.3 %copy-start.3 = (f32[128,512]{1,0:T(8,128)S(1)}, f32[128,512]{1,0:T(8,128)}, u32[]{:S(2)}) copy-start(f32[128,512]{1,0:T(8,128)} %refs_0_.3) | copy-start | bytes 786436
  41.3 22.3 %copy-start.4 = (f32[128,512]{1,0:T(8,128)S(1)}, f32[128,512]{1,0:T(8,128)}, u32[]{:S(2)}) copy-start(f32[128,512]{1,0:T(8,128)} %refs_1_.3) | copy-start | bytes 786436
  41.3 22.3 %copy-start.5 = (f32[128,512]{1,0:T(8,128)S(1)}, f32[128,512]{1,0:T(8,128)}, u32[]{:S(2)}) copy-start(f32[128,512]{1,0:T(8,128)} %refs_2_.3) | copy-start | bytes 786436
  41.3 22.3 %copy-start.6 = (f32[128,256]{1,0:T(8,128)S(1)}, f32[128,256]{1,0:T(8,128)}, u32[]{:S(2)}) copy-start(f32[128,256]{1,0:T(8,128)} %refs_3_.3) | copy-start | bytes 393220
  41.3 22.3 %copy-start.7 = (f32[128,256]{1,0:T(8,128)S(1)}, f32[128,256]{1,0:T(8,128)}, u32[]{:S(2)}) copy-start(f32[128,256]{1,0:T(8,128)} %refs_4_.3) | copy-start | bytes 393220
  41.4 9.0 %collective-permute-start.13 = (f32[768,256]{1,0:T(8,128)S(1)}, f32[768,256]{1,0:T(8,128)S(1)}, u32[]{:S(2)}, u32[]{:S(2)}) collective-permute-start(f32[768,256]{1,0:T(8,128)S(1)} %pad_maximum_fusion.2), channel_id=1, source_target_pairs={{0,1},{1,0},{2,3},{3,2},{4,5},{5,4},{6,7},{7,6},{8,9},{9,8},{10,11... | collective-permute-start | bytes 2359304 | tf_op jit(solution)/shard_map/ppermute | solution.py:207
  42.0 17.6 %collective-permute-start.12 = (f32[640,256]{1,0:T(8,128)S(1)}, f32[640,256]{1,0:T(8,128)S(1)}, u32[]{:S(2)}, u32[]{:S(2)}) collective-permute-start(f32[640,256]{1,0:T(8,128)S(1)} %collective-permute-done.11.refs_6_), channel_id=1, source_target_pairs={{0,16},{16,24},{24,8},{8,0},{1,17},{17,25},{25,9},{9,1},{2,18},{18... | collective-permute-start | bytes 1966088 | tf_op jit(solution)/shard_map/ppermute | solution.py:212
  49.6 2.4 %collective-permute-start.10 = (f32[32,4096]{1,0:T(8,128)S(1)}, f32[32,4096]{1,0:T(8,128)S(1)}, u32[]{:S(2)}, u32[]{:S(2)}) collective-permute-start(f32[32,4096]{1,0:T(8,128)S(1)} %get-tuple-element.49), channel_id=1, source_target_pairs={{0,1},{1,0},{2,3},{3,2},{4,5},{5,4},{6,7},{7,6},{8,9},{9,8},{10,11... | collective-permute-start | bytes 1572872 | tf_op jit(solution)/shard_map/ppermute | solution.py:207
  50.4 2.3 %collective-permute-start.9 = (f32[32,4096]{1,0:T(8,128)S(1)}, f32[32,4096]{1,0:T(8,128)S(1)}, u32[]{:S(2)}, u32[]{:S(2)}) collective-permute-start(f32[32,4096]{1,0:T(8,128)S(1)} %get-tuple-element.50), channel_id=1, source_target_pairs={{0,1},{1,0},{2,3},{3,2},{4,5},{5,4},{6,7},{7,6},{8,9},{9,8},{10,11... | collective-permute-start | bytes 1572872 | tf_op jit(solution)/shard_map/ppermute | solution.py:207
  59.6 7.3 %copy-start = (f32[4096,256]{1,0:T(8,128)S(1)}, f32[4096,256]{1,0:T(8,128)}, u32[]{:S(2)}) copy-start(f32[4096,256]{1,0:T(8,128)} %refs_19_.1) | copy-start | bytes 12582916
  59.7 7.3 %copy-start.1 = (f32[4096,64]{0,1:T(8,128)S(1)}, f32[4096,64]{0,1:T(8,128)}, u32[]{:S(2)}) copy-start(f32[4096,64]{0,1:T(8,128)} %param.12) | copy-start | bytes 3145732
  59.7 7.3 %copy-start.2 = (f32[4096,64]{0,1:T(8,128)S(1)}, f32[4096,64]{0,1:T(8,128)}, u32[]{:S(2)}) copy-start(f32[4096,64]{0,1:T(8,128)} %param.11) | copy-start | bytes 3145732
  59.7 1.8 %collective-permute-start.14 = (f32[384,256]{1,0:T(8,128)S(1)}, f32[384,256]{1,0:T(8,128)S(1)}, u32[]{:S(2)}, u32[]{:S(2)}) collective-permute-start(f32[384,256]{1,0:T(8,128)S(1)} %slice.31), channel_id=1, source_target_pairs={{0,1},{1,0},{2,3},{3,2},{4,5},{5,4},{6,7},{7,6},{8,9},{9,8},{10,11... | collective-permute-start | bytes 1179656 | tf_op jit(solution)/shard_map/ppermute | solution.py:207
  59.8 7.2 %collective-permute-start.16 = (f32[64,4096]{1,0:T(8,128)S(1)}, f32[64,4096]{1,0:T(8,128)S(1)}, u32[]{:S(2)}, u32[]{:S(2)}) collective-permute-start(f32[64,4096]{1,0:T(8,128)S(1)} %collective-permute-done.6.refs_9_), channel_id=1, source_target_pairs={{0,1},{1,0},{2,3},{3,2},{4,5},{5,4},{6,7},{7,6},{8,9},{9,8},{10,11... | collective-permute-start | bytes 3145736 | tf_op jit(solution)/shard_map/ppermute | solution.py:207
  61.5 5.5 %collective-permute-start.18 = (f32[128,2048]{1,0:T(8,128)S(1)}, f32[128,2048]{1,0:T(8,128)S(1)}, u32[]{:S(2)}, u32[]{:S(2)}) collective-permute-start(f32[128,2048]{1,0:T(8,128)S(1)} %collective-permute-done.17.refs_13_), channel_id=1, source_target_pairs={{0,1},{1,0},{2,3},{3,2},{4,5},{5,4},{6,7},{7,6},{8,9},{9,8},{10,11... | collective-permute-start | bytes 3145736 | tf_op jit(solution)/shard_map/ppermute | solution.py:207
  61.7 14.9 %collective-permute-start.15 = (f32[128,2048]{1,0:T(8,128)S(1)}, f32[128,2048]{1,0:T(8,128)S(1)}, u32[]{:S(2)}, u32[]{:S(2)}) collective-permute-start(f32[128,2048]{1,0:T(8,128)S(1)} %pad_maximum_fusion), channel_id=1, source_target_pairs={{0,4},{1,3},{2,6},{3,1},{4,0},{5,7},{6,2},{7,5},{8,12},{9,11},{10,... | collective-permute-start | bytes 3145736 | tf_op jit(solution)/shard_map/ppermute | solution.py:230
  76.6 2.7 %collective-permute-start.19 = (f32[128,2048]{1,0:T(8,128)S(1)}, f32[128,2048]{1,0:T(8,128)S(1)}, u32[]{:S(2)}, u32[]{:S(2)}) collective-permute-start(f32[128,2048]{1,0:T(8,128)S(1)} %collective-permute-done.15.refs_0_), channel_id=1, source_target_pairs={{0,1},{1,0},{2,3},{3,2},{4,5},{5,4},{6,7},{7,6},{8,9},{9,8},{10,11... | collective-permute-start | bytes 3145736 | tf_op jit(solution)/shard_map/ppermute | solution.py:207

commit v4 on v3

--- a/solution.py
+++ b/solution.py
@@ -9,6 +9,7 @@
 
 VMEM_BYTES = 24 * 2**20
 UPDATE_BYTES = 32 * 2**20
+UPDATE_TILE, LAST_TILE = 1024, 1024
 COST = pl.CostEstimate(flops=1024, bytes_accessed=1024, transcendentals=0)
 INNER = 8
 CORE, ACROSS, UP = 1, 2, 4
@@ -140,64 +141,127 @@
     )(*operands)
 
 
-def update_kernel(near_count, far_count, start, tile, *refs):
+def rows_of(t, tile, first=0):
+    return pl.ds(pl.multiple_of(first + t * tile, tile), tile)
+
+
+def turned_product(panels, factor, rows):
+    panel = jnp.concatenate([ref[:, rows] for ref in panels], axis=0)
+    return product(split(panel), factor, contract=0)
+
+
+def update_kernel(near_count, far_count, tile, *refs):
     near, refs = refs[:near_count], refs[near_count:]
     far, refs = refs[:far_count], refs[far_count:]
-    near_factor, refs = (refs[:2], refs[2:]) if near else (None, refs)
-    far_factor, refs = (refs[:2], refs[2:]) if far else (None, refs)
-    before, after, work, arrived, left = refs
-    tiles = work.shape[0] // tile
-    full = far[0].shape[1] // tile if far else 0
-
-    def rows_of(t, first=0):
-        return pl.ds(pl.multiple_of(first + t * tile, tile), tile)
-
-    def bring(t):
-        return pltpu.make_async_copy(before.at[rows_of(t, start)], work.at[rows_of(t)], arrived.at[t])
+    near_high, near_low, far_high, far_low, before, after, rest, work, arrived, left = refs
+    full, tiles = work.shape[0] // tile, before.shape[0] // tile
+
+    def bring(t, to, first):
+        here = before.at[rows_of(t, tile), :]
+        return pltpu.make_async_copy(here, to.at[rows_of(t - first, tile), :], arrived.at[t])
 
     def take(t):
-        return pltpu.make_async_copy(work.at[rows_of(t)], after.at[rows_of(t, start)], left.at[t])
-
-    def part(panels, factor, t):
-        panel = jnp.concatenate([ref[:, rows_of(t)] for ref in panels], axis=0)
-        return product(split(panel), (factor[0][...], factor[1][...]), contract=0)
-
-    def step(t, with_far):
-        total = part(near, near_factor, t) if near else 0.0
-        if with_far:
-            total = total + part(far, far_factor, t)
-        bring(t).wait()
-        work[rows_of(t), :] = work[rows_of(t), :] - total
+        return pltpu.make_async_copy(work.at[rows_of(t, tile), :], after.at[rows_of(t, tile), :], left.at[t])
+
+    for t in range(tiles):
+        bring(t, work if t < full else rest, 0 if t < full else full).start()
+
+    @pl.loop(0, full)
+    def _(t):
+        rows = rows_of(t, tile)
+        total = turned_product(near, (near_high[...], near_low[...]), rows)
+        total = total + turned_product(far, (far_high[...], far_low[...]), rows)
+        bring(t, work, 0).wait()
+        work[rows, :] = work[rows, :] - total
         take(t).start()
 
-    for t in range(tiles):
-        bring(t).start()
-    pl.loop(0, full)(lambda t: step(t, True))
-    if full < tiles:
-        pl.loop(full, tiles)(lambda t: step(t, False))
-    for t in range(tiles):
+    @pl.loop(full, tiles)
+    def _(t):
+        total = turned_product(near, (near_high[...], near_low[...]), rows_of(t, tile))
+        bring(t, rest, full).wait()
+        rows = rows_of(t - full, tile)
+        rest[rows, :] = rest[rows, :] - total
+
+    for t in range(full):
         take(t).wait()
 
 
-def update(near, near_factor, far, far_factor, before, start, tile, in_place):
-    rows, width = (near or far)[0].shape[1], before.shape[1]
-    tile = min(tile, rows)
-    operands = [*near, *far, *(near_factor if near else ()), *(far_factor if far else ())]
-    anywhere = pl.BlockSpec(memory_space=pl.ANY)
-    return pl.pallas_call(
-        functools.partial(update_kernel, len(near), len(far), start, tile),
-        out_shape=jax.ShapeDtypeStruct(before.shape, jnp.float32),
-        in_specs=[pl.BlockSpec(memory_space=pltpu.VMEM)] * len(operands) + [anywhere],
-        out_specs=anywhere,
-        input_output_aliases={len(operands): 0} if in_place else {},
+def update(near, near_factor, far, far_factor, before):
+    rows, width, full = before.shape[0], before.shape[1], far[0].shape[1]
+    tile = min(UPDATE_TILE, full)
+    operands = [*near, *far, *near_factor, *far_factor]
+    anywhere, inside = pl.BlockSpec(memory_space=pl.ANY), pl.BlockSpec(memory_space=pltpu.VMEM)
+    return pl.pallas_call(
+        functools.partial(update_kernel, len(near), len(far), tile),
+        out_shape=[
+            jax.ShapeDtypeStruct(before.shape, jnp.float32),
+            jax.ShapeDtypeStruct((rows - full, width), jnp.float32),
+        ],
+        in_specs=[inside] * len(operands) + [anywhere],
+        out_specs=[anywhere, inside],
         scratch_shapes=[
-            pltpu.VMEM((rows, width), jnp.float32),
+            pltpu.VMEM((full, width), jnp.float32),
             pltpu.SemaphoreType.DMA((rows // tile,)),
-            pltpu.SemaphoreType.DMA((rows // tile,)),
+            pltpu.SemaphoreType.DMA((full // tile,)),
         ],
         compiler_params=pltpu.CompilerParams(vmem_limit_bytes=UPDATE_BYTES),
         cost_estimate=COST,
     )(*operands, before)
+
+
+def subtract_kernel(tile, panel, high, low, before, after):
+    @pl.loop(0, before.shape[0] // tile)
+    def _(t):
+        rows = rows_of(t, tile)
+        half = pl.ds(0, panel.shape[0])
+        after[rows, :] = before[rows, :] - turned_product([panel], (high[half, :], low[half, :]), rows)
+
+
+def subtract(panel, factor, before):
+    inside = pl.BlockSpec(memory_space=pltpu.VMEM)
+    return pl.pallas_call(
+        functools.partial(subtract_kernel, min(LAST_TILE, before.shape[0])),
+        out_shape=jax.ShapeDtypeStruct(before.shape, jnp.float32),
+        in_specs=[inside] * 4,
+        out_specs=inside,
+        input_output_aliases={3: 0},
+        compiler_params=pltpu.CompilerParams(vmem_limit_bytes=VMEM_BYTES),
+        cost_estimate=COST,
+    )(panel, *factor, before)
+
+
+def finish_kernel(tile, panel, high, low, rest, before, after, work, left):
+    rows, start = rest.shape[0], after.shape[0] - rest.shape[0]
+
+    def take(t):
+        to = after.at[rows_of(t, tile, start), :]
+        return pltpu.make_async_copy(work.at[rows_of(t, tile), :], to, left.at[t])
+
+    @pl.loop(0, rows // tile)
+    def _(t):
+        here = rows_of(t, tile)
+        half = pl.ds(panel.shape[0], panel.shape[0])
+        work[here, :] = rest[here, :] - turned_product([panel], (high[half, :], low[half, :]), here)
+        take(t).start()
+
+    for t in range(rows // tile):
+        take(t).wait()
+
+
+def finish(panel, factor, rest, before):
+    rows = rest.shape[0]
+    tile = min(LAST_TILE, rows)
+    anywhere, inside = pl.BlockSpec(memory_space=pl.ANY), pl.BlockSpec(memory_space=pltpu.VMEM)
+    return pl.pallas_call(
+        functools.partial(finish_kernel, tile),
+        out_shape=jax.ShapeDtypeStruct(before.shape, jnp.float32),
+        in_specs=[inside] * 4 + [anywhere],
+        out_specs=anywhere,
+        input_output_aliases={4: 0},
+        scratch_shapes=[pltpu.VMEM(rest.shape, jnp.float32), pltpu.SemaphoreType.DMA((rows // tile,))],
+        compiler_params=pltpu.CompilerParams(vmem_limit_bytes=VMEM_BYTES),
+        cost_estimate=COST,
+    )(panel, *factor, rest, before)
 
 
 def solution(mesh):
@@ -232,6 +296,9 @@
         def beside(pair):
             return tuple(swap(x, CORE) for x in pair)
 
+        def halves(value):
+            return jnp.split(value, 2, axis=0)
+
         def after(values, *tokens):
             return lax.optimization_barrier((values, tokens))[0]
 
@@ -243,8 +310,7 @@
         beside_0 = beside(near_0)
         for j in range(row_count - 2):
             packs.append(onward(after(packs[-1], beside_0[0]) if j == row_count - 3 else packs[-1]))
-        cut = first.shape[0] // 2
-        beside_1 = beside((near_1[0][:cut], near_1[0][cut:]))
+        beside_1 = beside(halves(near_1[0]))
         cuts = [0, rest // 2, rest]
 
         def far_part(pair, a, b):
@@ -257,7 +323,7 @@
         )
         far += [far_part(near_0, a, b) for a, b in zip(cuts[1:-1], cuts[2:])]
         others = early, swap(packs[-1][:matrix_rows], CORE)
-        beside_1 = *beside_1, swap(near_1[1], CORE)
+        beside_1 += beside(halves(after(near_1[1], others)))
         near = [
             panel
             for pair in ((first, second), own_beside, near_0, beside_0, near_1, beside_1)
@@ -265,10 +331,11 @@
         ]
         *factors, solved_first, solved_second = solve(row_count, block, own, packs, others)
         near_factor, far_factor = factors[:2], factors[2:]
-        updated = update(near, near_factor, [far[0], swap(after(far[0], others), CORE)], far_factor, rhs_rest, 0, 1024, False)
-        for start, panel in zip(cuts[1:], far[1:]):
-            panel = after(panel, updated)
-            updated = update([], None, [panel, swap(panel, CORE)], far_factor, updated, start, 512, True)
+        near_far = [far[0], *beside(halves(after(far[0], others)))]
+        updated, last = update(near, near_factor, near_far, far_factor, rhs_rest)
+        panel = after(far[1], updated)
+        other = swap(panel, CORE)
+        updated = finish(other, far_factor, subtract(panel, far_factor, last), updated)
         return solved_first, solved_second, updated
 
     in_specs = (P("row", None),) * 3 + (P("row", "col"),) * 5

time: 82.7 us -> 79.8 us (0.965)
  waiting for transfers between devices: 41.9 us -> 40.6 us
  Pallas kernels: 17.1 us -> 16.2 us
  starting transfers between devices: 22.2 us -> 21.3 us
    ppermute x6, starting transfers between devices: 10.3 us -> 8.83 us  [cross(): lax.ppermute(value, 'col', [(i, i ^ masks[i % 2]) for i in range(col_coun...]
    ppermute x11 -> x13, waiting for transfers between devices: 5.62 us -> 4.37 us  [swap(): return lax.ppermute(value, 'col', [(i, i ^ bit) for i in range(col_count)])]
    pallas_call x2 -> x3, Pallas kernels: 11.6 us -> 10.7 us  [the longest x1 7.32 us: update(): pl.pallas_call(functools.partial(update_kernel, len(near), len(far), tile...]
    ppermute x11 -> x13, starting transfers between devices: 2.68 us -> 3.2 us  [swap(): return lax.ppermute(value, 'col', [(i, i ^ bit) for i in range(col_count)])]
  transfers between devices with their start and end apart: 20 -> 22, of which waited for: 12 -> 12; matrix products, arithmetic and copies ran while one was open for 1% -> 1% of each run, Pallas kernels for 17% -> 18%
where the time goes in v4:
time: 79.8 us; the launch traced here: 79.7 us
  waiting for transfers between devices  40.6 us (51%)
  starting transfers between devices  21.3 us (27%)
  Pallas kernels  16.2 us (20%)
  between operations  0.86 us (1%)
    ppermute x3, waiting for transfers between devices, onward(): return lax.ppermute(value, 'row', list(zip(ring, ring[1:] + ring[:1])))  21.5 us
    ppermute x6, waiting for transfers between devices, cross(): lax.ppermute(value, 'col', [(i, i ^ masks[i % 2]) for i in range(col_coun...  14.7 us
    ppermute x3, starting transfers between devices, onward(): return lax.ppermute(value, 'row', list(zip(ring, ring[1:] + ring[:1])))  9.24 us
    ppermute x6, starting transfers between devices, cross(): lax.ppermute(value, 'col', [(i, i ^ masks[i % 2]) for i in range(col_coun...  8.83 us
    pallas_call x1, Pallas kernels, update(): pl.pallas_call(functools.partial(update_kernel, len(near), len(far), tile...  7.32 us
    ppermute x13, waiting for transfers between devices, swap(): return lax.ppermute(value, 'col', [(i, i ^ bit) for i in range(col_count)])  4.37 us
    pallas_call x1, Pallas kernels, solve(): pl.pallas_call(functools.partial(solve_kernel, steps, block), out_shape=o...  3.34 us
    ppermute x13, starting transfers between devices, swap(): return lax.ppermute(value, 'col', [(i, i ^ bit) for i in range(col_count)])  3.2 us
  transfers between devices with their start and end apart: 22, of which 12 were waited for; matrix products, arithmetic and copies ran while one was open for 1% of the time, Pallas kernels for 18%

profile of v4, /device:TPU:0, one launch (start us, length us, event | category | flops | bytes accessed | tf_op | source)
XLA Modules:
  0.0 79.7 jit_solution(1517683072883412776)
XLA Ops:
  0.6 3.0 %collective-permute-start = (f32[64,4096]{1,0:T(8,128)}, f32[64,4096]{1,0:T(8,128)S(1)}, u32[]{:S(2)}, u32[]{:S(2)}) collective-permute-start(f32[64,4096]{1,0:T(8,128)} %bitcast.6), channel_id=1, source_target_pairs={{0,2},{1,5},{2,0},{3,7},{4,6},{5,1},{6,4},{7,3},{8,10},{9,13},{10,... | collective-permute-start | bytes 3145736 | tf_op jit(solution)/shard_map/ppermute | solution.py:294
  3.6 0.0 collective-permute-start.2
  3.6 0.5 collective-permute-start.3
  4.1 2.1 %shard_map.103 = f32[640,256]{1,0:T(8,128)} custom-call(f32[128,512]{1,0:T(8,128)} %refs_0_.3, f32[128,512]{1,0:T(8,128)} %refs_1_.3, f32[128,512]{1,0:T(8,128)} %refs_2_.3, f32[128,256]{1,0:T(8,128)} %refs_3_.3, f32[128,256]{1,0:T(8,128)} %refs_4_.3), custom_call_target="tpu_custom_call" | custom-call | flops 1024 | bytes 1024 | tf_op jit(solution)/shard_map/pallas_call | solution.py:58
  6.2 2.6 %collective-permute-start.4 = (f32[640,256]{1,0:T(8,128)}, f32[640,256]{1,0:T(8,128)S(1)}, u32[]{:S(2)}, u32[]{:S(2)}) collective-permute-start(f32[640,256]{1,0:T(8,128)} %shard_map.103), channel_id=1, source_target_pairs={{0,16},{16,24},{24,8},{8,0},{1,17},{17,25},{25,9},{9,1},{2,18},{18... | collective-permute-start | bytes 1966088 | tf_op jit(solution)/shard_map/ppermute | solution.py:276
  8.8 0.6 collective-permute-start.1
  9.4 7.2 %collective-permute-done.refs_4_ = f32[64,4096]{1,0:T(8,128)S(1)} collective-permute-done((f32[64,4096]{1,0:T(8,128)}, f32[64,4096]{1,0:T(8,128)S(1)}, u32[]{:S(2)}, u32[]{:S(2)}) %collective-permute-start) | collective-permute-done | bytes 1048608 | tf_op jit(solution)/shard_map/ppermute | solution.py:294
  16.6 0.0 collective-permute-start.7
  16.6 6.7 %collective-permute-done.4.refs_5_ = f32[640,256]{1,0:T(8,128)S(1)} collective-permute-done((f32[640,256]{1,0:T(8,128)}, f32[640,256]{1,0:T(8,128)S(1)}, u32[]{:S(2)}, u32[]{:S(2)}) %collective-permute-start.4) | collective-permute-done | bytes 655392 | tf_op jit(solution)/shard_map/ppermute | solution.py:276
  23.3 0.0 collective-permute-done.2.refs_2_
  23.3 0.0 collective-permute-done.3.refs_3_
  23.3 1.5 %collective-permute-start.5 = (f32[64,4096]{1,0:T(8,128)}, f32[64,4096]{1,0:T(8,128)S(1)}, u32[]{:S(2)}, u32[]{:S(2)}) collective-permute-start(f32[64,4096]{1,0:T(8,128)} %bitcast.8), channel_id=1, source_target_pairs={{0,4},{1,3},{2,6},{3,1},{4,0},{5,7},{6,2},{7,5},{8,12},{9,11},{10,... | collective-permute-start | bytes 3145736 | tf_op jit(solution)/shard_map/ppermute | solution.py:294
  24.8 3.3 %collective-permute-start.11 = (f32[640,256]{1,0:T(8,128)S(1)}, f32[640,256]{1,0:T(8,128)S(1)}, u32[]{:S(2)}, u32[]{:S(2)}) collective-permute-start(f32[640,256]{1,0:T(8,128)S(1)} %collective-permute-done.4.refs_5_), channel_id=1, source_target_pairs={{0,16},{16,24},{24,8},{8,0},{1,17},{17,25},{25,9},{9,1},{2,18},{18... | collective-permute-start | bytes 1966088 | tf_op jit(solution)/shard_map/ppermute | solution.py:276
  28.1 0.6 collective-permute-start.6
  28.8 1.6 %collective-permute-done.1.refs_5_ = f32[64,4096]{1,0:T(8,128)S(1)} collective-permute-done((f32[64,4096]{1,0:T(8,128)}, f32[64,4096]{1,0:T(8,128)S(1)}, u32[]{:S(2)}, u32[]{:S(2)}) %collective-permute-start.1) | collective-permute-done | bytes 1048608 | tf_op jit(solution)/shard_map/ppermute | solution.py:294
  30.4 0.1 pad_maximum_fusion.1
  30.5 2.7 %collective-permute-start.18 = (f32[128,2048]{1,0:T(8,128)S(1)}, f32[128,2048]{1,0:T(8,128)S(1)}, u32[]{:S(2)}, u32[]{:S(2)}) collective-permute-start(f32[128,2048]{1,0:T(8,128)S(1)} %pad_maximum_fusion.1), channel_id=1, source_target_pairs={{0,4},{1,3},{2,6},{3,1},{4,0},{5,7},{6,2},{7,5},{8,12},{9,11},{10,... | collective-permute-start | bytes 3145736 | tf_op jit(solution)/shard_map/ppermute | solution.py:294
  33.2 8.0 %collective-permute-done.11.refs_6_ = f32[640,256]{1,0:T(8,128)S(1)} collective-permute-done((f32[640,256]{1,0:T(8,128)S(1)}, f32[640,256]{1,0:T(8,128)S(1)}, u32[]{:S(2)}, u32[]{:S(2)}) %collective-permute-start.11) | collective-permute-done | bytes 655392 | tf_op jit(solution)/shard_map/ppermute | solution.py:276
  41.3 0.0 collective-permute-start.8
  41.3 0.1 pad_maximum_fusion.2
  41.4 0.0 collective-permute-done.7.refs_6_
  41.4 0.6 collective-permute-start.13
  41.9 0.0 collective-permute-done.5.refs_8_
  41.9 3.4 %collective-permute-start.12 = (f32[640,256]{1,0:T(8,128)S(1)}, f32[640,256]{1,0:T(8,128)S(1)}, u32[]{:S(2)}, u32[]{:S(2)}) collective-permute-start(f32[640,256]{1,0:T(8,128)S(1)} %collective-permute-done.11.refs_6_), channel_id=1, source_target_pairs={{0,16},{16,24},{24,8},{8,0},{1,17},{17,25},{25,9},{9,1},{2,18},{18... | collective-permute-start | bytes 1966088 | tf_op jit(solution)/shard_map/ppermute | solution.py:276
  45.3 0.1 fusion.2
  45.4 4.2 %collective-permute-done.6.refs_9_ = f32[64,4096]{1,0:T(8,128)S(1)} collective-permute-done((f32[64,4096]{1,0:T(8,128)}, f32[64,4096]{1,0:T(8,128)S(1)}, u32[]{:S(2)}, u32[]{:S(2)}) %collective-permute-start.6) | collective-permute-done | bytes 1048608 | tf_op jit(solution)/shard_map/ppermute | solution.py:294
  49.6 0.9 %collective-permute-start.10 = (f32[32,4096]{1,0:T(8,128)S(1)}, f32[32,4096]{1,0:T(8,128)S(1)}, u32[]{:S(2)}, u32[]{:S(2)}) collective-permute-start(f32[32,4096]{1,0:T(8,128)S(1)} %get-tuple-element.59), channel_id=1, source_target_pairs={{0,1},{1,0},{2,3},{3,2},{4,5},{5,4},{6,7},{7,6},{8,9},{9,8},{10,11... | collective-permute-start | bytes 1572872 | tf_op jit(solution)/shard_map/ppermute | solution.py:271
  50.4 0.0 collective-permute-done.13.refs_8_
  50.4 0.0 collective-permute-start.9
  50.5 0.0 collective-permute-done.8.refs_7_
  50.5 1.5 %collective-permute-done.10.refs_11_ = f32[32,4096]{1,0:T(8,128)S(1)} collective-permute-done((f32[32,4096]{1,0:T(8,128)S(1)}, f32[32,4096]{1,0:T(8,128)S(1)}, u32[]{:S(2)}, u32[]{:S(2)}) %collective-permute-start.10) | collective-permute-done | bytes 524320 | tf_op jit(solution)/shard_map/ppermute | solution.py:271
  52.0 0.7 collective-permute-done.9.refs_10_
  52.7 6.8 %collective-permute-done.12.refs_7_ = f32[640,256]{1,0:T(8,128)S(1)} collective-permute-done((f32[640,256]{1,0:T(8,128)S(1)}, f32[640,256]{1,0:T(8,128)S(1)}, u32[]{:S(2)}, u32[]{:S(2)}) %collective-permute-start.12) | collective-permute-done | bytes 655392 | tf_op jit(solution)/shard_map/ppermute | solution.py:276
  59.6 0.0 copy-start.3
  59.6 0.0 copy-start.4
  59.6 0.0 copy-start.5
  59.6 0.0 copy-start.6
  59.6 0.0 copy-start.7
  59.6 0.1 collective-permute-start.14
  59.8 0.1 pad_maximum_fusion
  59.9 0.0 copy-start
  59.9 0.0 copy-start.1
  59.9 0.0 copy-start.2
  59.9 0.5 collective-permute-start.15
  60.4 0.4 collective-permute-done.18.refs_14_
  60.8 0.6 collective-permute-done.14.refs_9_
  61.4 0.1 fusion
  61.5 0.2 collective-permute-start.19
  61.7 0.4 collective-permute-start.20
  62.1 0.1 fusion.1
  62.2 0.2 collective-permute-start.16
  62.4 0.4 collective-permute-start.17
  62.8 0.0 copy-done.4
  62.8 3.3 %shard_map.104 = (bf16[768,256]{1,0:T(8,128)(2,1)S(1)}, bf16[768,256]{1,0:T(8,128)(2,1)S(1)}, bf16[256,256]{1,0:T(8,128)(2,1)S(1)}, bf16[256,256]{1,0:T(8,128)(2...) custom-call(f32[128,512]{1,0:T(8,128)S(1)} %copy-done.3, f32[128,512]{1,0:T(8,128)S(1)} %copy-done.4, ...), custom_call_target="tpu_custom_call" | custom-call | flops 1024 | bytes 1024 | tf_op jit(solution)/shard_map/pallas_call | solution.py:128
  66.1 0.0 collective-permute-done.19.refs_15_
  66.1 0.0 collective-permute-done.20.refs_16_
  66.1 0.0 collective-permute-done.16.refs_12_
  66.1 0.0 collective-permute-done.17.refs_13_
  66.2 7.3 %shard_map.105 = (f32[4096,256]{1,0:T(8,128)}, f32[2048,256]{1,0:T(8,128)S(1)}) custom-call(f32[64,4096]{1,0:T(8,128)S(1)} %bitcast.9, f32[64,4096]{1,0:T(8,128)S(1)} %bitcast.5, f32[64,4096]{1,0:T(8,128)S(1)} %collective-permute-done.2.refs_2_, f32[64,4096]{1,0:T(8,128)S(1)} %collective-permute-done.3.refs_3_, f32[64,4096]{1,0:T(8,128)S(1)} %collective-permute-done.refs_4_, ...), custom_call_target="tpu_custom_call" | custom-call | flops 1024 | bytes 1024 | tf_op jit(solution)/shard_map/pallas_call | solution.py:194
  73.5 1.3 %collective-permute-done.15.panel = f32[128,2048]{1,0:T(8,128)S(1)} collective-permute-done((f32[128,2048]{1,0:T(8,128)S(1)}, f32[128,2048]{1,0:T(8,128)S(1)}, u32[]{:S(2)}, u32[]{:S(2)}) %collective-permute-start.15) | collective-permute-done | bytes 1048608 | tf_op jit(solution)/shard_map/ppermute | solution.py:294
  74.8 0.0 collective-permute-start.21
  74.8 1.2 %shard_map.106.rest = f32[2048,256]{1,0:T(8,128)S(1)} custom-call(f32[128,2048]{1,0:T(8,128)S(1)} %collective-permute-done.15.panel, bf16[256,256]{1,0:T(8,128)(2,1)S(1)} %get-tuple-element.50.refs_19_.high, bf16[256,256]{1,0:T(8,128)(2,1)S(1)} %get-tuple-element.51.refs_20_.low, ...), custom_call_target="tpu_custom_call", output_to_operand_aliasing={{}: (3, {})} | custom-call | flops 1024 | bytes 1024 | tf_op jit(solution)/shard_map/pallas_call | solution.py:222
  76.0 1.4 %collective-permute-done.21.panel = f32[128,2048]{1,0:T(8,128)S(1)} collective-permute-done((f32[128,2048]{1,0:T(8,128)S(1)}, f32[128,2048]{1,0:T(8,128)S(1)}, u32[]{:S(2)}, u32[]{:S(2)}) %collective-permute-start.21) | collective-permute-done | bytes 1048608 | tf_op jit(solution)/shard_map/ppermute | solution.py:271
  77.5 2.2 %shard_map.107 = f32[4096,256]{1,0:T(8,128)} custom-call(f32[128,2048]{1,0:T(8,128)S(1)} %collective-permute-done.21.panel, bf16[256,256]{1,0:T(8,128)(2,1)S(1)} %get-tuple-element.50.refs_19_.high, bf16[256,256]{1,0:T(8,128)(2,1)S(1)} %get-tuple-element.51.refs_20_.low, f32[2048,256]{1,0:T(8,128)S(1)} %shard_map.106.rest, ...), custom_call_target="tpu_custom_call", output_to_operand_aliasing={{}: (4, {})} | custom-call | flops 1024 | bytes 1024 | tf_op jit(solution)/shard_map/pallas_call | solution.py:255
  (14 shorter events, 0.2 us)
Async XLA Ops:
  0.6 16.0 %collective-permute-start = (f32[64,4096]{1,0:T(8,128)}, f32[64,4096]{1,0:T(8,128)S(1)}, u32[]{:S(2)}, u32[]{:S(2)}) collective-permute-start(f32[64,4096]{1,0:T(8,128)} %bitcast.6), channel_id=1, source_target_pairs={{0,2},{1,5},{2,0},{3,7},{4,6},{5,1},{6,4},{7,3},{8,10},{9,13},{10,... | collective-permute-start | bytes 3145736 | tf_op jit(solution)/shard_map/ppermute | solution.py:294
  3.6 19.7 %collective-permute-start.2 = (f32[64,4096]{1,0:T(8,128)}, f32[64,4096]{1,0:T(8,128)S(1)}, u32[]{:S(2)}, u32[]{:S(2)}) collective-permute-start(f32[64,4096]{1,0:T(8,128)} %bitcast.7), channel_id=1, source_target_pairs={{0,1},{1,0},{2,3},{3,2},{4,5},{5,4},{6,7},{7,6},{8,9},{9,8},{10,11... | collective-permute-start | bytes 3145736 | tf_op jit(solution)/shard_map/ppermute | solution.py:271
  3.6 19.7 %collective-permute-start.3 = (f32[64,4096]{1,0:T(8,128)}, f32[64,4096]{1,0:T(8,128)S(1)}, u32[]{:S(2)}, u32[]{:S(2)}) collective-permute-start(f32[64,4096]{1,0:T(8,128)} %bitcast.2), channel_id=1, source_target_pairs={{0,1},{1,0},{2,3},{3,2},{4,5},{5,4},{6,7},{7,6},{8,9},{9,8},{10,11... | collective-permute-start | bytes 3145736 | tf_op jit(solution)/shard_map/ppermute | solution.py:271
  6.2 17.1 %collective-permute-start.4 = (f32[640,256]{1,0:T(8,128)}, f32[640,256]{1,0:T(8,128)S(1)}, u32[]{:S(2)}, u32[]{:S(2)}) collective-permute-start(f32[640,256]{1,0:T(8,128)} %shard_map.103), channel_id=1, source_target_pairs={{0,16},{16,24},{24,8},{8,0},{1,17},{17,25},{25,9},{9,1},{2,18},{18... | collective-permute-start | bytes 1966088 | tf_op jit(solution)/shard_map/ppermute | solution.py:276
  8.8 21.6 %collective-permute-start.1 = (f32[64,4096]{1,0:T(8,128)}, f32[64,4096]{1,0:T(8,128)S(1)}, u32[]{:S(2)}, u32[]{:S(2)}) collective-permute-start(f32[64,4096]{1,0:T(8,128)} %bitcast.3), channel_id=1, source_target_pairs={{0,2},{1,5},{2,0},{3,7},{4,6},{5,1},{6,4},{7,3},{8,10},{9,13},{10,... | collective-permute-start | bytes 3145736 | tf_op jit(solution)/shard_map/ppermute | solution.py:294
  16.6 24.7 %collective-permute-start.7 = (f32[64,4096]{1,0:T(8,128)S(1)}, f32[64,4096]{1,0:T(8,128)S(1)}, u32[]{:S(2)}, u32[]{:S(2)}) collective-permute-start(f32[64,4096]{1,0:T(8,128)S(1)} %collective-permute-done.refs_4_), channel_id=1, source_target_pairs={{0,1},{1,0},{2,3},{3,2},{4,5},{5,4},{6,7},{7,6},{8,9},{9,8},{10,11... | collective-permute-start | bytes 3145736 | tf_op jit(solution)/shard_map/ppermute | solution.py:271
  23.3 18.6 %collective-permute-start.5 = (f32[64,4096]{1,0:T(8,128)}, f32[64,4096]{1,0:T(8,128)S(1)}, u32[]{:S(2)}, u32[]{:S(2)}) collective-permute-start(f32[64,4096]{1,0:T(8,128)} %bitcast.8), channel_id=1, source_target_pairs={{0,4},{1,3},{2,6},{3,1},{4,0},{5,7},{6,2},{7,5},{8,12},{9,11},{10,... | collective-permute-start | bytes 3145736 | tf_op jit(solution)/shard_map/ppermute | solution.py:294
  24.8 16.4 %collective-permute-start.11 = (f32[640,256]{1,0:T(8,128)S(1)}, f32[640,256]{1,0:T(8,128)S(1)}, u32[]{:S(2)}, u32[]{:S(2)}) collective-permute-start(f32[640,256]{1,0:T(8,128)S(1)} %collective-permute-done.4.refs_5_), channel_id=1, source_target_pairs={{0,16},{16,24},{24,8},{8,0},{1,17},{17,25},{25,9},{9,1},{2,18},{18... | collective-permute-start | bytes 1966088 | tf_op jit(solution)/shard_map/ppermute | solution.py:276
  28.1 21.4 %collective-permute-start.6 = (f32[64,4096]{1,0:T(8,128)}, f32[64,4096]{1,0:T(8,128)S(1)}, u32[]{:S(2)}, u32[]{:S(2)}) collective-permute-start(f32[64,4096]{1,0:T(8,128)} %bitcast.4), channel_id=1, source_target_pairs={{0,4},{1,3},{2,6},{3,1},{4,0},{5,7},{6,2},{7,5},{8,12},{9,11},{10,... | collective-permute-start | bytes 3145736 | tf_op jit(solution)/shard_map/ppermute | solution.py:294
  30.5 30.3 %collective-permute-start.18 = (f32[128,2048]{1,0:T(8,128)S(1)}, f32[128,2048]{1,0:T(8,128)S(1)}, u32[]{:S(2)}, u32[]{:S(2)}) collective-permute-start(f32[128,2048]{1,0:T(8,128)S(1)} %pad_maximum_fusion.1), channel_id=1, source_target_pairs={{0,4},{1,3},{2,6},{3,1},{4,0},{5,7},{6,2},{7,5},{8,12},{9,11},{10,... | collective-permute-start | bytes 3145736 | tf_op jit(solution)/shard_map/ppermute | solution.py:294
  41.3 9.2 %collective-permute-start.8 = (f32[64,4096]{1,0:T(8,128)S(1)}, f32[64,4096]{1,0:T(8,128)S(1)}, u32[]{:S(2)}, u32[]{:S(2)}) collective-permute-start(f32[64,4096]{1,0:T(8,128)S(1)} %collective-permute-done.1.refs_5_), channel_id=1, source_target_pairs={{0,1},{1,0},{2,3},{3,2},{4,5},{5,4},{6,7},{7,6},{8,9},{9,8},{10,11... | collective-permute-start | bytes 3145736 | tf_op jit(solution)/shard_map/ppermute | solution.py:271
  41.4 9.1 %collective-permute-start.13 = (f32[768,256]{1,0:T(8,128)S(1)}, f32[768,256]{1,0:T(8,128)S(1)}, u32[]{:S(2)}, u32[]{:S(2)}) collective-permute-start(f32[768,256]{1,0:T(8,128)S(1)} %pad_maximum_fusion.2), channel_id=1, source_target_pairs={{0,1},{1,0},{2,3},{3,2},{4,5},{5,4},{6,7},{7,6},{8,9},{9,8},{10,11... | collective-permute-start | bytes 2359304 | tf_op jit(solution)/shard_map/ppermute | solution.py:271
  41.9 17.6 %collective-permute-start.12 = (f32[640,256]{1,0:T(8,128)S(1)}, f32[640,256]{1,0:T(8,128)S(1)}, u32[]{:S(2)}, u32[]{:S(2)}) collective-permute-start(f32[640,256]{1,0:T(8,128)S(1)} %collective-permute-done.11.refs_6_), channel_id=1, source_target_pairs={{0,16},{16,24},{24,8},{8,0},{1,17},{17,25},{25,9},{9,1},{2,18},{18... | collective-permute-start | bytes 1966088 | tf_op jit(solution)/shard_map/ppermute | solution.py:276
  49.6 2.4 %collective-permute-start.10 = (f32[32,4096]{1,0:T(8,128)S(1)}, f32[32,4096]{1,0:T(8,128)S(1)}, u32[]{:S(2)}, u32[]{:S(2)}) collective-permute-start(f32[32,4096]{1,0:T(8,128)S(1)} %get-tuple-element.59), channel_id=1, source_target_pairs={{0,1},{1,0},{2,3},{3,2},{4,5},{5,4},{6,7},{7,6},{8,9},{9,8},{10,11... | collective-permute-start | bytes 1572872 | tf_op jit(solution)/shard_map/ppermute | solution.py:271
  50.4 2.3 %collective-permute-start.9 = (f32[32,4096]{1,0:T(8,128)S(1)}, f32[32,4096]{1,0:T(8,128)S(1)}, u32[]{:S(2)}, u32[]{:S(2)}) collective-permute-start(f32[32,4096]{1,0:T(8,128)S(1)} %get-tuple-element.60), channel_id=1, source_target_pairs={{0,1},{1,0},{2,3},{3,2},{4,5},{5,4},{6,7},{7,6},{8,9},{9,8},{10,11... | collective-permute-start | bytes 1572872 | tf_op jit(solution)/shard_map/ppermute | solution.py:271
  59.6 3.2 %copy-start.3 = (f32[128,512]{1,0:T(8,128)S(1)}, f32[128,512]{1,0:T(8,128)}, u32[]{:S(2)}) copy-start(f32[128,512]{1,0:T(8,128)} %refs_0_.3) | copy-start | bytes 786436
  59.6 3.2 %copy-start.4 = (f32[128,512]{1,0:T(8,128)S(1)}, f32[128,512]{1,0:T(8,128)}, u32[]{:S(2)}) copy-start(f32[128,512]{1,0:T(8,128)} %refs_1_.3) | copy-start | bytes 786436
  59.6 3.2 %copy-start.5 = (f32[128,512]{1,0:T(8,128)S(1)}, f32[128,512]{1,0:T(8,128)}, u32[]{:S(2)}) copy-start(f32[128,512]{1,0:T(8,128)} %refs_2_.3) | copy-start | bytes 786436
  59.6 3.1 %copy-start.6 = (f32[128,256]{1,0:T(8,128)S(1)}, f32[128,256]{1,0:T(8,128)}, u32[]{:S(2)}) copy-start(f32[128,256]{1,0:T(8,128)} %refs_3_.3) | copy-start | bytes 393220
  59.6 3.1 %copy-start.7 = (f32[128,256]{1,0:T(8,128)S(1)}, f32[128,256]{1,0:T(8,128)}, u32[]{:S(2)}) copy-start(f32[128,256]{1,0:T(8,128)} %refs_4_.3) | copy-start | bytes 393220
  59.6 1.8 %collective-permute-start.14 = (f32[384,256]{1,0:T(8,128)S(1)}, f32[384,256]{1,0:T(8,128)S(1)}, u32[]{:S(2)}, u32[]{:S(2)}) collective-permute-start(f32[384,256]{1,0:T(8,128)S(1)} %slice.23), channel_id=1, source_target_pairs={{0,1},{1,0},{2,3},{3,2},{4,5},{5,4},{6,7},{7,6},{8,9},{9,8},{10,11... | collective-permute-start | bytes 1179656 | tf_op jit(solution)/shard_map/ppermute | solution.py:271
  59.9 6.2 %copy-start = (f32[4096,256]{1,0:T(8,128)S(1)}, f32[4096,256]{1,0:T(8,128)}, u32[]{:S(2)}) copy-start(f32[4096,256]{1,0:T(8,128)} %refs_21_.1) | copy-start | bytes 12582916
  59.9 6.2 %copy-start.1 = (f32[4096,64]{0,1:T(8,128)S(1)}, f32[4096,64]{0,1:T(8,128)}, u32[]{:S(2)}) copy-start(f32[4096,64]{0,1:T(8,128)} %param.12) | copy-start | bytes 3145732
  59.9 6.2 %copy-start.2 = (f32[4096,64]{0,1:T(8,128)S(1)}, f32[4096,64]{0,1:T(8,128)}, u32[]{:S(2)}) copy-start(f32[4096,64]{0,1:T(8,128)} %param.11) | copy-start | bytes 3145732
  59.9 14.9 %collective-permute-start.15 = (f32[128,2048]{1,0:T(8,128)S(1)}, f32[128,2048]{1,0:T(8,128)S(1)}, u32[]{:S(2)}, u32[]{:S(2)}) collective-permute-start(f32[128,2048]{1,0:T(8,128)S(1)} %pad_maximum_fusion), channel_id=1, source_target_pairs={{0,4},{1,3},{2,6},{3,1},{4,0},{5,7},{6,2},{7,5},{8,12},{9,11},{10,... | collective-permute-start | bytes 3145736 | tf_op jit(solution)/shard_map/ppermute | solution.py:294
  61.5 4.6 %collective-permute-start.19 = (f32[64,2048]{1,0:T(8,128)S(1)}, f32[64,2048]{1,0:T(8,128)S(1)}, u32[]{:S(2)}, u32[]{:S(2)}) collective-permute-start(f32[64,2048]{1,0:T(8,128)S(1)} %get-tuple-element.56), channel_id=1, source_target_pairs={{0,1},{1,0},{2,3},{3,2},{4,5},{5,4},{6,7},{7,6},{8,9},{9,8},{10,11... | collective-permute-start | bytes 1572872 | tf_op jit(solution)/shard_map/ppermute | solution.py:271
  61.7 4.4 %collective-permute-start.20 = (f32[64,2048]{1,0:T(8,128)S(1)}, f32[64,2048]{1,0:T(8,128)S(1)}, u32[]{:S(2)}, u32[]{:S(2)}) collective-permute-start(f32[64,2048]{1,0:T(8,128)S(1)} %get-tuple-element.55), channel_id=1, source_target_pairs={{0,1},{1,0},{2,3},{3,2},{4,5},{5,4},{6,7},{7,6},{8,9},{9,8},{10,11... | collective-permute-start | bytes 1572872 | tf_op jit(solution)/shard_map/ppermute | solution.py:271
  62.2 4.0 %collective-permute-start.16 = (f32[32,4096]{1,0:T(8,128)S(1)}, f32[32,4096]{1,0:T(8,128)S(1)}, u32[]{:S(2)}, u32[]{:S(2)}) collective-permute-start(f32[32,4096]{1,0:T(8,128)S(1)} %get-tuple-element.58), channel_id=1, source_target_pairs={{0,1},{1,0},{2,3},{3,2},{4,5},{5,4},{6,7},{7,6},{8,9},{9,8},{10,11... | collective-permute-start | bytes 1572872 | tf_op jit(solution)/shard_map/ppermute | solution.py:271
  62.4 3.8 %collective-permute-start.17 = (f32[32,4096]{1,0:T(8,128)S(1)}, f32[32,4096]{1,0:T(8,128)S(1)}, u32[]{:S(2)}, u32[]{:S(2)}) collective-permute-start(f32[32,4096]{1,0:T(8,128)S(1)} %get-tuple-element.57), channel_id=1, source_target_pairs={{0,1},{1,0},{2,3},{3,2},{4,5},{5,4},{6,7},{7,6},{8,9},{9,8},{10,11... | collective-permute-start | bytes 1572872 | tf_op jit(solution)/shard_map/ppermute | solution.py:271
  74.8 2.7 %collective-permute-start.21 = (f32[128,2048]{1,0:T(8,128)S(1)}, f32[128,2048]{1,0:T(8,128)S(1)}, u32[]{:S(2)}, u32[]{:S(2)}) collective-permute-start(f32[128,2048]{1,0:T(8,128)S(1)} %collective-permute-done.15.panel), channel_id=1, source_target_pairs={{0,1},{1,0},{2,3},{3,2},{4,5},{5,4},{6,7},{7,6},{8,9},{9,8},{10,11... | collective-permute-start | bytes 3145736 | tf_op jit(solution)/shard_map/ppermute | solution.py:271

commit v5 on v4

--- a/solution.py
+++ b/solution.py
@@ -9,7 +9,7 @@
 
 VMEM_BYTES = 24 * 2**20
 UPDATE_BYTES = 32 * 2**20
-UPDATE_TILE, LAST_TILE = 1024, 1024
+UPDATE_TILE, LAST_TILE = 1024, 512
 COST = pl.CostEstimate(flops=1024, bytes_accessed=1024, transcendentals=0)
 INNER = 8
 CORE, ACROSS, UP = 1, 2, 4
@@ -68,7 +68,7 @@
     own, refs = refs[:5], refs[5:]
     pieces, (early, late, *refs) = refs[: steps - 1], refs[steps - 1 :]
     outs, (first_out, second_out, *scratch) = refs[: 2 * len(GROUPS)], refs[2 * len(GROUPS) :]
-    matrices, right_first, right_second, solved = scratch
+    matrices, right_first, right_second, solved, current = scratch
     here = lax.axis_index("row")
     lane = lax.axis_index("col")
     even = lax.rem(lane, 2) == 0
@@ -94,11 +94,16 @@
             other = others[at_row * rows : (at_row + 1) * rows, :]
             matrices[k, at(j + 1), :width] = jnp.where(even, mine, other)
             matrices[k, at(j + 1), width:] = jnp.where(even, other, mine)
-    solved[0] = product(split(matrices[0]), split(right_first[...]))
-    reduced = right_second[...] - product(split(matrices[2]), split(solved[0]))
-    solved[1] = product(split(matrices[1]), split(reduced))
+    current[...] = right_first[...]
+
+    @pl.loop(0, 3)
+    def _(k):
+        result = product(split(matrices[k]), split(current[...]))
+        solved[k] = result
+        current[...] = jnp.where(k == 1, right_second[...] - result, result)
+
     first_out[...] = solved[0, at(0), :]
-    second_out[...] = solved[1, at(0), :]
+    second_out[...] = solved[2, at(0), :]
 
     inner = lax.rem(lane, INNER)
     outer = solved.shape[1] // (INNER * block)
@@ -108,7 +113,7 @@
             which = lax.bitwise_xor(inner, jnp.where(even, mask, odd_mask))
             for o in range(outer):
                 start = pl.multiple_of((o * INNER + which) * block, block)
-                high, low = split(solved[part, pl.ds(start, block), :])
+                high, low = split(solved[2 * part, pl.ds(start, block), :])
                 high_out[to : to + block, :] = high
                 low_out[to : to + block, :] = low
                 to += block
@@ -134,7 +139,8 @@
             pltpu.VMEM((3, depth, depth), jnp.float32),
             pltpu.VMEM((depth, width), jnp.float32),
             pltpu.VMEM((depth, width), jnp.float32),
-            pltpu.VMEM((2, depth, width), jnp.float32),
+            pltpu.VMEM((3, depth, width), jnp.float32),
+            pltpu.VMEM((depth, width), jnp.float32),
         ],
         compiler_params=pltpu.CompilerParams(vmem_limit_bytes=VMEM_BYTES),
         cost_estimate=COST,
@@ -142,6 +148,8 @@
 
 
 def rows_of(t, tile, first=0):
+    if isinstance(t, int):
+        return pl.ds(first + t * tile, tile)
     return pl.ds(pl.multiple_of(first + t * tile, tile), tile)
 
 
@@ -237,13 +245,11 @@
         to = after.at[rows_of(t, tile, start), :]
         return pltpu.make_async_copy(work.at[rows_of(t, tile), :], to, left.at[t])
 
-    @pl.loop(0, rows // tile)
-    def _(t):
+    for t in range(rows // tile):
         here = rows_of(t, tile)
         half = pl.ds(panel.shape[0], panel.shape[0])
         work[here, :] = rest[here, :] - turned_product([panel], (high[half, :], low[half, :]), here)
         take(t).start()
-
     for t in range(rows // tile):
         take(t).wait()
 
@@ -289,7 +295,7 @@
             )
         rest = first.shape[1]
 
-        own = (inverse_first, inverse_second, coupling, rhs_first, rhs_second)
+        own = (inverse_first, coupling, inverse_second, rhs_first, rhs_second)
         def cross(value, masks):
             return lax.ppermute(value, "col", [(i, i ^ masks[i % 2]) for i in range(col_count)])
 

time: 79.8 us -> 79.7 us (level)
  transfers between devices with their start and end apart: 22 -> 22, of which waited for: 12 -> 13; matrix products, arithmetic and copies ran while one was open for 1% -> 1% of each run, Pallas kernels for 18% -> 17%
where the time goes in v5:
time: 79.7 us; the launch traced here: 79.6 us
  waiting for transfers between devices  40.8 us (51%)
  starting transfers between devices  21.3 us (27%)
  Pallas kernels  15.9 us (20%)
  between operations  0.84 us (1%)
    ppermute x3, waiting for transfers between devices, onward(): return lax.ppermute(value, 'row', list(zip(ring, ring[1:] + ring[:1])))  21.5 us
    ppermute x6, waiting for transfers between devices, cross(): lax.ppermute(value, 'col', [(i, i ^ masks[i % 2]) for i in range(col_coun...  15.1 us
    ppermute x3, starting transfers between devices, onward(): return lax.ppermute(value, 'row', list(zip(ring, ring[1:] + ring[:1])))  9.24 us
    ppermute x6, starting transfers between devices, cross(): lax.ppermute(value, 'col', [(i, i ^ masks[i % 2]) for i in range(col_coun...  8.83 us
    pallas_call x1, Pallas kernels, update(): pl.pallas_call(functools.partial(update_kernel, len(near), len(far), tile...  7.32 us
    ppermute x13, waiting for transfers between devices, swap(): return lax.ppermute(value, 'col', [(i, i ^ bit) for i in range(col_count)])  4.1 us
    ppermute x13, starting transfers between devices, swap(): return lax.ppermute(value, 'col', [(i, i ^ bit) for i in range(col_count)])  3.2 us
    pallas_call x1, Pallas kernels, solve(): pl.pallas_call(functools.partial(solve_kernel, steps, block), out_shape=o...  2.86 us
  transfers between devices with their start and end apart: 22, of which 13 were waited for; matrix products, arithmetic and copies ran while one was open for 1% of the time, Pallas kernels for 17%

profile of v5, /device:TPU:0, one launch (start us, length us, event | category | flops | bytes accessed | tf_op | source)
XLA Modules:
  0.0 79.6 jit_solution(10790495563269202057)
XLA Ops:
  0.6 3.0 %collective-permute-start = (f32[64,4096]{1,0:T(8,128)}, f32[64,4096]{1,0:T(8,128)S(1)}, u32[]{:S(2)}, u32[]{:S(2)}) collective-permute-start(f32[64,4096]{1,0:T(8,128)} %bitcast.6), channel_id=1, source_target_pairs={{0,2},{1,5},{2,0},{3,7},{4,6},{5,1},{6,4},{7,3},{8,10},{9,13},{10,... | collective-permute-start | bytes 3145736 | tf_op jit(solution)/shard_map/ppermute | solution.py:300
  3.6 0.0 collective-permute-start.2
  3.6 0.5 collective-permute-start.3
  4.1 2.1 %shard_map.103 = f32[640,256]{1,0:T(8,128)} custom-call(f32[128,512]{1,0:T(8,128)} %refs_0_.3, f32[128,512]{1,0:T(8,128)} %refs_1_.3, f32[128,512]{1,0:T(8,128)} %refs_2_.3, f32[128,256]{1,0:T(8,128)} %refs_3_.3, f32[128,256]{1,0:T(8,128)} %refs_4_.3), custom_call_target="tpu_custom_call" | custom-call | flops 1024 | bytes 1024 | tf_op jit(solution)/shard_map/pallas_call | solution.py:58
  6.2 2.6 %collective-permute-start.4 = (f32[640,256]{1,0:T(8,128)}, f32[640,256]{1,0:T(8,128)S(1)}, u32[]{:S(2)}, u32[]{:S(2)}) collective-permute-start(f32[640,256]{1,0:T(8,128)} %shard_map.103), channel_id=1, source_target_pairs={{0,16},{16,24},{24,8},{8,0},{1,17},{17,25},{25,9},{9,1},{2,18},{18... | collective-permute-start | bytes 1966088 | tf_op jit(solution)/shard_map/ppermute | solution.py:282
  8.8 0.6 collective-permute-start.1
  9.4 7.2 %collective-permute-done.refs_4_ = f32[64,4096]{1,0:T(8,128)S(1)} collective-permute-done((f32[64,4096]{1,0:T(8,128)}, f32[64,4096]{1,0:T(8,128)S(1)}, u32[]{:S(2)}, u32[]{:S(2)}) %collective-permute-start) | collective-permute-done | bytes 1048608 | tf_op jit(solution)/shard_map/ppermute | solution.py:300
  16.6 0.0 collective-permute-start.7
  16.6 6.7 %collective-permute-done.4.refs_5_ = f32[640,256]{1,0:T(8,128)S(1)} collective-permute-done((f32[640,256]{1,0:T(8,128)}, f32[640,256]{1,0:T(8,128)S(1)}, u32[]{:S(2)}, u32[]{:S(2)}) %collective-permute-start.4) | collective-permute-done | bytes 655392 | tf_op jit(solution)/shard_map/ppermute | solution.py:282
  23.3 0.0 collective-permute-done.2.refs_2_
  23.3 0.0 collective-permute-done.3.refs_3_
  23.3 1.5 %collective-permute-start.5 = (f32[64,4096]{1,0:T(8,128)}, f32[64,4096]{1,0:T(8,128)S(1)}, u32[]{:S(2)}, u32[]{:S(2)}) collective-permute-start(f32[64,4096]{1,0:T(8,128)} %bitcast.8), channel_id=1, source_target_pairs={{0,4},{1,3},{2,6},{3,1},{4,0},{5,7},{6,2},{7,5},{8,12},{9,11},{10,... | collective-permute-start | bytes 3145736 | tf_op jit(solution)/shard_map/ppermute | solution.py:300
  24.8 3.3 %collective-permute-start.11 = (f32[640,256]{1,0:T(8,128)S(1)}, f32[640,256]{1,0:T(8,128)S(1)}, u32[]{:S(2)}, u32[]{:S(2)}) collective-permute-start(f32[640,256]{1,0:T(8,128)S(1)} %collective-permute-done.4.refs_5_), channel_id=1, source_target_pairs={{0,16},{16,24},{24,8},{8,0},{1,17},{17,25},{25,9},{9,1},{2,18},{18... | collective-permute-start | bytes 1966088 | tf_op jit(solution)/shard_map/ppermute | solution.py:282
  28.1 0.6 collective-permute-start.6
  28.8 1.6 %collective-permute-done.1.refs_5_ = f32[64,4096]{1,0:T(8,128)S(1)} collective-permute-done((f32[64,4096]{1,0:T(8,128)}, f32[64,4096]{1,0:T(8,128)S(1)}, u32[]{:S(2)}, u32[]{:S(2)}) %collective-permute-start.1) | collective-permute-done | bytes 1048608 | tf_op jit(solution)/shard_map/ppermute | solution.py:300
  30.4 0.1 pad_maximum_fusion.1
  30.5 2.7 %collective-permute-start.18 = (f32[128,2048]{1,0:T(8,128)S(1)}, f32[128,2048]{1,0:T(8,128)S(1)}, u32[]{:S(2)}, u32[]{:S(2)}) collective-permute-start(f32[128,2048]{1,0:T(8,128)S(1)} %pad_maximum_fusion.1), channel_id=1, source_target_pairs={{0,4},{1,3},{2,6},{3,1},{4,0},{5,7},{6,2},{7,5},{8,12},{9,11},{10,... | collective-permute-start | bytes 3145736 | tf_op jit(solution)/shard_map/ppermute | solution.py:300
  33.2 8.0 %collective-permute-done.11.refs_6_ = f32[640,256]{1,0:T(8,128)S(1)} collective-permute-done((f32[640,256]{1,0:T(8,128)S(1)}, f32[640,256]{1,0:T(8,128)S(1)}, u32[]{:S(2)}, u32[]{:S(2)}) %collective-permute-start.11) | collective-permute-done | bytes 655392 | tf_op jit(solution)/shard_map/ppermute | solution.py:282
  41.3 0.0 collective-permute-start.8
  41.3 0.1 pad_maximum_fusion.2
  41.4 0.0 collective-permute-done.7.refs_6_
  41.4 0.6 collective-permute-start.13
  41.9 0.0 collective-permute-done.5.refs_8_
  41.9 3.4 %collective-permute-start.12 = (f32[640,256]{1,0:T(8,128)S(1)}, f32[640,256]{1,0:T(8,128)S(1)}, u32[]{:S(2)}, u32[]{:S(2)}) collective-permute-start(f32[640,256]{1,0:T(8,128)S(1)} %collective-permute-done.11.refs_6_), channel_id=1, source_target_pairs={{0,16},{16,24},{24,8},{8,0},{1,17},{17,25},{25,9},{9,1},{2,18},{18... | collective-permute-start | bytes 1966088 | tf_op jit(solution)/shard_map/ppermute | solution.py:282
  45.3 0.1 fusion.2
  45.4 4.2 %collective-permute-done.6.refs_9_ = f32[64,4096]{1,0:T(8,128)S(1)} collective-permute-done((f32[64,4096]{1,0:T(8,128)}, f32[64,4096]{1,0:T(8,128)S(1)}, u32[]{:S(2)}, u32[]{:S(2)}) %collective-permute-start.6) | collective-permute-done | bytes 1048608 | tf_op jit(solution)/shard_map/ppermute | solution.py:300
  49.6 0.9 %collective-permute-start.10 = (f32[32,4096]{1,0:T(8,128)S(1)}, f32[32,4096]{1,0:T(8,128)S(1)}, u32[]{:S(2)}, u32[]{:S(2)}) collective-permute-start(f32[32,4096]{1,0:T(8,128)S(1)} %get-tuple-element.59), channel_id=1, source_target_pairs={{0,1},{1,0},{2,3},{3,2},{4,5},{5,4},{6,7},{7,6},{8,9},{9,8},{10,11... | collective-permute-start | bytes 1572872 | tf_op jit(solution)/shard_map/ppermute | solution.py:277
  50.4 0.0 collective-permute-done.13.refs_8_
  50.4 0.0 collective-permute-start.9
  50.5 0.0 collective-permute-done.8.refs_7_
  50.5 1.5 %collective-permute-done.10.refs_11_ = f32[32,4096]{1,0:T(8,128)S(1)} collective-permute-done((f32[32,4096]{1,0:T(8,128)S(1)}, f32[32,4096]{1,0:T(8,128)S(1)}, u32[]{:S(2)}, u32[]{:S(2)}) %collective-permute-start.10) | collective-permute-done | bytes 524320 | tf_op jit(solution)/shard_map/ppermute | solution.py:277
  52.0 0.7 collective-permute-done.9.refs_10_
  52.7 6.8 %collective-permute-done.12.refs_7_ = f32[640,256]{1,0:T(8,128)S(1)} collective-permute-done((f32[640,256]{1,0:T(8,128)S(1)}, f32[640,256]{1,0:T(8,128)S(1)}, u32[]{:S(2)}, u32[]{:S(2)}) %collective-permute-start.12) | collective-permute-done | bytes 655392 | tf_op jit(solution)/shard_map/ppermute | solution.py:282
  59.6 0.0 copy-start.3
  59.6 0.0 copy-start.4
  59.6 0.0 copy-start.5
  59.6 0.0 copy-start.6
  59.6 0.0 copy-start.7
  59.6 0.1 collective-permute-start.14
  59.8 0.1 pad_maximum_fusion
  59.9 0.0 copy-start
  59.9 0.0 copy-start.1
  59.9 0.0 copy-start.2
  59.9 0.5 collective-permute-start.15
  60.4 0.4 collective-permute-done.18.refs_14_
  60.8 0.6 collective-permute-done.14.refs_9_
  61.4 0.1 fusion
  61.5 0.2 collective-permute-start.19
  61.7 0.4 collective-permute-start.20
  62.1 0.1 fusion.1
  62.2 0.2 collective-permute-start.16
  62.4 0.4 collective-permute-start.17
  62.8 0.0 copy-done.6
  62.8 2.9 %shard_map.104 = (bf16[768,256]{1,0:T(8,128)(2,1)S(1)}, bf16[768,256]{1,0:T(8,128)(2,1)S(1)}, bf16[256,256]{1,0:T(8,128)(2,1)S(1)}, bf16[256,256]{1,0:T(8,128)(2...) custom-call(f32[128,512]{1,0:T(8,128)S(1)} %copy-done.3, f32[128,512]{1,0:T(8,128)S(1)} %copy-done.4, ...), custom_call_target="tpu_custom_call" | custom-call | flops 1024 | bytes 1024 | tf_op jit(solution)/shard_map/pallas_call | solution.py:133
  65.6 0.0 collective-permute-done.19.refs_15_
  65.6 0.0 collective-permute-done.20.refs_16_
  65.7 0.0 collective-permute-done.16.refs_12_
  65.7 0.1 collective-permute-done.17.refs_13_
  65.8 7.3 %shard_map.105 = (f32[4096,256]{1,0:T(8,128)}, f32[2048,256]{1,0:T(8,128)S(1)}) custom-call(f32[64,4096]{1,0:T(8,128)S(1)} %bitcast.9, f32[64,4096]{1,0:T(8,128)S(1)} %bitcast.5, f32[64,4096]{1,0:T(8,128)S(1)} %collective-permute-done.2.refs_2_, f32[64,4096]{1,0:T(8,128)S(1)} %collective-permute-done.3.refs_3_, f32[64,4096]{1,0:T(8,128)S(1)} %collective-permute-done.refs_4_, ...), custom_call_target="tpu_custom_call" | custom-call | flops 1024 | bytes 1024 | tf_op jit(solution)/shard_map/pallas_call | solution.py:202
  73.1 1.7 %collective-permute-done.15.panel = f32[128,2048]{1,0:T(8,128)S(1)} collective-permute-done((f32[128,2048]{1,0:T(8,128)S(1)}, f32[128,2048]{1,0:T(8,128)S(1)}, u32[]{:S(2)}, u32[]{:S(2)}) %collective-permute-start.15) | collective-permute-done | bytes 1048608 | tf_op jit(solution)/shard_map/ppermute | solution.py:300
  74.8 0.0 collective-permute-start.21
  74.8 1.6 %shard_map.106.rest = f32[2048,256]{1,0:T(8,128)S(1)} custom-call(f32[128,2048]{1,0:T(8,128)S(1)} %collective-permute-done.15.panel, bf16[256,256]{1,0:T(8,128)(2,1)S(1)} %get-tuple-element.50.refs_19_.high, bf16[256,256]{1,0:T(8,128)(2,1)S(1)} %get-tuple-element.51.refs_20_.low, ...), custom_call_target="tpu_custom_call", output_to_operand_aliasing={{}: (3, {})} | custom-call | flops 1024 | bytes 1024 | tf_op jit(solution)/shard_map/pallas_call | solution.py:230
  76.4 1.1 %collective-permute-done.21.panel = f32[128,2048]{1,0:T(8,128)S(1)} collective-permute-done((f32[128,2048]{1,0:T(8,128)S(1)}, f32[128,2048]{1,0:T(8,128)S(1)}, u32[]{:S(2)}, u32[]{:S(2)}) %collective-permute-start.21) | collective-permute-done | bytes 1048608 | tf_op jit(solution)/shard_map/ppermute | solution.py:277
  77.5 2.1 %shard_map.107 = f32[4096,256]{1,0:T(8,128)} custom-call(f32[128,2048]{1,0:T(8,128)S(1)} %collective-permute-done.21.panel, bf16[256,256]{1,0:T(8,128)(2,1)S(1)} %get-tuple-element.50.refs_19_.high, bf16[256,256]{1,0:T(8,128)(2,1)S(1)} %get-tuple-element.51.refs_20_.low, f32[2048,256]{1,0:T(8,128)S(1)} %shard_map.106.rest, ...), custom_call_target="tpu_custom_call", output_to_operand_aliasing={{}: (4, {})} | custom-call | flops 1024 | bytes 1024 | tf_op jit(solution)/shard_map/pallas_call | solution.py:261
  (14 shorter events, 0.2 us)
Async XLA Ops:
  0.6 16.0 %collective-permute-start = (f32[64,4096]{1,0:T(8,128)}, f32[64,4096]{1,0:T(8,128)S(1)}, u32[]{:S(2)}, u32[]{:S(2)}) collective-permute-start(f32[64,4096]{1,0:T(8,128)} %bitcast.6), channel_id=1, source_target_pairs={{0,2},{1,5},{2,0},{3,7},{4,6},{5,1},{6,4},{7,3},{8,10},{9,13},{10,... | collective-permute-start | bytes 3145736 | tf_op jit(solution)/shard_map/ppermute | solution.py:300
  3.6 19.7 %collective-permute-start.2 = (f32[64,4096]{1,0:T(8,128)}, f32[64,4096]{1,0:T(8,128)S(1)}, u32[]{:S(2)}, u32[]{:S(2)}) collective-permute-start(f32[64,4096]{1,0:T(8,128)} %bitcast.7), channel_id=1, source_target_pairs={{0,1},{1,0},{2,3},{3,2},{4,5},{5,4},{6,7},{7,6},{8,9},{9,8},{10,11... | collective-permute-start | bytes 3145736 | tf_op jit(solution)/shard_map/ppermute | solution.py:277
  3.6 19.7 %collective-permute-start.3 = (f32[64,4096]{1,0:T(8,128)}, f32[64,4096]{1,0:T(8,128)S(1)}, u32[]{:S(2)}, u32[]{:S(2)}) collective-permute-start(f32[64,4096]{1,0:T(8,128)} %bitcast.2), channel_id=1, source_target_pairs={{0,1},{1,0},{2,3},{3,2},{4,5},{5,4},{6,7},{7,6},{8,9},{9,8},{10,11... | collective-permute-start | bytes 3145736 | tf_op jit(solution)/shard_map/ppermute | solution.py:277
  6.2 17.1 %collective-permute-start.4 = (f32[640,256]{1,0:T(8,128)}, f32[640,256]{1,0:T(8,128)S(1)}, u32[]{:S(2)}, u32[]{:S(2)}) collective-permute-start(f32[640,256]{1,0:T(8,128)} %shard_map.103), channel_id=1, source_target_pairs={{0,16},{16,24},{24,8},{8,0},{1,17},{17,25},{25,9},{9,1},{2,18},{18... | collective-permute-start | bytes 1966088 | tf_op jit(solution)/shard_map/ppermute | solution.py:282
  8.8 21.6 %collective-permute-start.1 = (f32[64,4096]{1,0:T(8,128)}, f32[64,4096]{1,0:T(8,128)S(1)}, u32[]{:S(2)}, u32[]{:S(2)}) collective-permute-start(f32[64,4096]{1,0:T(8,128)} %bitcast.3), channel_id=1, source_target_pairs={{0,2},{1,5},{2,0},{3,7},{4,6},{5,1},{6,4},{7,3},{8,10},{9,13},{10,... | collective-permute-start | bytes 3145736 | tf_op jit(solution)/shard_map/ppermute | solution.py:300
  16.6 24.7 %collective-permute-start.7 = (f32[64,4096]{1,0:T(8,128)S(1)}, f32[64,4096]{1,0:T(8,128)S(1)}, u32[]{:S(2)}, u32[]{:S(2)}) collective-permute-start(f32[64,4096]{1,0:T(8,128)S(1)} %collective-permute-done.refs_4_), channel_id=1, source_target_pairs={{0,1},{1,0},{2,3},{3,2},{4,5},{5,4},{6,7},{7,6},{8,9},{9,8},{10,11... | collective-permute-start | bytes 3145736 | tf_op jit(solution)/shard_map/ppermute | solution.py:277
  23.3 18.6 %collective-permute-start.5 = (f32[64,4096]{1,0:T(8,128)}, f32[64,4096]{1,0:T(8,128)S(1)}, u32[]{:S(2)}, u32[]{:S(2)}) collective-permute-start(f32[64,4096]{1,0:T(8,128)} %bitcast.8), channel_id=1, source_target_pairs={{0,4},{1,3},{2,6},{3,1},{4,0},{5,7},{6,2},{7,5},{8,12},{9,11},{10,... | collective-permute-start | bytes 3145736 | tf_op jit(solution)/shard_map/ppermute | solution.py:300
  24.8 16.4 %collective-permute-start.11 = (f32[640,256]{1,0:T(8,128)S(1)}, f32[640,256]{1,0:T(8,128)S(1)}, u32[]{:S(2)}, u32[]{:S(2)}) collective-permute-start(f32[640,256]{1,0:T(8,128)S(1)} %collective-permute-done.4.refs_5_), channel_id=1, source_target_pairs={{0,16},{16,24},{24,8},{8,0},{1,17},{17,25},{25,9},{9,1},{2,18},{18... | collective-permute-start | bytes 1966088 | tf_op jit(solution)/shard_map/ppermute | solution.py:282
  28.1 21.4 %collective-permute-start.6 = (f32[64,4096]{1,0:T(8,128)}, f32[64,4096]{1,0:T(8,128)S(1)}, u32[]{:S(2)}, u32[]{:S(2)}) collective-permute-start(f32[64,4096]{1,0:T(8,128)} %bitcast.4), channel_id=1, source_target_pairs={{0,4},{1,3},{2,6},{3,1},{4,0},{5,7},{6,2},{7,5},{8,12},{9,11},{10,... | collective-permute-start | bytes 3145736 | tf_op jit(solution)/shard_map/ppermute | solution.py:300
  30.5 30.3 %collective-permute-start.18 = (f32[128,2048]{1,0:T(8,128)S(1)}, f32[128,2048]{1,0:T(8,128)S(1)}, u32[]{:S(2)}, u32[]{:S(2)}) collective-permute-start(f32[128,2048]{1,0:T(8,128)S(1)} %pad_maximum_fusion.1), channel_id=1, source_target_pairs={{0,4},{1,3},{2,6},{3,1},{4,0},{5,7},{6,2},{7,5},{8,12},{9,11},{10,... | collective-permute-start | bytes 3145736 | tf_op jit(solution)/shard_map/ppermute | solution.py:300
  41.3 9.2 %collective-permute-start.8 = (f32[64,4096]{1,0:T(8,128)S(1)}, f32[64,4096]{1,0:T(8,128)S(1)}, u32[]{:S(2)}, u32[]{:S(2)}) collective-permute-start(f32[64,4096]{1,0:T(8,128)S(1)} %collective-permute-done.1.refs_5_), channel_id=1, source_target_pairs={{0,1},{1,0},{2,3},{3,2},{4,5},{5,4},{6,7},{7,6},{8,9},{9,8},{10,11... | collective-permute-start | bytes 3145736 | tf_op jit(solution)/shard_map/ppermute | solution.py:277
  41.4 9.1 %collective-permute-start.13 = (f32[768,256]{1,0:T(8,128)S(1)}, f32[768,256]{1,0:T(8,128)S(1)}, u32[]{:S(2)}, u32[]{:S(2)}) collective-permute-start(f32[768,256]{1,0:T(8,128)S(1)} %pad_maximum_fusion.2), channel_id=1, source_target_pairs={{0,1},{1,0},{2,3},{3,2},{4,5},{5,4},{6,7},{7,6},{8,9},{9,8},{10,11... | collective-permute-start | bytes 2359304 | tf_op jit(solution)/shard_map/ppermute | solution.py:277
  41.9 17.6 %collective-permute-start.12 = (f32[640,256]{1,0:T(8,128)S(1)}, f32[640,256]{1,0:T(8,128)S(1)}, u32[]{:S(2)}, u32[]{:S(2)}) collective-permute-start(f32[640,256]{1,0:T(8,128)S(1)} %collective-permute-done.11.refs_6_), channel_id=1, source_target_pairs={{0,16},{16,24},{24,8},{8,0},{1,17},{17,25},{25,9},{9,1},{2,18},{18... | collective-permute-start | bytes 1966088 | tf_op jit(solution)/shard_map/ppermute | solution.py:282
  49.6 2.4 %collective-permute-start.10 = (f32[32,4096]{1,0:T(8,128)S(1)}, f32[32,4096]{1,0:T(8,128)S(1)}, u32[]{:S(2)}, u32[]{:S(2)}) collective-permute-start(f32[32,4096]{1,0:T(8,128)S(1)} %get-tuple-element.59), channel_id=1, source_target_pairs={{0,1},{1,0},{2,3},{3,2},{4,5},{5,4},{6,7},{7,6},{8,9},{9,8},{10,11... | collective-permute-start | bytes 1572872 | tf_op jit(solution)/shard_map/ppermute | solution.py:277
  50.4 2.3 %collective-permute-start.9 = (f32[32,4096]{1,0:T(8,128)S(1)}, f32[32,4096]{1,0:T(8,128)S(1)}, u32[]{:S(2)}, u32[]{:S(2)}) collective-permute-start(f32[32,4096]{1,0:T(8,128)S(1)} %get-tuple-element.60), channel_id=1, source_target_pairs={{0,1},{1,0},{2,3},{3,2},{4,5},{5,4},{6,7},{7,6},{8,9},{9,8},{10,11... | collective-permute-start | bytes 1572872 | tf_op jit(solution)/shard_map/ppermute | solution.py:277
  59.6 3.2 %copy-start.3 = (f32[128,512]{1,0:T(8,128)S(1)}, f32[128,512]{1,0:T(8,128)}, u32[]{:S(2)}) copy-start(f32[128,512]{1,0:T(8,128)} %refs_0_.3) | copy-start | bytes 786436
  59.6 3.2 %copy-start.4 = (f32[128,512]{1,0:T(8,128)S(1)}, f32[128,512]{1,0:T(8,128)}, u32[]{:S(2)}) copy-start(f32[128,512]{1,0:T(8,128)} %refs_1_.3) | copy-start | bytes 786436
  59.6 3.2 %copy-start.5 = (f32[128,512]{1,0:T(8,128)S(1)}, f32[128,512]{1,0:T(8,128)}, u32[]{:S(2)}) copy-start(f32[128,512]{1,0:T(8,128)} %refs_2_.3) | copy-start | bytes 786436
  59.6 3.1 %copy-start.6 = (f32[128,256]{1,0:T(8,128)S(1)}, f32[128,256]{1,0:T(8,128)}, u32[]{:S(2)}) copy-start(f32[128,256]{1,0:T(8,128)} %refs_3_.3) | copy-start | bytes 393220
  59.6 3.1 %copy-start.7 = (f32[128,256]{1,0:T(8,128)S(1)}, f32[128,256]{1,0:T(8,128)}, u32[]{:S(2)}) copy-start(f32[128,256]{1,0:T(8,128)} %refs_4_.3) | copy-start | bytes 393220
  59.6 1.8 %collective-permute-start.14 = (f32[384,256]{1,0:T(8,128)S(1)}, f32[384,256]{1,0:T(8,128)S(1)}, u32[]{:S(2)}, u32[]{:S(2)}) collective-permute-start(f32[384,256]{1,0:T(8,128)S(1)} %slice.23), channel_id=1, source_target_pairs={{0,1},{1,0},{2,3},{3,2},{4,5},{5,4},{6,7},{7,6},{8,9},{9,8},{10,11... | collective-permute-start | bytes 1179656 | tf_op jit(solution)/shard_map/ppermute | solution.py:277
  59.9 5.8 %copy-start = (f32[4096,256]{1,0:T(8,128)S(1)}, f32[4096,256]{1,0:T(8,128)}, u32[]{:S(2)}) copy-start(f32[4096,256]{1,0:T(8,128)} %refs_21_.1) | copy-start | bytes 12582916
  59.9 5.8 %copy-start.1 = (f32[4096,64]{0,1:T(8,128)S(1)}, f32[4096,64]{0,1:T(8,128)}, u32[]{:S(2)}) copy-start(f32[4096,64]{0,1:T(8,128)} %param.12) | copy-start | bytes 3145732
  59.9 5.8 %copy-start.2 = (f32[4096,64]{0,1:T(8,128)S(1)}, f32[4096,64]{0,1:T(8,128)}, u32[]{:S(2)}) copy-start(f32[4096,64]{0,1:T(8,128)} %param.11) | copy-start | bytes 3145732
  59.9 14.9 %collective-permute-start.15 = (f32[128,2048]{1,0:T(8,128)S(1)}, f32[128,2048]{1,0:T(8,128)S(1)}, u32[]{:S(2)}, u32[]{:S(2)}) collective-permute-start(f32[128,2048]{1,0:T(8,128)S(1)} %pad_maximum_fusion), channel_id=1, source_target_pairs={{0,4},{1,3},{2,6},{3,1},{4,0},{5,7},{6,2},{7,5},{8,12},{9,11},{10,... | collective-permute-start | bytes 3145736 | tf_op jit(solution)/shard_map/ppermute | solution.py:300
  61.5 4.1 %collective-permute-start.19 = (f32[64,2048]{1,0:T(8,128)S(1)}, f32[64,2048]{1,0:T(8,128)S(1)}, u32[]{:S(2)}, u32[]{:S(2)}) collective-permute-start(f32[64,2048]{1,0:T(8,128)S(1)} %get-tuple-element.56), channel_id=1, source_target_pairs={{0,1},{1,0},{2,3},{3,2},{4,5},{5,4},{6,7},{7,6},{8,9},{9,8},{10,11... | collective-permute-start | bytes 1572872 | tf_op jit(solution)/shard_map/ppermute | solution.py:277
  61.7 3.9 %collective-permute-start.20 = (f32[64,2048]{1,0:T(8,128)S(1)}, f32[64,2048]{1,0:T(8,128)S(1)}, u32[]{:S(2)}, u32[]{:S(2)}) collective-permute-start(f32[64,2048]{1,0:T(8,128)S(1)} %get-tuple-element.55), channel_id=1, source_target_pairs={{0,1},{1,0},{2,3},{3,2},{4,5},{5,4},{6,7},{7,6},{8,9},{9,8},{10,11... | collective-permute-start | bytes 1572872 | tf_op jit(solution)/shard_map/ppermute | solution.py:277
  62.2 3.5 %collective-permute-start.16 = (f32[32,4096]{1,0:T(8,128)S(1)}, f32[32,4096]{1,0:T(8,128)S(1)}, u32[]{:S(2)}, u32[]{:S(2)}) collective-permute-start(f32[32,4096]{1,0:T(8,128)S(1)} %get-tuple-element.58), channel_id=1, source_target_pairs={{0,1},{1,0},{2,3},{3,2},{4,5},{5,4},{6,7},{7,6},{8,9},{9,8},{10,11... | collective-permute-start | bytes 1572872 | tf_op jit(solution)/shard_map/ppermute | solution.py:277
  62.4 3.4 %collective-permute-start.17 = (f32[32,4096]{1,0:T(8,128)S(1)}, f32[32,4096]{1,0:T(8,128)S(1)}, u32[]{:S(2)}, u32[]{:S(2)}) collective-permute-start(f32[32,4096]{1,0:T(8,128)S(1)} %get-tuple-element.57), channel_id=1, source_target_pairs={{0,1},{1,0},{2,3},{3,2},{4,5},{5,4},{6,7},{7,6},{8,9},{9,8},{10,11... | collective-permute-start | bytes 1572872 | tf_op jit(solution)/shard_map/ppermute | solution.py:277
  74.8 2.7 %collective-permute-start.21 = (f32[128,2048]{1,0:T(8,128)S(1)}, f32[128,2048]{1,0:T(8,128)S(1)}, u32[]{:S(2)}, u32[]{:S(2)}) collective-permute-start(f32[128,2048]{1,0:T(8,128)S(1)} %collective-permute-done.15.panel), channel_id=1, source_target_pairs={{0,1},{1,0},{2,3},{3,2},{4,5},{5,4},{6,7},{7,6},{8,9},{9,8},{10,11... | collective-permute-start | bytes 3145736 | tf_op jit(solution)/shard_map/ppermute | solution.py:277

commit v6 on v5

--- a/solution.py
+++ b/solution.py
@@ -154,8 +154,10 @@
 
 
 def turned_product(panels, factor, rows):
-    panel = jnp.concatenate([ref[:, rows] for ref in panels], axis=0)
-    return product(split(panel), factor, contract=0)
+    high, low = split(jnp.concatenate([ref[:, rows] for ref in panels], axis=0))
+    left = jnp.concatenate([high, high, low], axis=0)
+    right = jnp.concatenate([factor[0], factor[1], factor[0]], axis=0)
+    return lax.dot_general(left, right, (((0,), (0,)), ((), ())), preferred_element_type=jnp.float32)
 
 
 def update_kernel(near_count, far_count, tile, *refs):

time: 79.7 us -> 79.5 us (level)
  no operation moved by 1% of the time
where the time goes in v6:
time: 79.5 us; the launch traced here: 79.3 us
  waiting for transfers between devices  40.9 us (51%)
  starting transfers between devices  21.3 us (27%)
  Pallas kernels  15.6 us (20%)
  between operations  0.84 us (1%)
    ppermute x3, waiting for transfers between devices, onward(): return lax.ppermute(value, 'row', list(zip(ring, ring[1:] + ring[:1])))  21.5 us
    ppermute x6, waiting for transfers between devices, cross(): lax.ppermute(value, 'col', [(i, i ^ masks[i % 2]) for i in range(col_coun...  15 us
    ppermute x3, starting transfers between devices, onward(): return lax.ppermute(value, 'row', list(zip(ring, ring[1:] + ring[:1])))  9.24 us
    ppermute x6, starting transfers between devices, cross(): lax.ppermute(value, 'col', [(i, i ^ masks[i % 2]) for i in range(col_coun...  8.83 us
    pallas_call x1, Pallas kernels, update(): pl.pallas_call(functools.partial(update_kernel, len(near), len(far), tile...  7.42 us
    ppermute x13, waiting for transfers between devices, swap(): return lax.ppermute(value, 'col', [(i, i ^ bit) for i in range(col_count)])  4.33 us
    ppermute x13, starting transfers between devices, swap(): return lax.ppermute(value, 'col', [(i, i ^ bit) for i in range(col_count)])  3.2 us
    pallas_call x1, Pallas kernels, solve(): pl.pallas_call(functools.partial(solve_kernel, steps, block), out_shape=o...  2.86 us
  transfers between devices with their start and end apart: 22, of which 13 were waited for; matrix products, arithmetic and copies ran while one was open for 1% of the time, Pallas kernels for 17%

profile of v6, /device:TPU:0, one launch (start us, length us, event | category | flops | bytes accessed | tf_op | source)
XLA Modules:
  0.0 79.3 jit_solution(4836624249486242720)
XLA Ops:
  0.6 3.0 %collective-permute-start = (f32[64,4096]{1,0:T(8,128)}, f32[64,4096]{1,0:T(8,128)S(1)}, u32[]{:S(2)}, u32[]{:S(2)}) collective-permute-start(f32[64,4096]{1,0:T(8,128)} %bitcast.6), channel_id=1, source_target_pairs={{0,2},{1,5},{2,0},{3,7},{4,6},{5,1},{6,4},{7,3},{8,10},{9,13},{10,... | collective-permute-start | bytes 3145736 | tf_op jit(solution)/shard_map/ppermute | solution.py:302
  3.6 0.0 collective-permute-start.2
  3.6 0.5 collective-permute-start.3
  4.1 2.1 %shard_map.103 = f32[640,256]{1,0:T(8,128)} custom-call(f32[128,512]{1,0:T(8,128)} %refs_0_.3, f32[128,512]{1,0:T(8,128)} %refs_1_.3, f32[128,512]{1,0:T(8,128)} %refs_2_.3, f32[128,256]{1,0:T(8,128)} %refs_3_.3, f32[128,256]{1,0:T(8,128)} %refs_4_.3), custom_call_target="tpu_custom_call" | custom-call | flops 1024 | bytes 1024 | tf_op jit(solution)/shard_map/pallas_call | solution.py:58
  6.2 2.6 %collective-permute-start.4 = (f32[640,256]{1,0:T(8,128)}, f32[640,256]{1,0:T(8,128)S(1)}, u32[]{:S(2)}, u32[]{:S(2)}) collective-permute-start(f32[640,256]{1,0:T(8,128)} %shard_map.103), channel_id=1, source_target_pairs={{0,16},{16,24},{24,8},{8,0},{1,17},{17,25},{25,9},{9,1},{2,18},{18... | collective-permute-start | bytes 1966088 | tf_op jit(solution)/shard_map/ppermute | solution.py:284
  8.8 0.6 collective-permute-start.1
  9.4 7.2 %collective-permute-done.refs_4_ = f32[64,4096]{1,0:T(8,128)S(1)} collective-permute-done((f32[64,4096]{1,0:T(8,128)}, f32[64,4096]{1,0:T(8,128)S(1)}, u32[]{:S(2)}, u32[]{:S(2)}) %collective-permute-start) | collective-permute-done | bytes 1048608 | tf_op jit(solution)/shard_map/ppermute | solution.py:302
  16.6 0.0 collective-permute-start.7
  16.6 6.7 %collective-permute-done.4.refs_5_ = f32[640,256]{1,0:T(8,128)S(1)} collective-permute-done((f32[640,256]{1,0:T(8,128)}, f32[640,256]{1,0:T(8,128)S(1)}, u32[]{:S(2)}, u32[]{:S(2)}) %collective-permute-start.4) | collective-permute-done | bytes 655392 | tf_op jit(solution)/shard_map/ppermute | solution.py:284
  23.3 0.0 collective-permute-done.2.refs_2_
  23.3 0.0 collective-permute-done.3.refs_3_
  23.3 1.5 %collective-permute-start.5 = (f32[64,4096]{1,0:T(8,128)}, f32[64,4096]{1,0:T(8,128)S(1)}, u32[]{:S(2)}, u32[]{:S(2)}) collective-permute-start(f32[64,4096]{1,0:T(8,128)} %bitcast.8), channel_id=1, source_target_pairs={{0,4},{1,3},{2,6},{3,1},{4,0},{5,7},{6,2},{7,5},{8,12},{9,11},{10,... | collective-permute-start | bytes 3145736 | tf_op jit(solution)/shard_map/ppermute | solution.py:302
  24.8 3.3 %collective-permute-start.11 = (f32[640,256]{1,0:T(8,128)S(1)}, f32[640,256]{1,0:T(8,128)S(1)}, u32[]{:S(2)}, u32[]{:S(2)}) collective-permute-start(f32[640,256]{1,0:T(8,128)S(1)} %collective-permute-done.4.refs_5_), channel_id=1, source_target_pairs={{0,16},{16,24},{24,8},{8,0},{1,17},{17,25},{25,9},{9,1},{2,18},{18... | collective-permute-start | bytes 1966088 | tf_op jit(solution)/shard_map/ppermute | solution.py:284
  28.1 0.6 collective-permute-start.6
  28.8 1.6 %collective-permute-done.1.refs_5_ = f32[64,4096]{1,0:T(8,128)S(1)} collective-permute-done((f32[64,4096]{1,0:T(8,128)}, f32[64,4096]{1,0:T(8,128)S(1)}, u32[]{:S(2)}, u32[]{:S(2)}) %collective-permute-start.1) | collective-permute-done | bytes 1048608 | tf_op jit(solution)/shard_map/ppermute | solution.py:302
  30.4 0.1 pad_maximum_fusion.1
  30.5 2.7 %collective-permute-start.18 = (f32[128,2048]{1,0:T(8,128)S(1)}, f32[128,2048]{1,0:T(8,128)S(1)}, u32[]{:S(2)}, u32[]{:S(2)}) collective-permute-start(f32[128,2048]{1,0:T(8,128)S(1)} %pad_maximum_fusion.1), channel_id=1, source_target_pairs={{0,4},{1,3},{2,6},{3,1},{4,0},{5,7},{6,2},{7,5},{8,12},{9,11},{10,... | collective-permute-start | bytes 3145736 | tf_op jit(solution)/shard_map/ppermute | solution.py:302
  33.2 8.0 %collective-permute-done.11.refs_6_ = f32[640,256]{1,0:T(8,128)S(1)} collective-permute-done((f32[640,256]{1,0:T(8,128)S(1)}, f32[640,256]{1,0:T(8,128)S(1)}, u32[]{:S(2)}, u32[]{:S(2)}) %collective-permute-start.11) | collective-permute-done | bytes 655392 | tf_op jit(solution)/shard_map/ppermute | solution.py:284
  41.3 0.0 collective-permute-start.8
  41.3 0.1 pad_maximum_fusion.2
  41.4 0.0 collective-permute-done.7.refs_6_
  41.4 0.6 collective-permute-start.13
  41.9 0.0 collective-permute-done.5.refs_8_
  41.9 3.4 %collective-permute-start.12 = (f32[640,256]{1,0:T(8,128)S(1)}, f32[640,256]{1,0:T(8,128)S(1)}, u32[]{:S(2)}, u32[]{:S(2)}) collective-permute-start(f32[640,256]{1,0:T(8,128)S(1)} %collective-permute-done.11.refs_6_), channel_id=1, source_target_pairs={{0,16},{16,24},{24,8},{8,0},{1,17},{17,25},{25,9},{9,1},{2,18},{18... | collective-permute-start | bytes 1966088 | tf_op jit(solution)/shard_map/ppermute | solution.py:284
  45.3 0.1 fusion.2
  45.4 4.2 %collective-permute-done.6.refs_9_ = f32[64,4096]{1,0:T(8,128)S(1)} collective-permute-done((f32[64,4096]{1,0:T(8,128)}, f32[64,4096]{1,0:T(8,128)S(1)}, u32[]{:S(2)}, u32[]{:S(2)}) %collective-permute-start.6) | collective-permute-done | bytes 1048608 | tf_op jit(solution)/shard_map/ppermute | solution.py:302
  49.6 0.9 %collective-permute-start.10 = (f32[32,4096]{1,0:T(8,128)S(1)}, f32[32,4096]{1,0:T(8,128)S(1)}, u32[]{:S(2)}, u32[]{:S(2)}) collective-permute-start(f32[32,4096]{1,0:T(8,128)S(1)} %get-tuple-element.59), channel_id=1, source_target_pairs={{0,1},{1,0},{2,3},{3,2},{4,5},{5,4},{6,7},{7,6},{8,9},{9,8},{10,11... | collective-permute-start | bytes 1572872 | tf_op jit(solution)/shard_map/ppermute | solution.py:279
  50.4 0.0 collective-permute-done.13.refs_8_
  50.4 0.0 collective-permute-start.9
  50.5 0.0 collective-permute-done.8.refs_7_
  50.5 1.5 %collective-permute-done.10.refs_11_ = f32[32,4096]{1,0:T(8,128)S(1)} collective-permute-done((f32[32,4096]{1,0:T(8,128)S(1)}, f32[32,4096]{1,0:T(8,128)S(1)}, u32[]{:S(2)}, u32[]{:S(2)}) %collective-permute-start.10) | collective-permute-done | bytes 524320 | tf_op jit(solution)/shard_map/ppermute | solution.py:279
  52.0 0.7 collective-permute-done.9.refs_10_
  52.7 6.8 %collective-permute-done.12.refs_7_ = f32[640,256]{1,0:T(8,128)S(1)} collective-permute-done((f32[640,256]{1,0:T(8,128)S(1)}, f32[640,256]{1,0:T(8,128)S(1)}, u32[]{:S(2)}, u32[]{:S(2)}) %collective-permute-start.12) | collective-permute-done | bytes 655392 | tf_op jit(solution)/shard_map/ppermute | solution.py:284
  59.6 0.0 copy-start.3
  59.6 0.0 copy-start.4
  59.6 0.0 copy-start.5
  59.6 0.0 copy-start.6
  59.6 0.0 copy-start.7
  59.6 0.1 collective-permute-start.14
  59.8 0.1 pad_maximum_fusion
  59.9 0.0 copy-start
  59.9 0.0 copy-start.1
  59.9 0.0 copy-start.2
  59.9 0.5 collective-permute-start.15
  60.4 0.4 collective-permute-done.18.refs_14_
  60.8 0.6 collective-permute-done.14.refs_9_
  61.4 0.1 fusion
  61.5 0.2 collective-permute-start.19
  61.7 0.4 collective-permute-start.20
  62.1 0.1 fusion.1
  62.2 0.2 collective-permute-start.16
  62.4 0.4 collective-permute-start.17
  62.8 0.0 copy-done.4
  62.8 2.9 %shard_map.104 = (bf16[768,256]{1,0:T(8,128)(2,1)S(1)}, bf16[768,256]{1,0:T(8,128)(2,1)S(1)}, bf16[256,256]{1,0:T(8,128)(2,1)S(1)}, bf16[256,256]{1,0:T(8,128)(2...) custom-call(f32[128,512]{1,0:T(8,128)S(1)} %copy-done.3, f32[128,512]{1,0:T(8,128)S(1)} %copy-done.4, ...), custom_call_target="tpu_custom_call" | custom-call | flops 1024 | bytes 1024 | tf_op jit(solution)/shard_map/pallas_call | solution.py:133
  65.6 0.0 collective-permute-done.19.refs_15_
  65.6 0.0 collective-permute-done.20.refs_16_
  65.7 0.0 collective-permute-done.16.refs_12_
  65.7 0.1 collective-permute-done.17.refs_13_
  65.8 7.4 %shard_map.105 = (f32[4096,256]{1,0:T(8,128)}, f32[2048,256]{1,0:T(8,128)S(1)}) custom-call(f32[64,4096]{1,0:T(8,128)S(1)} %bitcast.9, f32[64,4096]{1,0:T(8,128)S(1)} %bitcast.5, f32[64,4096]{1,0:T(8,128)S(1)} %collective-permute-done.2.refs_2_, f32[64,4096]{1,0:T(8,128)S(1)} %collective-permute-done.3.refs_3_, f32[64,4096]{1,0:T(8,128)S(1)} %collective-permute-done.refs_4_, ...), custom_call_target="tpu_custom_call" | custom-call | flops 1024 | bytes 1024 | tf_op jit(solution)/shard_map/pallas_call | solution.py:204
  73.2 1.6 %collective-permute-done.15.panel = f32[128,2048]{1,0:T(8,128)S(1)} collective-permute-done((f32[128,2048]{1,0:T(8,128)S(1)}, f32[128,2048]{1,0:T(8,128)S(1)}, u32[]{:S(2)}, u32[]{:S(2)}) %collective-permute-start.15) | collective-permute-done | bytes 1048608 | tf_op jit(solution)/shard_map/ppermute | solution.py:302
  74.8 0.0 collective-permute-start.21
  74.8 1.4 %shard_map.106.rest = f32[2048,256]{1,0:T(8,128)S(1)} custom-call(f32[128,2048]{1,0:T(8,128)S(1)} %collective-permute-done.15.panel, bf16[256,256]{1,0:T(8,128)(2,1)S(1)} %get-tuple-element.50.refs_19_.high, bf16[256,256]{1,0:T(8,128)(2,1)S(1)} %get-tuple-element.51.refs_20_.low, ...), custom_call_target="tpu_custom_call", output_to_operand_aliasing={{}: (3, {})} | custom-call | flops 1024 | bytes 1024 | tf_op jit(solution)/shard_map/pallas_call | solution.py:232
  76.2 1.3 %collective-permute-done.21.panel = f32[128,2048]{1,0:T(8,128)S(1)} collective-permute-done((f32[128,2048]{1,0:T(8,128)S(1)}, f32[128,2048]{1,0:T(8,128)S(1)}, u32[]{:S(2)}, u32[]{:S(2)}) %collective-permute-start.21) | collective-permute-done | bytes 1048608 | tf_op jit(solution)/shard_map/ppermute | solution.py:279
  77.5 1.8 %shard_map.107 = f32[4096,256]{1,0:T(8,128)} custom-call(f32[128,2048]{1,0:T(8,128)S(1)} %collective-permute-done.21.panel, bf16[256,256]{1,0:T(8,128)(2,1)S(1)} %get-tuple-element.50.refs_19_.high, bf16[256,256]{1,0:T(8,128)(2,1)S(1)} %get-tuple-element.51.refs_20_.low, f32[2048,256]{1,0:T(8,128)S(1)} %shard_map.106.rest, ...), custom_call_target="tpu_custom_call", output_to_operand_aliasing={{}: (4, {})} | custom-call | flops 1024 | bytes 1024 | tf_op jit(solution)/shard_map/pallas_call | solution.py:263
  (14 shorter events, 0.2 us)
Async XLA Ops:
  0.6 16.0 %collective-permute-start = (f32[64,4096]{1,0:T(8,128)}, f32[64,4096]{1,0:T(8,128)S(1)}, u32[]{:S(2)}, u32[]{:S(2)}) collective-permute-start(f32[64,4096]{1,0:T(8,128)} %bitcast.6), channel_id=1, source_target_pairs={{0,2},{1,5},{2,0},{3,7},{4,6},{5,1},{6,4},{7,3},{8,10},{9,13},{10,... | collective-permute-start | bytes 3145736 | tf_op jit(solution)/shard_map/ppermute | solution.py:302
  3.6 19.7 %collective-permute-start.2 = (f32[64,4096]{1,0:T(8,128)}, f32[64,4096]{1,0:T(8,128)S(1)}, u32[]{:S(2)}, u32[]{:S(2)}) collective-permute-start(f32[64,4096]{1,0:T(8,128)} %bitcast.7), channel_id=1, source_target_pairs={{0,1},{1,0},{2,3},{3,2},{4,5},{5,4},{6,7},{7,6},{8,9},{9,8},{10,11... | collective-permute-start | bytes 3145736 | tf_op jit(solution)/shard_map/ppermute | solution.py:279
  3.6 19.7 %collective-permute-start.3 = (f32[64,4096]{1,0:T(8,128)}, f32[64,4096]{1,0:T(8,128)S(1)}, u32[]{:S(2)}, u32[]{:S(2)}) collective-permute-start(f32[64,4096]{1,0:T(8,128)} %bitcast.2), channel_id=1, source_target_pairs={{0,1},{1,0},{2,3},{3,2},{4,5},{5,4},{6,7},{7,6},{8,9},{9,8},{10,11... | collective-permute-start | bytes 3145736 | tf_op jit(solution)/shard_map/ppermute | solution.py:279
  6.2 17.1 %collective-permute-start.4 = (f32[640,256]{1,0:T(8,128)}, f32[640,256]{1,0:T(8,128)S(1)}, u32[]{:S(2)}, u32[]{:S(2)}) collective-permute-start(f32[640,256]{1,0:T(8,128)} %shard_map.103), channel_id=1, source_target_pairs={{0,16},{16,24},{24,8},{8,0},{1,17},{17,25},{25,9},{9,1},{2,18},{18... | collective-permute-start | bytes 1966088 | tf_op jit(solution)/shard_map/ppermute | solution.py:284
  8.8 21.6 %collective-permute-start.1 = (f32[64,4096]{1,0:T(8,128)}, f32[64,4096]{1,0:T(8,128)S(1)}, u32[]{:S(2)}, u32[]{:S(2)}) collective-permute-start(f32[64,4096]{1,0:T(8,128)} %bitcast.3), channel_id=1, source_target_pairs={{0,2},{1,5},{2,0},{3,7},{4,6},{5,1},{6,4},{7,3},{8,10},{9,13},{10,... | collective-permute-start | bytes 3145736 | tf_op jit(solution)/shard_map/ppermute | solution.py:302
  16.6 24.7 %collective-permute-start.7 = (f32[64,4096]{1,0:T(8,128)S(1)}, f32[64,4096]{1,0:T(8,128)S(1)}, u32[]{:S(2)}, u32[]{:S(2)}) collective-permute-start(f32[64,4096]{1,0:T(8,128)S(1)} %collective-permute-done.refs_4_), channel_id=1, source_target_pairs={{0,1},{1,0},{2,3},{3,2},{4,5},{5,4},{6,7},{7,6},{8,9},{9,8},{10,11... | collective-permute-start | bytes 3145736 | tf_op jit(solution)/shard_map/ppermute | solution.py:279
  23.3 18.6 %collective-permute-start.5 = (f32[64,4096]{1,0:T(8,128)}, f32[64,4096]{1,0:T(8,128)S(1)}, u32[]{:S(2)}, u32[]{:S(2)}) collective-permute-start(f32[64,4096]{1,0:T(8,128)} %bitcast.8), channel_id=1, source_target_pairs={{0,4},{1,3},{2,6},{3,1},{4,0},{5,7},{6,2},{7,5},{8,12},{9,11},{10,... | collective-permute-start | bytes 3145736 | tf_op jit(solution)/shard_map/ppermute | solution.py:302
  24.8 16.4 %collective-permute-start.11 = (f32[640,256]{1,0:T(8,128)S(1)}, f32[640,256]{1,0:T(8,128)S(1)}, u32[]{:S(2)}, u32[]{:S(2)}) collective-permute-start(f32[640,256]{1,0:T(8,128)S(1)} %collective-permute-done.4.refs_5_), channel_id=1, source_target_pairs={{0,16},{16,24},{24,8},{8,0},{1,17},{17,25},{25,9},{9,1},{2,18},{18... | collective-permute-start | bytes 1966088 | tf_op jit(solution)/shard_map/ppermute | solution.py:284
  28.1 21.4 %collective-permute-start.6 = (f32[64,4096]{1,0:T(8,128)}, f32[64,4096]{1,0:T(8,128)S(1)}, u32[]{:S(2)}, u32[]{:S(2)}) collective-permute-start(f32[64,4096]{1,0:T(8,128)} %bitcast.4), channel_id=1, source_target_pairs={{0,4},{1,3},{2,6},{3,1},{4,0},{5,7},{6,2},{7,5},{8,12},{9,11},{10,... | collective-permute-start | bytes 3145736 | tf_op jit(solution)/shard_map/ppermute | solution.py:302
  30.5 30.3 %collective-permute-start.18 = (f32[128,2048]{1,0:T(8,128)S(1)}, f32[128,2048]{1,0:T(8,128)S(1)}, u32[]{:S(2)}, u32[]{:S(2)}) collective-permute-start(f32[128,2048]{1,0:T(8,128)S(1)} %pad_maximum_fusion.1), channel_id=1, source_target_pairs={{0,4},{1,3},{2,6},{3,1},{4,0},{5,7},{6,2},{7,5},{8,12},{9,11},{10,... | collective-permute-start | bytes 3145736 | tf_op jit(solution)/shard_map/ppermute | solution.py:302
  41.3 9.2 %collective-permute-start.8 = (f32[64,4096]{1,0:T(8,128)S(1)}, f32[64,4096]{1,0:T(8,128)S(1)}, u32[]{:S(2)}, u32[]{:S(2)}) collective-permute-start(f32[64,4096]{1,0:T(8,128)S(1)} %collective-permute-done.1.refs_5_), channel_id=1, source_target_pairs={{0,1},{1,0},{2,3},{3,2},{4,5},{5,4},{6,7},{7,6},{8,9},{9,8},{10,11... | collective-permute-start | bytes 3145736 | tf_op jit(solution)/shard_map/ppermute | solution.py:279
  41.4 9.1 %collective-permute-start.13 = (f32[768,256]{1,0:T(8,128)S(1)}, f32[768,256]{1,0:T(8,128)S(1)}, u32[]{:S(2)}, u32[]{:S(2)}) collective-permute-start(f32[768,256]{1,0:T(8,128)S(1)} %pad_maximum_fusion.2), channel_id=1, source_target_pairs={{0,1},{1,0},{2,3},{3,2},{4,5},{5,4},{6,7},{7,6},{8,9},{9,8},{10,11... | collective-permute-start | bytes 2359304 | tf_op jit(solution)/shard_map/ppermute | solution.py:279
  41.9 17.6 %collective-permute-start.12 = (f32[640,256]{1,0:T(8,128)S(1)}, f32[640,256]{1,0:T(8,128)S(1)}, u32[]{:S(2)}, u32[]{:S(2)}) collective-permute-start(f32[640,256]{1,0:T(8,128)S(1)} %collective-permute-done.11.refs_6_), channel_id=1, source_target_pairs={{0,16},{16,24},{24,8},{8,0},{1,17},{17,25},{25,9},{9,1},{2,18},{18... | collective-permute-start | bytes 1966088 | tf_op jit(solution)/shard_map/ppermute | solution.py:284
  49.6 2.4 %collective-permute-start.10 = (f32[32,4096]{1,0:T(8,128)S(1)}, f32[32,4096]{1,0:T(8,128)S(1)}, u32[]{:S(2)}, u32[]{:S(2)}) collective-permute-start(f32[32,4096]{1,0:T(8,128)S(1)} %get-tuple-element.59), channel_id=1, source_target_pairs={{0,1},{1,0},{2,3},{3,2},{4,5},{5,4},{6,7},{7,6},{8,9},{9,8},{10,11... | collective-permute-start | bytes 1572872 | tf_op jit(solution)/shard_map/ppermute | solution.py:279
  50.4 2.3 %collective-permute-start.9 = (f32[32,4096]{1,0:T(8,128)S(1)}, f32[32,4096]{1,0:T(8,128)S(1)}, u32[]{:S(2)}, u32[]{:S(2)}) collective-permute-start(f32[32,4096]{1,0:T(8,128)S(1)} %get-tuple-element.60), channel_id=1, source_target_pairs={{0,1},{1,0},{2,3},{3,2},{4,5},{5,4},{6,7},{7,6},{8,9},{9,8},{10,11... | collective-permute-start | bytes 1572872 | tf_op jit(solution)/shard_map/ppermute | solution.py:279
  59.6 3.2 %copy-start.3 = (f32[128,512]{1,0:T(8,128)S(1)}, f32[128,512]{1,0:T(8,128)}, u32[]{:S(2)}) copy-start(f32[128,512]{1,0:T(8,128)} %refs_0_.3) | copy-start | bytes 786436
  59.6 3.2 %copy-start.4 = (f32[128,512]{1,0:T(8,128)S(1)}, f32[128,512]{1,0:T(8,128)}, u32[]{:S(2)}) copy-start(f32[128,512]{1,0:T(8,128)} %refs_1_.3) | copy-start | bytes 786436
  59.6 3.2 %copy-start.5 = (f32[128,512]{1,0:T(8,128)S(1)}, f32[128,512]{1,0:T(8,128)}, u32[]{:S(2)}) copy-start(f32[128,512]{1,0:T(8,128)} %refs_2_.3) | copy-start | bytes 786436
  59.6 3.1 %copy-start.6 = (f32[128,256]{1,0:T(8,128)S(1)}, f32[128,256]{1,0:T(8,128)}, u32[]{:S(2)}) copy-start(f32[128,256]{1,0:T(8,128)} %refs_3_.3) | copy-start | bytes 393220
  59.6 3.1 %copy-start.7 = (f32[128,256]{1,0:T(8,128)S(1)}, f32[128,256]{1,0:T(8,128)}, u32[]{:S(2)}) copy-start(f32[128,256]{1,0:T(8,128)} %refs_4_.3) | copy-start | bytes 393220
  59.6 1.8 %collective-permute-start.14 = (f32[384,256]{1,0:T(8,128)S(1)}, f32[384,256]{1,0:T(8,128)S(1)}, u32[]{:S(2)}, u32[]{:S(2)}) collective-permute-start(f32[384,256]{1,0:T(8,128)S(1)} %slice.23), channel_id=1, source_target_pairs={{0,1},{1,0},{2,3},{3,2},{4,5},{5,4},{6,7},{7,6},{8,9},{9,8},{10,11... | collective-permute-start | bytes 1179656 | tf_op jit(solution)/shard_map/ppermute | solution.py:279
  59.9 5.8 %copy-start = (f32[4096,256]{1,0:T(8,128)S(1)}, f32[4096,256]{1,0:T(8,128)}, u32[]{:S(2)}) copy-start(f32[4096,256]{1,0:T(8,128)} %refs_21_.1) | copy-start | bytes 12582916
  59.9 5.8 %copy-start.1 = (f32[4096,64]{0,1:T(8,128)S(1)}, f32[4096,64]{0,1:T(8,128)}, u32[]{:S(2)}) copy-start(f32[4096,64]{0,1:T(8,128)} %param.12) | copy-start | bytes 3145732
  59.9 5.8 %copy-start.2 = (f32[4096,64]{0,1:T(8,128)S(1)}, f32[4096,64]{0,1:T(8,128)}, u32[]{:S(2)}) copy-start(f32[4096,64]{0,1:T(8,128)} %param.11) | copy-start | bytes 3145732
  59.9 14.9 %collective-permute-start.15 = (f32[128,2048]{1,0:T(8,128)S(1)}, f32[128,2048]{1,0:T(8,128)S(1)}, u32[]{:S(2)}, u32[]{:S(2)}) collective-permute-start(f32[128,2048]{1,0:T(8,128)S(1)} %pad_maximum_fusion), channel_id=1, source_target_pairs={{0,4},{1,3},{2,6},{3,1},{4,0},{5,7},{6,2},{7,5},{8,12},{9,11},{10,... | collective-permute-start | bytes 3145736 | tf_op jit(solution)/shard_map/ppermute | solution.py:302
  61.5 4.1 %collective-permute-start.19 = (f32[64,2048]{1,0:T(8,128)S(1)}, f32[64,2048]{1,0:T(8,128)S(1)}, u32[]{:S(2)}, u32[]{:S(2)}) collective-permute-start(f32[64,2048]{1,0:T(8,128)S(1)} %get-tuple-element.56), channel_id=1, source_target_pairs={{0,1},{1,0},{2,3},{3,2},{4,5},{5,4},{6,7},{7,6},{8,9},{9,8},{10,11... | collective-permute-start | bytes 1572872 | tf_op jit(solution)/shard_map/ppermute | solution.py:279
  61.7 3.9 %collective-permute-start.20 = (f32[64,2048]{1,0:T(8,128)S(1)}, f32[64,2048]{1,0:T(8,128)S(1)}, u32[]{:S(2)}, u32[]{:S(2)}) collective-permute-start(f32[64,2048]{1,0:T(8,128)S(1)} %get-tuple-element.55), channel_id=1, source_target_pairs={{0,1},{1,0},{2,3},{3,2},{4,5},{5,4},{6,7},{7,6},{8,9},{9,8},{10,11... | collective-permute-start | bytes 1572872 | tf_op jit(solution)/shard_map/ppermute | solution.py:279
  62.2 3.5 %collective-permute-start.16 = (f32[32,4096]{1,0:T(8,128)S(1)}, f32[32,4096]{1,0:T(8,128)S(1)}, u32[]{:S(2)}, u32[]{:S(2)}) collective-permute-start(f32[32,4096]{1,0:T(8,128)S(1)} %get-tuple-element.58), channel_id=1, source_target_pairs={{0,1},{1,0},{2,3},{3,2},{4,5},{5,4},{6,7},{7,6},{8,9},{9,8},{10,11... | collective-permute-start | bytes 1572872 | tf_op jit(solution)/shard_map/ppermute | solution.py:279
  62.4 3.4 %collective-permute-start.17 = (f32[32,4096]{1,0:T(8,128)S(1)}, f32[32,4096]{1,0:T(8,128)S(1)}, u32[]{:S(2)}, u32[]{:S(2)}) collective-permute-start(f32[32,4096]{1,0:T(8,128)S(1)} %get-tuple-element.57), channel_id=1, source_target_pairs={{0,1},{1,0},{2,3},{3,2},{4,5},{5,4},{6,7},{7,6},{8,9},{9,8},{10,11... | collective-permute-start | bytes 1572872 | tf_op jit(solution)/shard_map/ppermute | solution.py:279
  74.8 2.7 %collective-permute-start.21 = (f32[128,2048]{1,0:T(8,128)S(1)}, f32[128,2048]{1,0:T(8,128)S(1)}, u32[]{:S(2)}, u32[]{:S(2)}) collective-permute-start(f32[128,2048]{1,0:T(8,128)S(1)} %collective-permute-done.15.panel), channel_id=1, source_target_pairs={{0,1},{1,0},{2,3},{3,2},{4,5},{5,4},{6,7},{7,6},{8,9},{9,8},{10,11... | collective-permute-start | bytes 3145736 | tf_op jit(solution)/shard_map/ppermute | solution.py:279

commit v7 on v6

--- a/solution.py
+++ b/solution.py
@@ -9,7 +9,7 @@
 
 VMEM_BYTES = 24 * 2**20
 UPDATE_BYTES = 32 * 2**20
-UPDATE_TILE, LAST_TILE = 1024, 512
+UPDATE_TILE, LAST_TILE = 1024, 256
 COST = pl.CostEstimate(flops=1024, bytes_accessed=1024, transcendentals=0)
 INNER = 8
 CORE, ACROSS, UP = 1, 2, 4

time: 79.5 us -> 79.3 us (level)
  waiting for transfers between devices: 40.9 us -> 40.1 us
  transfers between devices with their start and end apart: 22 -> 22, of which waited for: 13 -> 13; matrix products, arithmetic and copies ran while one was open for 1% -> 1% of each run, Pallas kernels for 17% -> 18%
where the time goes in v7:
time: 79.3 us; the launch traced here: 79.2 us
  waiting for transfers between devices  40.1 us (51%)
  starting transfers between devices  21.3 us (27%)
  Pallas kernels  16.2 us (20%)
  between operations  0.84 us (1%)
    ppermute x3, waiting for transfers between devices, onward(): return lax.ppermute(value, 'row', list(zip(ring, ring[1:] + ring[:1])))  21.5 us
    ppermute x6, waiting for transfers between devices, cross(): lax.ppermute(value, 'col', [(i, i ^ masks[i % 2]) for i in range(col_coun...  15 us
    ppermute x3, starting transfers between devices, onward(): return lax.ppermute(value, 'row', list(zip(ring, ring[1:] + ring[:1])))  9.24 us
    ppermute x6, starting transfers between devices, cross(): lax.ppermute(value, 'col', [(i, i ^ masks[i % 2]) for i in range(col_coun...  8.83 us
    pallas_call x1, Pallas kernels, update(): pl.pallas_call(functools.partial(update_kernel, len(near), len(far), tile...  7.42 us
    ppermute x13, waiting for transfers between devices, swap(): return lax.ppermute(value, 'col', [(i, i ^ bit) for i in range(col_count)])  3.59 us
    ppermute x13, starting transfers between devices, swap(): return lax.ppermute(value, 'col', [(i, i ^ bit) for i in range(col_count)])  3.2 us
    pallas_call x1, Pallas kernels, solve(): pl.pallas_call(functools.partial(solve_kernel, steps, block), out_shape=o...  2.86 us
  transfers between devices with their start and end apart: 22, of which 13 were waited for; matrix products, arithmetic and copies ran while one was open for 1% of the time, Pallas kernels for 18%

profile of v7, /device:TPU:0, one launch (start us, length us, event | category | flops | bytes accessed | tf_op | source)
XLA Modules:
  0.0 79.2 jit_solution(14612460383998425759)
XLA Ops:
  0.6 3.0 %collective-permute-start = (f32[64,4096]{1,0:T(8,128)}, f32[64,4096]{1,0:T(8,128)S(1)}, u32[]{:S(2)}, u32[]{:S(2)}) collective-permute-start(f32[64,4096]{1,0:T(8,128)} %bitcast.6), channel_id=1, source_target_pairs={{0,2},{1,5},{2,0},{3,7},{4,6},{5,1},{6,4},{7,3},{8,10},{9,13},{10,... | collective-permute-start | bytes 3145736 | tf_op jit(solution)/shard_map/ppermute | solution.py:302
  3.6 0.0 collective-permute-start.2
  3.6 0.5 collective-permute-start.3
  4.1 2.1 %shard_map.103 = f32[640,256]{1,0:T(8,128)} custom-call(f32[128,512]{1,0:T(8,128)} %refs_0_.3, f32[128,512]{1,0:T(8,128)} %refs_1_.3, f32[128,512]{1,0:T(8,128)} %refs_2_.3, f32[128,256]{1,0:T(8,128)} %refs_3_.3, f32[128,256]{1,0:T(8,128)} %refs_4_.3), custom_call_target="tpu_custom_call" | custom-call | flops 1024 | bytes 1024 | tf_op jit(solution)/shard_map/pallas_call | solution.py:58
  6.2 2.6 %collective-permute-start.4 = (f32[640,256]{1,0:T(8,128)}, f32[640,256]{1,0:T(8,128)S(1)}, u32[]{:S(2)}, u32[]{:S(2)}) collective-permute-start(f32[640,256]{1,0:T(8,128)} %shard_map.103), channel_id=1, source_target_pairs={{0,16},{16,24},{24,8},{8,0},{1,17},{17,25},{25,9},{9,1},{2,18},{18... | collective-permute-start | bytes 1966088 | tf_op jit(solution)/shard_map/ppermute | solution.py:284
  8.8 0.6 collective-permute-start.1
  9.4 7.2 %collective-permute-done.refs_4_ = f32[64,4096]{1,0:T(8,128)S(1)} collective-permute-done((f32[64,4096]{1,0:T(8,128)}, f32[64,4096]{1,0:T(8,128)S(1)}, u32[]{:S(2)}, u32[]{:S(2)}) %collective-permute-start) | collective-permute-done | bytes 1048608 | tf_op jit(solution)/shard_map/ppermute | solution.py:302
  16.6 0.0 collective-permute-start.7
  16.6 6.7 %collective-permute-done.4.refs_5_ = f32[640,256]{1,0:T(8,128)S(1)} collective-permute-done((f32[640,256]{1,0:T(8,128)}, f32[640,256]{1,0:T(8,128)S(1)}, u32[]{:S(2)}, u32[]{:S(2)}) %collective-permute-start.4) | collective-permute-done | bytes 655392 | tf_op jit(solution)/shard_map/ppermute | solution.py:284
  23.3 0.0 collective-permute-done.2.refs_2_
  23.3 0.0 collective-permute-done.3.refs_3_
  23.3 1.5 %collective-permute-start.5 = (f32[64,4096]{1,0:T(8,128)}, f32[64,4096]{1,0:T(8,128)S(1)}, u32[]{:S(2)}, u32[]{:S(2)}) collective-permute-start(f32[64,4096]{1,0:T(8,128)} %bitcast.8), channel_id=1, source_target_pairs={{0,4},{1,3},{2,6},{3,1},{4,0},{5,7},{6,2},{7,5},{8,12},{9,11},{10,... | collective-permute-start | bytes 3145736 | tf_op jit(solution)/shard_map/ppermute | solution.py:302
  24.8 3.3 %collective-permute-start.11 = (f32[640,256]{1,0:T(8,128)S(1)}, f32[640,256]{1,0:T(8,128)S(1)}, u32[]{:S(2)}, u32[]{:S(2)}) collective-permute-start(f32[640,256]{1,0:T(8,128)S(1)} %collective-permute-done.4.refs_5_), channel_id=1, source_target_pairs={{0,16},{16,24},{24,8},{8,0},{1,17},{17,25},{25,9},{9,1},{2,18},{18... | collective-permute-start | bytes 1966088 | tf_op jit(solution)/shard_map/ppermute | solution.py:284
  28.1 0.6 collective-permute-start.6
  28.8 1.6 %collective-permute-done.1.refs_5_ = f32[64,4096]{1,0:T(8,128)S(1)} collective-permute-done((f32[64,4096]{1,0:T(8,128)}, f32[64,4096]{1,0:T(8,128)S(1)}, u32[]{:S(2)}, u32[]{:S(2)}) %collective-permute-start.1) | collective-permute-done | bytes 1048608 | tf_op jit(solution)/shard_map/ppermute | solution.py:302
  30.4 0.1 pad_maximum_fusion.1
  30.5 2.7 %collective-permute-start.18 = (f32[128,2048]{1,0:T(8,128)S(1)}, f32[128,2048]{1,0:T(8,128)S(1)}, u32[]{:S(2)}, u32[]{:S(2)}) collective-permute-start(f32[128,2048]{1,0:T(8,128)S(1)} %pad_maximum_fusion.1), channel_id=1, source_target_pairs={{0,4},{1,3},{2,6},{3,1},{4,0},{5,7},{6,2},{7,5},{8,12},{9,11},{10,... | collective-permute-start | bytes 3145736 | tf_op jit(solution)/shard_map/ppermute | solution.py:302
  33.2 8.0 %collective-permute-done.11.refs_6_ = f32[640,256]{1,0:T(8,128)S(1)} collective-permute-done((f32[640,256]{1,0:T(8,128)S(1)}, f32[640,256]{1,0:T(8,128)S(1)}, u32[]{:S(2)}, u32[]{:S(2)}) %collective-permute-start.11) | collective-permute-done | bytes 655392 | tf_op jit(solution)/shard_map/ppermute | solution.py:284
  41.3 0.0 collective-permute-start.8
  41.3 0.1 pad_maximum_fusion.2
  41.4 0.0 collective-permute-done.7.refs_6_
  41.4 0.6 collective-permute-start.13
  41.9 0.0 collective-permute-done.5.refs_8_
  41.9 3.4 %collective-permute-start.12 = (f32[640,256]{1,0:T(8,128)S(1)}, f32[640,256]{1,0:T(8,128)S(1)}, u32[]{:S(2)}, u32[]{:S(2)}) collective-permute-start(f32[640,256]{1,0:T(8,128)S(1)} %collective-permute-done.11.refs_6_), channel_id=1, source_target_pairs={{0,16},{16,24},{24,8},{8,0},{1,17},{17,25},{25,9},{9,1},{2,18},{18... | collective-permute-start | bytes 1966088 | tf_op jit(solution)/shard_map/ppermute | solution.py:284
  45.3 0.1 fusion.2
  45.4 4.2 %collective-permute-done.6.refs_9_ = f32[64,4096]{1,0:T(8,128)S(1)} collective-permute-done((f32[64,4096]{1,0:T(8,128)}, f32[64,4096]{1,0:T(8,128)S(1)}, u32[]{:S(2)}, u32[]{:S(2)}) %collective-permute-start.6) | collective-permute-done | bytes 1048608 | tf_op jit(solution)/shard_map/ppermute | solution.py:302
  49.6 0.9 %collective-permute-start.10 = (f32[32,4096]{1,0:T(8,128)S(1)}, f32[32,4096]{1,0:T(8,128)S(1)}, u32[]{:S(2)}, u32[]{:S(2)}) collective-permute-start(f32[32,4096]{1,0:T(8,128)S(1)} %get-tuple-element.59), channel_id=1, source_target_pairs={{0,1},{1,0},{2,3},{3,2},{4,5},{5,4},{6,7},{7,6},{8,9},{9,8},{10,11... | collective-permute-start | bytes 1572872 | tf_op jit(solution)/shard_map/ppermute | solution.py:279
  50.4 0.0 collective-permute-done.13.refs_8_
  50.4 0.0 collective-permute-start.9
  50.5 0.0 collective-permute-done.8.refs_7_
  50.5 1.5 %collective-permute-done.10.refs_11_ = f32[32,4096]{1,0:T(8,128)S(1)} collective-permute-done((f32[32,4096]{1,0:T(8,128)S(1)}, f32[32,4096]{1,0:T(8,128)S(1)}, u32[]{:S(2)}, u32[]{:S(2)}) %collective-permute-start.10) | collective-permute-done | bytes 524320 | tf_op jit(solution)/shard_map/ppermute | solution.py:279
  52.0 0.7 collective-permute-done.9.refs_10_
  52.7 6.8 %collective-permute-done.12.refs_7_ = f32[640,256]{1,0:T(8,128)S(1)} collective-permute-done((f32[640,256]{1,0:T(8,128)S(1)}, f32[640,256]{1,0:T(8,128)S(1)}, u32[]{:S(2)}, u32[]{:S(2)}) %collective-permute-start.12) | collective-permute-done | bytes 655392 | tf_op jit(solution)/shard_map/ppermute | solution.py:284
  59.6 0.0 copy-start.3
  59.6 0.0 copy-start.4
  59.6 0.0 copy-start.5
  59.6 0.0 copy-start.6
  59.6 0.0 copy-start.7
  59.6 0.1 collective-permute-start.14
  59.8 0.1 pad_maximum_fusion
  59.9 0.0 copy-start
  59.9 0.0 copy-start.1
  59.9 0.0 copy-start.2
  59.9 0.5 collective-permute-start.15
  60.4 0.4 collective-permute-done.18.refs_14_
  60.8 0.6 collective-permute-done.14.refs_9_
  61.4 0.1 fusion
  61.5 0.2 collective-permute-start.19
  61.7 0.4 collective-permute-start.20
  62.1 0.1 fusion.1
  62.2 0.2 collective-permute-start.16
  62.4 0.4 collective-permute-start.17
  62.8 0.0 copy-done.3
  62.8 2.9 %shard_map.104 = (bf16[768,256]{1,0:T(8,128)(2,1)S(1)}, bf16[768,256]{1,0:T(8,128)(2,1)S(1)}, bf16[256,256]{1,0:T(8,128)(2,1)S(1)}, bf16[256,256]{1,0:T(8,128)(2...) custom-call(f32[128,512]{1,0:T(8,128)S(1)} %copy-done.3, f32[128,512]{1,0:T(8,128)S(1)} %copy-done.4, ...), custom_call_target="tpu_custom_call" | custom-call | flops 1024 | bytes 1024 | tf_op jit(solution)/shard_map/pallas_call | solution.py:133
  65.6 0.0 collective-permute-done.19.refs_15_
  65.6 0.0 collective-permute-done.20.refs_16_
  65.7 0.0 collective-permute-done.16.refs_12_
  65.7 0.1 collective-permute-done.17.refs_13_
  65.8 7.4 %shard_map.105 = (f32[4096,256]{1,0:T(8,128)}, f32[2048,256]{1,0:T(8,128)S(1)}) custom-call(f32[64,4096]{1,0:T(8,128)S(1)} %bitcast.9, f32[64,4096]{1,0:T(8,128)S(1)} %bitcast.5, f32[64,4096]{1,0:T(8,128)S(1)} %collective-permute-done.2.refs_2_, f32[64,4096]{1,0:T(8,128)S(1)} %collective-permute-done.3.refs_3_, f32[64,4096]{1,0:T(8,128)S(1)} %collective-permute-done.refs_4_, ...), custom_call_target="tpu_custom_call" | custom-call | flops 1024 | bytes 1024 | tf_op jit(solution)/shard_map/pallas_call | solution.py:204
  73.2 1.6 %collective-permute-done.15.panel = f32[128,2048]{1,0:T(8,128)S(1)} collective-permute-done((f32[128,2048]{1,0:T(8,128)S(1)}, f32[128,2048]{1,0:T(8,128)S(1)}, u32[]{:S(2)}, u32[]{:S(2)}) %collective-permute-start.15) | collective-permute-done | bytes 1048608 | tf_op jit(solution)/shard_map/ppermute | solution.py:302
  74.8 0.0 collective-permute-start.21
  74.8 2.1 %shard_map.106.rest = f32[2048,256]{1,0:T(8,128)S(1)} custom-call(f32[128,2048]{1,0:T(8,128)S(1)} %collective-permute-done.15.panel, bf16[256,256]{1,0:T(8,128)(2,1)S(1)} %get-tuple-element.50.refs_19_.high, bf16[256,256]{1,0:T(8,128)(2,1)S(1)} %get-tuple-element.51.refs_20_.low, ...), custom_call_target="tpu_custom_call", output_to_operand_aliasing={{}: (3, {})} | custom-call | flops 1024 | bytes 1024 | tf_op jit(solution)/shard_map/pallas_call | solution.py:232
  76.9 0.6 collective-permute-done.21.panel
  77.5 1.7 %shard_map.107 = f32[4096,256]{1,0:T(8,128)} custom-call(f32[128,2048]{1,0:T(8,128)S(1)} %collective-permute-done.21.panel, bf16[256,256]{1,0:T(8,128)(2,1)S(1)} %get-tuple-element.50.refs_19_.high, bf16[256,256]{1,0:T(8,128)(2,1)S(1)} %get-tuple-element.51.refs_20_.low, f32[2048,256]{1,0:T(8,128)S(1)} %shard_map.106.rest, ...), custom_call_target="tpu_custom_call", output_to_operand_aliasing={{}: (4, {})} | custom-call | flops 1024 | bytes 1024 | tf_op jit(solution)/shard_map/pallas_call | solution.py:263
  (14 shorter events, 0.2 us)
Async XLA Ops:
  0.6 16.0 %collective-permute-start = (f32[64,4096]{1,0:T(8,128)}, f32[64,4096]{1,0:T(8,128)S(1)}, u32[]{:S(2)}, u32[]{:S(2)}) collective-permute-start(f32[64,4096]{1,0:T(8,128)} %bitcast.6), channel_id=1, source_target_pairs={{0,2},{1,5},{2,0},{3,7},{4,6},{5,1},{6,4},{7,3},{8,10},{9,13},{10,... | collective-permute-start | bytes 3145736 | tf_op jit(solution)/shard_map/ppermute | solution.py:302
  3.6 19.7 %collective-permute-start.2 = (f32[64,4096]{1,0:T(8,128)}, f32[64,4096]{1,0:T(8,128)S(1)}, u32[]{:S(2)}, u32[]{:S(2)}) collective-permute-start(f32[64,4096]{1,0:T(8,128)} %bitcast.7), channel_id=1, source_target_pairs={{0,1},{1,0},{2,3},{3,2},{4,5},{5,4},{6,7},{7,6},{8,9},{9,8},{10,11... | collective-permute-start | bytes 3145736 | tf_op jit(solution)/shard_map/ppermute | solution.py:279
  3.6 19.7 %collective-permute-start.3 = (f32[64,4096]{1,0:T(8,128)}, f32[64,4096]{1,0:T(8,128)S(1)}, u32[]{:S(2)}, u32[]{:S(2)}) collective-permute-start(f32[64,4096]{1,0:T(8,128)} %bitcast.2), channel_id=1, source_target_pairs={{0,1},{1,0},{2,3},{3,2},{4,5},{5,4},{6,7},{7,6},{8,9},{9,8},{10,11... | collective-permute-start | bytes 3145736 | tf_op jit(solution)/shard_map/ppermute | solution.py:279
  6.2 17.1 %collective-permute-start.4 = (f32[640,256]{1,0:T(8,128)}, f32[640,256]{1,0:T(8,128)S(1)}, u32[]{:S(2)}, u32[]{:S(2)}) collective-permute-start(f32[640,256]{1,0:T(8,128)} %shard_map.103), channel_id=1, source_target_pairs={{0,16},{16,24},{24,8},{8,0},{1,17},{17,25},{25,9},{9,1},{2,18},{18... | collective-permute-start | bytes 1966088 | tf_op jit(solution)/shard_map/ppermute | solution.py:284
  8.8 21.6 %collective-permute-start.1 = (f32[64,4096]{1,0:T(8,128)}, f32[64,4096]{1,0:T(8,128)S(1)}, u32[]{:S(2)}, u32[]{:S(2)}) collective-permute-start(f32[64,4096]{1,0:T(8,128)} %bitcast.3), channel_id=1, source_target_pairs={{0,2},{1,5},{2,0},{3,7},{4,6},{5,1},{6,4},{7,3},{8,10},{9,13},{10,... | collective-permute-start | bytes 3145736 | tf_op jit(solution)/shard_map/ppermute | solution.py:302
  16.6 24.7 %collective-permute-start.7 = (f32[64,4096]{1,0:T(8,128)S(1)}, f32[64,4096]{1,0:T(8,128)S(1)}, u32[]{:S(2)}, u32[]{:S(2)}) collective-permute-start(f32[64,4096]{1,0:T(8,128)S(1)} %collective-permute-done.refs_4_), channel_id=1, source_target_pairs={{0,1},{1,0},{2,3},{3,2},{4,5},{5,4},{6,7},{7,6},{8,9},{9,8},{10,11... | collective-permute-start | bytes 3145736 | tf_op jit(solution)/shard_map/ppermute | solution.py:279
  23.3 18.6 %collective-permute-start.5 = (f32[64,4096]{1,0:T(8,128)}, f32[64,4096]{1,0:T(8,128)S(1)}, u32[]{:S(2)}, u32[]{:S(2)}) collective-permute-start(f32[64,4096]{1,0:T(8,128)} %bitcast.8), channel_id=1, source_target_pairs={{0,4},{1,3},{2,6},{3,1},{4,0},{5,7},{6,2},{7,5},{8,12},{9,11},{10,... | collective-permute-start | bytes 3145736 | tf_op jit(solution)/shard_map/ppermute | solution.py:302
  24.8 16.4 %collective-permute-start.11 = (f32[640,256]{1,0:T(8,128)S(1)}, f32[640,256]{1,0:T(8,128)S(1)}, u32[]{:S(2)}, u32[]{:S(2)}) collective-permute-start(f32[640,256]{1,0:T(8,128)S(1)} %collective-permute-done.4.refs_5_), channel_id=1, source_target_pairs={{0,16},{16,24},{24,8},{8,0},{1,17},{17,25},{25,9},{9,1},{2,18},{18... | collective-permute-start | bytes 1966088 | tf_op jit(solution)/shard_map/ppermute | solution.py:284
  28.1 21.4 %collective-permute-start.6 = (f32[64,4096]{1,0:T(8,128)}, f32[64,4096]{1,0:T(8,128)S(1)}, u32[]{:S(2)}, u32[]{:S(2)}) collective-permute-start(f32[64,4096]{1,0:T(8,128)} %bitcast.4), channel_id=1, source_target_pairs={{0,4},{1,3},{2,6},{3,1},{4,0},{5,7},{6,2},{7,5},{8,12},{9,11},{10,... | collective-permute-start | bytes 3145736 | tf_op jit(solution)/shard_map/ppermute | solution.py:302
  30.5 30.3 %collective-permute-start.18 = (f32[128,2048]{1,0:T(8,128)S(1)}, f32[128,2048]{1,0:T(8,128)S(1)}, u32[]{:S(2)}, u32[]{:S(2)}) collective-permute-start(f32[128,2048]{1,0:T(8,128)S(1)} %pad_maximum_fusion.1), channel_id=1, source_target_pairs={{0,4},{1,3},{2,6},{3,1},{4,0},{5,7},{6,2},{7,5},{8,12},{9,11},{10,... | collective-permute-start | bytes 3145736 | tf_op jit(solution)/shard_map/ppermute | solution.py:302
  41.3 9.2 %collective-permute-start.8 = (f32[64,4096]{1,0:T(8,128)S(1)}, f32[64,4096]{1,0:T(8,128)S(1)}, u32[]{:S(2)}, u32[]{:S(2)}) collective-permute-start(f32[64,4096]{1,0:T(8,128)S(1)} %collective-permute-done.1.refs_5_), channel_id=1, source_target_pairs={{0,1},{1,0},{2,3},{3,2},{4,5},{5,4},{6,7},{7,6},{8,9},{9,8},{10,11... | collective-permute-start | bytes 3145736 | tf_op jit(solution)/shard_map/ppermute | solution.py:279
  41.4 9.1 %collective-permute-start.13 = (f32[768,256]{1,0:T(8,128)S(1)}, f32[768,256]{1,0:T(8,128)S(1)}, u32[]{:S(2)}, u32[]{:S(2)}) collective-permute-start(f32[768,256]{1,0:T(8,128)S(1)} %pad_maximum_fusion.2), channel_id=1, source_target_pairs={{0,1},{1,0},{2,3},{3,2},{4,5},{5,4},{6,7},{7,6},{8,9},{9,8},{10,11... | collective-permute-start | bytes 2359304 | tf_op jit(solution)/shard_map/ppermute | solution.py:279
  41.9 17.6 %collective-permute-start.12 = (f32[640,256]{1,0:T(8,128)S(1)}, f32[640,256]{1,0:T(8,128)S(1)}, u32[]{:S(2)}, u32[]{:S(2)}) collective-permute-start(f32[640,256]{1,0:T(8,128)S(1)} %collective-permute-done.11.refs_6_), channel_id=1, source_target_pairs={{0,16},{16,24},{24,8},{8,0},{1,17},{17,25},{25,9},{9,1},{2,18},{18... | collective-permute-start | bytes 1966088 | tf_op jit(solution)/shard_map/ppermute | solution.py:284
  49.6 2.4 %collective-permute-start.10 = (f32[32,4096]{1,0:T(8,128)S(1)}, f32[32,4096]{1,0:T(8,128)S(1)}, u32[]{:S(2)}, u32[]{:S(2)}) collective-permute-start(f32[32,4096]{1,0:T(8,128)S(1)} %get-tuple-element.59), channel_id=1, source_target_pairs={{0,1},{1,0},{2,3},{3,2},{4,5},{5,4},{6,7},{7,6},{8,9},{9,8},{10,11... | collective-permute-start | bytes 1572872 | tf_op jit(solution)/shard_map/ppermute | solution.py:279
  50.4 2.3 %collective-permute-start.9 = (f32[32,4096]{1,0:T(8,128)S(1)}, f32[32,4096]{1,0:T(8,128)S(1)}, u32[]{:S(2)}, u32[]{:S(2)}) collective-permute-start(f32[32,4096]{1,0:T(8,128)S(1)} %get-tuple-element.60), channel_id=1, source_target_pairs={{0,1},{1,0},{2,3},{3,2},{4,5},{5,4},{6,7},{7,6},{8,9},{9,8},{10,11... | collective-permute-start | bytes 1572872 | tf_op jit(solution)/shard_map/ppermute | solution.py:279
  59.6 3.2 %copy-start.3 = (f32[128,512]{1,0:T(8,128)S(1)}, f32[128,512]{1,0:T(8,128)}, u32[]{:S(2)}) copy-start(f32[128,512]{1,0:T(8,128)} %refs_0_.3) | copy-start | bytes 786436
  59.6 3.2 %copy-start.4 = (f32[128,512]{1,0:T(8,128)S(1)}, f32[128,512]{1,0:T(8,128)}, u32[]{:S(2)}) copy-start(f32[128,512]{1,0:T(8,128)} %refs_1_.3) | copy-start | bytes 786436
  59.6 3.2 %copy-start.5 = (f32[128,512]{1,0:T(8,128)S(1)}, f32[128,512]{1,0:T(8,128)}, u32[]{:S(2)}) copy-start(f32[128,512]{1,0:T(8,128)} %refs_2_.3) | copy-start | bytes 786436
  59.6 3.1 %copy-start.6 = (f32[128,256]{1,0:T(8,128)S(1)}, f32[128,256]{1,0:T(8,128)}, u32[]{:S(2)}) copy-start(f32[128,256]{1,0:T(8,128)} %refs_3_.3) | copy-start | bytes 393220
  59.6 3.1 %copy-start.7 = (f32[128,256]{1,0:T(8,128)S(1)}, f32[128,256]{1,0:T(8,128)}, u32[]{:S(2)}) copy-start(f32[128,256]{1,0:T(8,128)} %refs_4_.3) | copy-start | bytes 393220
  59.6 1.8 %collective-permute-start.14 = (f32[384,256]{1,0:T(8,128)S(1)}, f32[384,256]{1,0:T(8,128)S(1)}, u32[]{:S(2)}, u32[]{:S(2)}) collective-permute-start(f32[384,256]{1,0:T(8,128)S(1)} %slice.23), channel_id=1, source_target_pairs={{0,1},{1,0},{2,3},{3,2},{4,5},{5,4},{6,7},{7,6},{8,9},{9,8},{10,11... | collective-permute-start | bytes 1179656 | tf_op jit(solution)/shard_map/ppermute | solution.py:279
  59.9 5.8 %copy-start = (f32[4096,256]{1,0:T(8,128)S(1)}, f32[4096,256]{1,0:T(8,128)}, u32[]{:S(2)}) copy-start(f32[4096,256]{1,0:T(8,128)} %refs_21_.1) | copy-start | bytes 12582916
  59.9 5.8 %copy-start.1 = (f32[4096,64]{0,1:T(8,128)S(1)}, f32[4096,64]{0,1:T(8,128)}, u32[]{:S(2)}) copy-start(f32[4096,64]{0,1:T(8,128)} %param.12) | copy-start | bytes 3145732
  59.9 5.8 %copy-start.2 = (f32[4096,64]{0,1:T(8,128)S(1)}, f32[4096,64]{0,1:T(8,128)}, u32[]{:S(2)}) copy-start(f32[4096,64]{0,1:T(8,128)} %param.11) | copy-start | bytes 3145732
  59.9 14.9 %collective-permute-start.15 = (f32[128,2048]{1,0:T(8,128)S(1)}, f32[128,2048]{1,0:T(8,128)S(1)}, u32[]{:S(2)}, u32[]{:S(2)}) collective-permute-start(f32[128,2048]{1,0:T(8,128)S(1)} %pad_maximum_fusion), channel_id=1, source_target_pairs={{0,4},{1,3},{2,6},{3,1},{4,0},{5,7},{6,2},{7,5},{8,12},{9,11},{10,... | collective-permute-start | bytes 3145736 | tf_op jit(solution)/shard_map/ppermute | solution.py:302
  61.5 4.1 %collective-permute-start.19 = (f32[64,2048]{1,0:T(8,128)S(1)}, f32[64,2048]{1,0:T(8,128)S(1)}, u32[]{:S(2)}, u32[]{:S(2)}) collective-permute-start(f32[64,2048]{1,0:T(8,128)S(1)} %get-tuple-element.56), channel_id=1, source_target_pairs={{0,1},{1,0},{2,3},{3,2},{4,5},{5,4},{6,7},{7,6},{8,9},{9,8},{10,11... | collective-permute-start | bytes 1572872 | tf_op jit(solution)/shard_map/ppermute | solution.py:279
  61.7 3.9 %collective-permute-start.20 = (f32[64,2048]{1,0:T(8,128)S(1)}, f32[64,2048]{1,0:T(8,128)S(1)}, u32[]{:S(2)}, u32[]{:S(2)}) collective-permute-start(f32[64,2048]{1,0:T(8,128)S(1)} %get-tuple-element.55), channel_id=1, source_target_pairs={{0,1},{1,0},{2,3},{3,2},{4,5},{5,4},{6,7},{7,6},{8,9},{9,8},{10,11... | collective-permute-start | bytes 1572872 | tf_op jit(solution)/shard_map/ppermute | solution.py:279
  62.2 3.5 %collective-permute-start.16 = (f32[32,4096]{1,0:T(8,128)S(1)}, f32[32,4096]{1,0:T(8,128)S(1)}, u32[]{:S(2)}, u32[]{:S(2)}) collective-permute-start(f32[32,4096]{1,0:T(8,128)S(1)} %get-tuple-element.58), channel_id=1, source_target_pairs={{0,1},{1,0},{2,3},{3,2},{4,5},{5,4},{6,7},{7,6},{8,9},{9,8},{10,11... | collective-permute-start | bytes 1572872 | tf_op jit(solution)/shard_map/ppermute | solution.py:279
  62.4 3.4 %collective-permute-start.17 = (f32[32,4096]{1,0:T(8,128)S(1)}, f32[32,4096]{1,0:T(8,128)S(1)}, u32[]{:S(2)}, u32[]{:S(2)}) collective-permute-start(f32[32,4096]{1,0:T(8,128)S(1)} %get-tuple-element.57), channel_id=1, source_target_pairs={{0,1},{1,0},{2,3},{3,2},{4,5},{5,4},{6,7},{7,6},{8,9},{9,8},{10,11... | collective-permute-start | bytes 1572872 | tf_op jit(solution)/shard_map/ppermute | solution.py:279
  74.8 2.7 %collective-permute-start.21 = (f32[128,2048]{1,0:T(8,128)S(1)}, f32[128,2048]{1,0:T(8,128)S(1)}, u32[]{:S(2)}, u32[]{:S(2)}) collective-permute-start(f32[128,2048]{1,0:T(8,128)S(1)} %collective-permute-done.15.panel), channel_id=1, source_target_pairs={{0,1},{1,0},{2,3},{3,2},{4,5},{5,4},{6,7},{7,6},{8,9},{9,8},{10,11... | collective-permute-start | bytes 3145736 | tf_op jit(solution)/shard_map/ppermute | solution.py:279

commit v8 on v7

--- a/solution.py
+++ b/solution.py
@@ -230,7 +230,7 @@
 def subtract(panel, factor, before):
     inside = pl.BlockSpec(memory_space=pltpu.VMEM)
     return pl.pallas_call(
-        functools.partial(subtract_kernel, min(LAST_TILE, before.shape[0])),
+        functools.partial(subtract_kernel, min(UPDATE_TILE, before.shape[0])),
         out_shape=jax.ShapeDtypeStruct(before.shape, jnp.float32),
         in_specs=[inside] * 4,
         out_specs=inside,

time: 79.3 us -> 79.3 us (level)
  waiting for transfers between devices: 40.1 us -> 41.2 us
  Pallas kernels: 16.2 us -> 15.2 us
    pallas_call x1, Pallas kernels: 2.1 us -> 1.06 us  [subtract(): pl.pallas_call(functools.partial(subtract_kernel, min(UPDATE_TILE, before...]
    ppermute x13, waiting for transfers between devices: 3.59 us -> 4.62 us  [swap(): return lax.ppermute(value, 'col', [(i, i ^ bit) for i in range(col_count)])]
  transfers between devices with their start and end apart: 22 -> 22, of which waited for: 13 -> 13; matrix products, arithmetic and copies ran while one was open for 1% -> 1% of each run, Pallas kernels for 18% -> 17%
where the time goes in v8:
time: 79.3 us; the launch traced here: 79.2 us
  waiting for transfers between devices  41.2 us (52%)
  starting transfers between devices  21.3 us (27%)
  Pallas kernels  15.2 us (19%)
  between operations  0.84 us (1%)
    ppermute x3, waiting for transfers between devices, onward(): return lax.ppermute(value, 'row', list(zip(ring, ring[1:] + ring[:1])))  21.5 us
    ppermute x6, waiting for transfers between devices, cross(): lax.ppermute(value, 'col', [(i, i ^ masks[i % 2]) for i in range(col_coun...  15 us
    ppermute x3, starting transfers between devices, onward(): return lax.ppermute(value, 'row', list(zip(ring, ring[1:] + ring[:1])))  9.24 us
    ppermute x6, starting transfers between devices, cross(): lax.ppermute(value, 'col', [(i, i ^ masks[i % 2]) for i in range(col_coun...  8.83 us
    pallas_call x1, Pallas kernels, update(): pl.pallas_call(functools.partial(update_kernel, len(near), len(far), tile...  7.42 us
    ppermute x13, waiting for transfers between devices, swap(): return lax.ppermute(value, 'col', [(i, i ^ bit) for i in range(col_count)])  4.62 us
    ppermute x13, starting transfers between devices, swap(): return lax.ppermute(value, 'col', [(i, i ^ bit) for i in range(col_count)])  3.2 us
    pallas_call x1, Pallas kernels, solve(): pl.pallas_call(functools.partial(solve_kernel, steps, block), out_shape=o...  2.86 us
  transfers between devices with their start and end apart: 22, of which 13 were waited for; matrix products, arithmetic and copies ran while one was open for 1% of the time, Pallas kernels for 17%

profile of v8, /device:TPU:0, one launch (start us, length us, event | category | flops | bytes accessed | tf_op | source)
XLA Modules:
  0.0 79.2 jit_solution(250746441955899997)
XLA Ops:
  0.6 3.0 %collective-permute-start = (f32[64,4096]{1,0:T(8,128)}, f32[64,4096]{1,0:T(8,128)S(1)}, u32[]{:S(2)}, u32[]{:S(2)}) collective-permute-start(f32[64,4096]{1,0:T(8,128)} %bitcast.6), channel_id=1, source_target_pairs={{0,2},{1,5},{2,0},{3,7},{4,6},{5,1},{6,4},{7,3},{8,10},{9,13},{10,... | collective-permute-start | bytes 3145736 | tf_op jit(solution)/shard_map/ppermute | solution.py:302
  3.6 0.0 collective-permute-start.2
  3.6 0.5 collective-permute-start.3
  4.1 2.1 %shard_map.103 = f32[640,256]{1,0:T(8,128)} custom-call(f32[128,512]{1,0:T(8,128)} %refs_0_.3, f32[128,512]{1,0:T(8,128)} %refs_1_.3, f32[128,512]{1,0:T(8,128)} %refs_2_.3, f32[128,256]{1,0:T(8,128)} %refs_3_.3, f32[128,256]{1,0:T(8,128)} %refs_4_.3), custom_call_target="tpu_custom_call" | custom-call | flops 1024 | bytes 1024 | tf_op jit(solution)/shard_map/pallas_call | solution.py:58
  6.2 2.6 %collective-permute-start.4 = (f32[640,256]{1,0:T(8,128)}, f32[640,256]{1,0:T(8,128)S(1)}, u32[]{:S(2)}, u32[]{:S(2)}) collective-permute-start(f32[640,256]{1,0:T(8,128)} %shard_map.103), channel_id=1, source_target_pairs={{0,16},{16,24},{24,8},{8,0},{1,17},{17,25},{25,9},{9,1},{2,18},{18... | collective-permute-start | bytes 1966088 | tf_op jit(solution)/shard_map/ppermute | solution.py:284
  8.8 0.6 collective-permute-start.1
  9.4 7.2 %collective-permute-done.refs_4_ = f32[64,4096]{1,0:T(8,128)S(1)} collective-permute-done((f32[64,4096]{1,0:T(8,128)}, f32[64,4096]{1,0:T(8,128)S(1)}, u32[]{:S(2)}, u32[]{:S(2)}) %collective-permute-start) | collective-permute-done | bytes 1048608 | tf_op jit(solution)/shard_map/ppermute | solution.py:302
  16.6 0.0 collective-permute-start.7
  16.6 6.7 %collective-permute-done.4.refs_5_ = f32[640,256]{1,0:T(8,128)S(1)} collective-permute-done((f32[640,256]{1,0:T(8,128)}, f32[640,256]{1,0:T(8,128)S(1)}, u32[]{:S(2)}, u32[]{:S(2)}) %collective-permute-start.4) | collective-permute-done | bytes 655392 | tf_op jit(solution)/shard_map/ppermute | solution.py:284
  23.3 0.0 collective-permute-done.2.refs_2_
  23.3 0.0 collective-permute-done.3.refs_3_
  23.3 1.5 %collective-permute-start.5 = (f32[64,4096]{1,0:T(8,128)}, f32[64,4096]{1,0:T(8,128)S(1)}, u32[]{:S(2)}, u32[]{:S(2)}) collective-permute-start(f32[64,4096]{1,0:T(8,128)} %bitcast.8), channel_id=1, source_target_pairs={{0,4},{1,3},{2,6},{3,1},{4,0},{5,7},{6,2},{7,5},{8,12},{9,11},{10,... | collective-permute-start | bytes 3145736 | tf_op jit(solution)/shard_map/ppermute | solution.py:302
  24.8 3.3 %collective-permute-start.11 = (f32[640,256]{1,0:T(8,128)S(1)}, f32[640,256]{1,0:T(8,128)S(1)}, u32[]{:S(2)}, u32[]{:S(2)}) collective-permute-start(f32[640,256]{1,0:T(8,128)S(1)} %collective-permute-done.4.refs_5_), channel_id=1, source_target_pairs={{0,16},{16,24},{24,8},{8,0},{1,17},{17,25},{25,9},{9,1},{2,18},{18... | collective-permute-start | bytes 1966088 | tf_op jit(solution)/shard_map/ppermute | solution.py:284
  28.1 0.6 collective-permute-start.6
  28.8 1.6 %collective-permute-done.1.refs_5_ = f32[64,4096]{1,0:T(8,128)S(1)} collective-permute-done((f32[64,4096]{1,0:T(8,128)}, f32[64,4096]{1,0:T(8,128)S(1)}, u32[]{:S(2)}, u32[]{:S(2)}) %collective-permute-start.1) | collective-permute-done | bytes 1048608 | tf_op jit(solution)/shard_map/ppermute | solution.py:302
  30.4 0.1 pad_maximum_fusion.1
  30.5 2.7 %collective-permute-start.18 = (f32[128,2048]{1,0:T(8,128)S(1)}, f32[128,2048]{1,0:T(8,128)S(1)}, u32[]{:S(2)}, u32[]{:S(2)}) collective-permute-start(f32[128,2048]{1,0:T(8,128)S(1)} %pad_maximum_fusion.1), channel_id=1, source_target_pairs={{0,4},{1,3},{2,6},{3,1},{4,0},{5,7},{6,2},{7,5},{8,12},{9,11},{10,... | collective-permute-start | bytes 3145736 | tf_op jit(solution)/shard_map/ppermute | solution.py:302
  33.2 8.0 %collective-permute-done.11.refs_6_ = f32[640,256]{1,0:T(8,128)S(1)} collective-permute-done((f32[640,256]{1,0:T(8,128)S(1)}, f32[640,256]{1,0:T(8,128)S(1)}, u32[]{:S(2)}, u32[]{:S(2)}) %collective-permute-start.11) | collective-permute-done | bytes 655392 | tf_op jit(solution)/shard_map/ppermute | solution.py:284
  41.3 0.0 collective-permute-start.8
  41.3 0.1 pad_maximum_fusion.2
  41.4 0.0 collective-permute-done.7.refs_6_
  41.4 0.6 collective-permute-start.13
  41.9 0.0 collective-permute-done.5.refs_8_
  41.9 3.4 %collective-permute-start.12 = (f32[640,256]{1,0:T(8,128)S(1)}, f32[640,256]{1,0:T(8,128)S(1)}, u32[]{:S(2)}, u32[]{:S(2)}) collective-permute-start(f32[640,256]{1,0:T(8,128)S(1)} %collective-permute-done.11.refs_6_), channel_id=1, source_target_pairs={{0,16},{16,24},{24,8},{8,0},{1,17},{17,25},{25,9},{9,1},{2,18},{18... | collective-permute-start | bytes 1966088 | tf_op jit(solution)/shard_map/ppermute | solution.py:284
  45.3 0.1 fusion.2
  45.4 4.2 %collective-permute-done.6.refs_9_ = f32[64,4096]{1,0:T(8,128)S(1)} collective-permute-done((f32[64,4096]{1,0:T(8,128)}, f32[64,4096]{1,0:T(8,128)S(1)}, u32[]{:S(2)}, u32[]{:S(2)}) %collective-permute-start.6) | collective-permute-done | bytes 1048608 | tf_op jit(solution)/shard_map/ppermute | solution.py:302
  49.6 0.9 %collective-permute-start.10 = (f32[32,4096]{1,0:T(8,128)S(1)}, f32[32,4096]{1,0:T(8,128)S(1)}, u32[]{:S(2)}, u32[]{:S(2)}) collective-permute-start(f32[32,4096]{1,0:T(8,128)S(1)} %get-tuple-element.59), channel_id=1, source_target_pairs={{0,1},{1,0},{2,3},{3,2},{4,5},{5,4},{6,7},{7,6},{8,9},{9,8},{10,11... | collective-permute-start | bytes 1572872 | tf_op jit(solution)/shard_map/ppermute | solution.py:279
  50.4 0.0 collective-permute-done.13.refs_8_
  50.4 0.0 collective-permute-start.9
  50.5 0.0 collective-permute-done.8.refs_7_
  50.5 1.5 %collective-permute-done.10.refs_11_ = f32[32,4096]{1,0:T(8,128)S(1)} collective-permute-done((f32[32,4096]{1,0:T(8,128)S(1)}, f32[32,4096]{1,0:T(8,128)S(1)}, u32[]{:S(2)}, u32[]{:S(2)}) %collective-permute-start.10) | collective-permute-done | bytes 524320 | tf_op jit(solution)/shard_map/ppermute | solution.py:279
  52.0 0.7 collective-permute-done.9.refs_10_
  52.7 6.8 %collective-permute-done.12.refs_7_ = f32[640,256]{1,0:T(8,128)S(1)} collective-permute-done((f32[640,256]{1,0:T(8,128)S(1)}, f32[640,256]{1,0:T(8,128)S(1)}, u32[]{:S(2)}, u32[]{:S(2)}) %collective-permute-start.12) | collective-permute-done | bytes 655392 | tf_op jit(solution)/shard_map/ppermute | solution.py:284
  59.6 0.0 copy-start.3
  59.6 0.0 copy-start.4
  59.6 0.0 copy-start.5
  59.6 0.0 copy-start.6
  59.6 0.0 copy-start.7
  59.6 0.1 collective-permute-start.14
  59.8 0.1 pad_maximum_fusion
  59.9 0.0 copy-start
  59.9 0.0 copy-start.1
  59.9 0.0 copy-start.2
  59.9 0.5 collective-permute-start.15
  60.4 0.4 collective-permute-done.18.refs_14_
  60.8 0.6 collective-permute-done.14.refs_9_
  61.4 0.1 fusion
  61.5 0.2 collective-permute-start.19
  61.7 0.4 collective-permute-start.20
  62.1 0.1 fusion.1
  62.2 0.2 collective-permute-start.16
  62.4 0.4 collective-permute-start.17
  62.8 0.0 copy-done.3
  62.8 2.9 %shard_map.104 = (bf16[768,256]{1,0:T(8,128)(2,1)S(1)}, bf16[768,256]{1,0:T(8,128)(2,1)S(1)}, bf16[256,256]{1,0:T(8,128)(2,1)S(1)}, bf16[256,256]{1,0:T(8,128)(2...) custom-call(f32[128,512]{1,0:T(8,128)S(1)} %copy-done.3, f32[128,512]{1,0:T(8,128)S(1)} %copy-done.4, ...), custom_call_target="tpu_custom_call" | custom-call | flops 1024 | bytes 1024 | tf_op jit(solution)/shard_map/pallas_call | solution.py:133
  65.6 0.0 collective-permute-done.19.refs_15_
  65.6 0.0 collective-permute-done.20.refs_16_
  65.7 0.0 collective-permute-done.16.refs_12_
  65.7 0.1 collective-permute-done.17.refs_13_
  65.8 7.4 %shard_map.105 = (f32[4096,256]{1,0:T(8,128)}, f32[2048,256]{1,0:T(8,128)S(1)}) custom-call(f32[64,4096]{1,0:T(8,128)S(1)} %bitcast.9, f32[64,4096]{1,0:T(8,128)S(1)} %bitcast.5, f32[64,4096]{1,0:T(8,128)S(1)} %collective-permute-done.2.refs_2_, f32[64,4096]{1,0:T(8,128)S(1)} %collective-permute-done.3.refs_3_, f32[64,4096]{1,0:T(8,128)S(1)} %collective-permute-done.refs_4_, ...), custom_call_target="tpu_custom_call" | custom-call | flops 1024 | bytes 1024 | tf_op jit(solution)/shard_map/pallas_call | solution.py:204
  73.2 1.6 %collective-permute-done.15.panel = f32[128,2048]{1,0:T(8,128)S(1)} collective-permute-done((f32[128,2048]{1,0:T(8,128)S(1)}, f32[128,2048]{1,0:T(8,128)S(1)}, u32[]{:S(2)}, u32[]{:S(2)}) %collective-permute-start.15) | collective-permute-done | bytes 1048608 | tf_op jit(solution)/shard_map/ppermute | solution.py:302
  74.8 0.0 collective-permute-start.21
  74.8 1.1 %shard_map.106.rest = f32[2048,256]{1,0:T(8,128)S(1)} custom-call(f32[128,2048]{1,0:T(8,128)S(1)} %collective-permute-done.15.panel, bf16[256,256]{1,0:T(8,128)(2,1)S(1)} %get-tuple-element.50.refs_19_.high, bf16[256,256]{1,0:T(8,128)(2,1)S(1)} %get-tuple-element.51.refs_20_.low, ...), custom_call_target="tpu_custom_call", output_to_operand_aliasing={{}: (3, {})} | custom-call | flops 1024 | bytes 1024 | tf_op jit(solution)/shard_map/pallas_call | solution.py:232
  75.9 1.6 %collective-permute-done.21.panel = f32[128,2048]{1,0:T(8,128)S(1)} collective-permute-done((f32[128,2048]{1,0:T(8,128)S(1)}, f32[128,2048]{1,0:T(8,128)S(1)}, u32[]{:S(2)}, u32[]{:S(2)}) %collective-permute-start.21) | collective-permute-done | bytes 1048608 | tf_op jit(solution)/shard_map/ppermute | solution.py:279
  77.5 1.7 %shard_map.107 = f32[4096,256]{1,0:T(8,128)} custom-call(f32[128,2048]{1,0:T(8,128)S(1)} %collective-permute-done.21.panel, bf16[256,256]{1,0:T(8,128)(2,1)S(1)} %get-tuple-element.50.refs_19_.high, bf16[256,256]{1,0:T(8,128)(2,1)S(1)} %get-tuple-element.51.refs_20_.low, f32[2048,256]{1,0:T(8,128)S(1)} %shard_map.106.rest, ...), custom_call_target="tpu_custom_call", output_to_operand_aliasing={{}: (4, {})} | custom-call | flops 1024 | bytes 1024 | tf_op jit(solution)/shard_map/pallas_call | solution.py:263
  (14 shorter events, 0.2 us)
Async XLA Ops:
  0.6 16.0 %collective-permute-start = (f32[64,4096]{1,0:T(8,128)}, f32[64,4096]{1,0:T(8,128)S(1)}, u32[]{:S(2)}, u32[]{:S(2)}) collective-permute-start(f32[64,4096]{1,0:T(8,128)} %bitcast.6), channel_id=1, source_target_pairs={{0,2},{1,5},{2,0},{3,7},{4,6},{5,1},{6,4},{7,3},{8,10},{9,13},{10,... | collective-permute-start | bytes 3145736 | tf_op jit(solution)/shard_map/ppermute | solution.py:302
  3.6 19.7 %collective-permute-start.2 = (f32[64,4096]{1,0:T(8,128)}, f32[64,4096]{1,0:T(8,128)S(1)}, u32[]{:S(2)}, u32[]{:S(2)}) collective-permute-start(f32[64,4096]{1,0:T(8,128)} %bitcast.7), channel_id=1, source_target_pairs={{0,1},{1,0},{2,3},{3,2},{4,5},{5,4},{6,7},{7,6},{8,9},{9,8},{10,11... | collective-permute-start | bytes 3145736 | tf_op jit(solution)/shard_map/ppermute | solution.py:279
  3.6 19.7 %collective-permute-start.3 = (f32[64,4096]{1,0:T(8,128)}, f32[64,4096]{1,0:T(8,128)S(1)}, u32[]{:S(2)}, u32[]{:S(2)}) collective-permute-start(f32[64,4096]{1,0:T(8,128)} %bitcast.2), channel_id=1, source_target_pairs={{0,1},{1,0},{2,3},{3,2},{4,5},{5,4},{6,7},{7,6},{8,9},{9,8},{10,11... | collective-permute-start | bytes 3145736 | tf_op jit(solution)/shard_map/ppermute | solution.py:279
  6.2 17.1 %collective-permute-start.4 = (f32[640,256]{1,0:T(8,128)}, f32[640,256]{1,0:T(8,128)S(1)}, u32[]{:S(2)}, u32[]{:S(2)}) collective-permute-start(f32[640,256]{1,0:T(8,128)} %shard_map.103), channel_id=1, source_target_pairs={{0,16},{16,24},{24,8},{8,0},{1,17},{17,25},{25,9},{9,1},{2,18},{18... | collective-permute-start | bytes 1966088 | tf_op jit(solution)/shard_map/ppermute | solution.py:284
  8.8 21.6 %collective-permute-start.1 = (f32[64,4096]{1,0:T(8,128)}, f32[64,4096]{1,0:T(8,128)S(1)}, u32[]{:S(2)}, u32[]{:S(2)}) collective-permute-start(f32[64,4096]{1,0:T(8,128)} %bitcast.3), channel_id=1, source_target_pairs={{0,2},{1,5},{2,0},{3,7},{4,6},{5,1},{6,4},{7,3},{8,10},{9,13},{10,... | collective-permute-start | bytes 3145736 | tf_op jit(solution)/shard_map/ppermute | solution.py:302
  16.6 24.7 %collective-permute-start.7 = (f32[64,4096]{1,0:T(8,128)S(1)}, f32[64,4096]{1,0:T(8,128)S(1)}, u32[]{:S(2)}, u32[]{:S(2)}) collective-permute-start(f32[64,4096]{1,0:T(8,128)S(1)} %collective-permute-done.refs_4_), channel_id=1, source_target_pairs={{0,1},{1,0},{2,3},{3,2},{4,5},{5,4},{6,7},{7,6},{8,9},{9,8},{10,11... | collective-permute-start | bytes 3145736 | tf_op jit(solution)/shard_map/ppermute | solution.py:279
  23.3 18.6 %collective-permute-start.5 = (f32[64,4096]{1,0:T(8,128)}, f32[64,4096]{1,0:T(8,128)S(1)}, u32[]{:S(2)}, u32[]{:S(2)}) collective-permute-start(f32[64,4096]{1,0:T(8,128)} %bitcast.8), channel_id=1, source_target_pairs={{0,4},{1,3},{2,6},{3,1},{4,0},{5,7},{6,2},{7,5},{8,12},{9,11},{10,... | collective-permute-start | bytes 3145736 | tf_op jit(solution)/shard_map/ppermute | solution.py:302
  24.8 16.4 %collective-permute-start.11 = (f32[640,256]{1,0:T(8,128)S(1)}, f32[640,256]{1,0:T(8,128)S(1)}, u32[]{:S(2)}, u32[]{:S(2)}) collective-permute-start(f32[640,256]{1,0:T(8,128)S(1)} %collective-permute-done.4.refs_5_), channel_id=1, source_target_pairs={{0,16},{16,24},{24,8},{8,0},{1,17},{17,25},{25,9},{9,1},{2,18},{18... | collective-permute-start | bytes 1966088 | tf_op jit(solution)/shard_map/ppermute | solution.py:284
  28.1 21.4 %collective-permute-start.6 = (f32[64,4096]{1,0:T(8,128)}, f32[64,4096]{1,0:T(8,128)S(1)}, u32[]{:S(2)}, u32[]{:S(2)}) collective-permute-start(f32[64,4096]{1,0:T(8,128)} %bitcast.4), channel_id=1, source_target_pairs={{0,4},{1,3},{2,6},{3,1},{4,0},{5,7},{6,2},{7,5},{8,12},{9,11},{10,... | collective-permute-start | bytes 3145736 | tf_op jit(solution)/shard_map/ppermute | solution.py:302
  30.5 30.3 %collective-permute-start.18 = (f32[128,2048]{1,0:T(8,128)S(1)}, f32[128,2048]{1,0:T(8,128)S(1)}, u32[]{:S(2)}, u32[]{:S(2)}) collective-permute-start(f32[128,2048]{1,0:T(8,128)S(1)} %pad_maximum_fusion.1), channel_id=1, source_target_pairs={{0,4},{1,3},{2,6},{3,1},{4,0},{5,7},{6,2},{7,5},{8,12},{9,11},{10,... | collective-permute-start | bytes 3145736 | tf_op jit(solution)/shard_map/ppermute | solution.py:302
  41.3 9.2 %collective-permute-start.8 = (f32[64,4096]{1,0:T(8,128)S(1)}, f32[64,4096]{1,0:T(8,128)S(1)}, u32[]{:S(2)}, u32[]{:S(2)}) collective-permute-start(f32[64,4096]{1,0:T(8,128)S(1)} %collective-permute-done.1.refs_5_), channel_id=1, source_target_pairs={{0,1},{1,0},{2,3},{3,2},{4,5},{5,4},{6,7},{7,6},{8,9},{9,8},{10,11... | collective-permute-start | bytes 3145736 | tf_op jit(solution)/shard_map/ppermute | solution.py:279
  41.4 9.1 %collective-permute-start.13 = (f32[768,256]{1,0:T(8,128)S(1)}, f32[768,256]{1,0:T(8,128)S(1)}, u32[]{:S(2)}, u32[]{:S(2)}) collective-permute-start(f32[768,256]{1,0:T(8,128)S(1)} %pad_maximum_fusion.2), channel_id=1, source_target_pairs={{0,1},{1,0},{2,3},{3,2},{4,5},{5,4},{6,7},{7,6},{8,9},{9,8},{10,11... | collective-permute-start | bytes 2359304 | tf_op jit(solution)/shard_map/ppermute | solution.py:279
  41.9 17.6 %collective-permute-start.12 = (f32[640,256]{1,0:T(8,128)S(1)}, f32[640,256]{1,0:T(8,128)S(1)}, u32[]{:S(2)}, u32[]{:S(2)}) collective-permute-start(f32[640,256]{1,0:T(8,128)S(1)} %collective-permute-done.11.refs_6_), channel_id=1, source_target_pairs={{0,16},{16,24},{24,8},{8,0},{1,17},{17,25},{25,9},{9,1},{2,18},{18... | collective-permute-start | bytes 1966088 | tf_op jit(solution)/shard_map/ppermute | solution.py:284
  49.6 2.4 %collective-permute-start.10 = (f32[32,4096]{1,0:T(8,128)S(1)}, f32[32,4096]{1,0:T(8,128)S(1)}, u32[]{:S(2)}, u32[]{:S(2)}) collective-permute-start(f32[32,4096]{1,0:T(8,128)S(1)} %get-tuple-element.59), channel_id=1, source_target_pairs={{0,1},{1,0},{2,3},{3,2},{4,5},{5,4},{6,7},{7,6},{8,9},{9,8},{10,11... | collective-permute-start | bytes 1572872 | tf_op jit(solution)/shard_map/ppermute | solution.py:279
  50.4 2.3 %collective-permute-start.9 = (f32[32,4096]{1,0:T(8,128)S(1)}, f32[32,4096]{1,0:T(8,128)S(1)}, u32[]{:S(2)}, u32[]{:S(2)}) collective-permute-start(f32[32,4096]{1,0:T(8,128)S(1)} %get-tuple-element.60), channel_id=1, source_target_pairs={{0,1},{1,0},{2,3},{3,2},{4,5},{5,4},{6,7},{7,6},{8,9},{9,8},{10,11... | collective-permute-start | bytes 1572872 | tf_op jit(solution)/shard_map/ppermute | solution.py:279
  59.6 3.2 %copy-start.3 = (f32[128,512]{1,0:T(8,128)S(1)}, f32[128,512]{1,0:T(8,128)}, u32[]{:S(2)}) copy-start(f32[128,512]{1,0:T(8,128)} %refs_0_.3) | copy-start | bytes 786436
  59.6 3.2 %copy-start.4 = (f32[128,512]{1,0:T(8,128)S(1)}, f32[128,512]{1,0:T(8,128)}, u32[]{:S(2)}) copy-start(f32[128,512]{1,0:T(8,128)} %refs_1_.3) | copy-start | bytes 786436
  59.6 3.2 %copy-start.5 = (f32[128,512]{1,0:T(8,128)S(1)}, f32[128,512]{1,0:T(8,128)}, u32[]{:S(2)}) copy-start(f32[128,512]{1,0:T(8,128)} %refs_2_.3) | copy-start | bytes 786436
  59.6 3.1 %copy-start.6 = (f32[128,256]{1,0:T(8,128)S(1)}, f32[128,256]{1,0:T(8,128)}, u32[]{:S(2)}) copy-start(f32[128,256]{1,0:T(8,128)} %refs_3_.3) | copy-start | bytes 393220
  59.6 3.1 %copy-start.7 = (f32[128,256]{1,0:T(8,128)S(1)}, f32[128,256]{1,0:T(8,128)}, u32[]{:S(2)}) copy-start(f32[128,256]{1,0:T(8,128)} %refs_4_.3) | copy-start | bytes 393220
  59.6 1.8 %collective-permute-start.14 = (f32[384,256]{1,0:T(8,128)S(1)}, f32[384,256]{1,0:T(8,128)S(1)}, u32[]{:S(2)}, u32[]{:S(2)}) collective-permute-start(f32[384,256]{1,0:T(8,128)S(1)} %slice.23), channel_id=1, source_target_pairs={{0,1},{1,0},{2,3},{3,2},{4,5},{5,4},{6,7},{7,6},{8,9},{9,8},{10,11... | collective-permute-start | bytes 1179656 | tf_op jit(solution)/shard_map/ppermute | solution.py:279
  59.9 5.8 %copy-start = (f32[4096,256]{1,0:T(8,128)S(1)}, f32[4096,256]{1,0:T(8,128)}, u32[]{:S(2)}) copy-start(f32[4096,256]{1,0:T(8,128)} %refs_21_.1) | copy-start | bytes 12582916
  59.9 5.8 %copy-start.1 = (f32[4096,64]{0,1:T(8,128)S(1)}, f32[4096,64]{0,1:T(8,128)}, u32[]{:S(2)}) copy-start(f32[4096,64]{0,1:T(8,128)} %param.12) | copy-start | bytes 3145732
  59.9 5.8 %copy-start.2 = (f32[4096,64]{0,1:T(8,128)S(1)}, f32[4096,64]{0,1:T(8,128)}, u32[]{:S(2)}) copy-start(f32[4096,64]{0,1:T(8,128)} %param.11) | copy-start | bytes 3145732
  59.9 14.9 %collective-permute-start.15 = (f32[128,2048]{1,0:T(8,128)S(1)}, f32[128,2048]{1,0:T(8,128)S(1)}, u32[]{:S(2)}, u32[]{:S(2)}) collective-permute-start(f32[128,2048]{1,0:T(8,128)S(1)} %pad_maximum_fusion), channel_id=1, source_target_pairs={{0,4},{1,3},{2,6},{3,1},{4,0},{5,7},{6,2},{7,5},{8,12},{9,11},{10,... | collective-permute-start | bytes 3145736 | tf_op jit(solution)/shard_map/ppermute | solution.py:302
  61.5 4.1 %collective-permute-start.19 = (f32[64,2048]{1,0:T(8,128)S(1)}, f32[64,2048]{1,0:T(8,128)S(1)}, u32[]{:S(2)}, u32[]{:S(2)}) collective-permute-start(f32[64,2048]{1,0:T(8,128)S(1)} %get-tuple-element.56), channel_id=1, source_target_pairs={{0,1},{1,0},{2,3},{3,2},{4,5},{5,4},{6,7},{7,6},{8,9},{9,8},{10,11... | collective-permute-start | bytes 1572872 | tf_op jit(solution)/shard_map/ppermute | solution.py:279
  61.7 3.9 %collective-permute-start.20 = (f32[64,2048]{1,0:T(8,128)S(1)}, f32[64,2048]{1,0:T(8,128)S(1)}, u32[]{:S(2)}, u32[]{:S(2)}) collective-permute-start(f32[64,2048]{1,0:T(8,128)S(1)} %get-tuple-element.55), channel_id=1, source_target_pairs={{0,1},{1,0},{2,3},{3,2},{4,5},{5,4},{6,7},{7,6},{8,9},{9,8},{10,11... | collective-permute-start | bytes 1572872 | tf_op jit(solution)/shard_map/ppermute | solution.py:279
  62.2 3.5 %collective-permute-start.16 = (f32[32,4096]{1,0:T(8,128)S(1)}, f32[32,4096]{1,0:T(8,128)S(1)}, u32[]{:S(2)}, u32[]{:S(2)}) collective-permute-start(f32[32,4096]{1,0:T(8,128)S(1)} %get-tuple-element.58), channel_id=1, source_target_pairs={{0,1},{1,0},{2,3},{3,2},{4,5},{5,4},{6,7},{7,6},{8,9},{9,8},{10,11... | collective-permute-start | bytes 1572872 | tf_op jit(solution)/shard_map/ppermute | solution.py:279
  62.4 3.4 %collective-permute-start.17 = (f32[32,4096]{1,0:T(8,128)S(1)}, f32[32,4096]{1,0:T(8,128)S(1)}, u32[]{:S(2)}, u32[]{:S(2)}) collective-permute-start(f32[32,4096]{1,0:T(8,128)S(1)} %get-tuple-element.57), channel_id=1, source_target_pairs={{0,1},{1,0},{2,3},{3,2},{4,5},{5,4},{6,7},{7,6},{8,9},{9,8},{10,11... | collective-permute-start | bytes 1572872 | tf_op jit(solution)/shard_map/ppermute | solution.py:279
  74.8 2.7 %collective-permute-start.21 = (f32[128,2048]{1,0:T(8,128)S(1)}, f32[128,2048]{1,0:T(8,128)S(1)}, u32[]{:S(2)}, u32[]{:S(2)}) collective-permute-start(f32[128,2048]{1,0:T(8,128)S(1)} %collective-permute-done.15.panel), channel_id=1, source_target_pairs={{0,1},{1,0},{2,3},{3,2},{4,5},{5,4},{6,7},{7,6},{8,9},{9,8},{10,11... | collective-permute-start | bytes 3145736 | tf_op jit(solution)/shard_map/ppermute | solution.py:279

commit v9 on v8

--- a/solution.py
+++ b/solution.py
@@ -14,7 +14,7 @@
 INNER = 8
 CORE, ACROSS, UP = 1, 2, 4
 FIRST, SECOND = 0, 1
-ONE, OTHER = (ACROSS, UP), (UP, ACROSS)
+ONE, OTHER = (UP, ACROSS), (ACROSS, UP)
 
 
 def beyond(masks):

time: 79.3 us -> 79.3 us (level)
  no operation moved by 1% of the time
where the time goes in v9:
time: 79.3 us; the launch traced here: 79.2 us
  waiting for transfers between devices  41.2 us (52%)
  starting transfers between devices  21.2 us (27%)
  Pallas kernels  15.2 us (19%)
  between operations  0.84 us (1%)
    ppermute x3, waiting for transfers between devices, onward(): return lax.ppermute(value, 'row', list(zip(ring, ring[1:] + ring[:1])))  21.5 us
    ppermute x6, waiting for transfers between devices, cross(): lax.ppermute(value, 'col', [(i, i ^ masks[i % 2]) for i in range(col_coun...  15.2 us
    ppermute x3, starting transfers between devices, onward(): return lax.ppermute(value, 'row', list(zip(ring, ring[1:] + ring[:1])))  9.24 us
    ppermute x6, starting transfers between devices, cross(): lax.ppermute(value, 'col', [(i, i ^ masks[i % 2]) for i in range(col_coun...  8.78 us
    pallas_call x1, Pallas kernels, update(): pl.pallas_call(functools.partial(update_kernel, len(near), len(far), tile...  7.42 us
    ppermute x13, waiting for transfers between devices, swap(): return lax.ppermute(value, 'col', [(i, i ^ bit) for i in range(col_count)])  4.6 us
    ppermute x13, starting transfers between devices, swap(): return lax.ppermute(value, 'col', [(i, i ^ bit) for i in range(col_count)])  3.2 us
    pallas_call x1, Pallas kernels, solve(): pl.pallas_call(functools.partial(solve_kernel, steps, block), out_shape=o...  2.86 us
  transfers between devices with their start and end apart: 22, of which 13 were waited for; matrix products, arithmetic and copies ran while one was open for 1% of the time, Pallas kernels for 17%

profile of v9, /device:TPU:0, one launch (start us, length us, event | category | flops | bytes accessed | tf_op | source)
XLA Modules:
  0.0 79.2 jit_solution(15572570771605359822)
XLA Ops:
  0.6 3.0 %collective-permute-start = (f32[64,4096]{1,0:T(8,128)}, f32[64,4096]{1,0:T(8,128)S(1)}, u32[]{:S(2)}, u32[]{:S(2)}) collective-permute-start(f32[64,4096]{1,0:T(8,128)} %bitcast.6), channel_id=1, source_target_pairs={{0,4},{1,3},{2,6},{3,1},{4,0},{5,7},{6,2},{7,5},{8,12},{9,11},{10,... | collective-permute-start | bytes 3145736 | tf_op jit(solution)/shard_map/ppermute | solution.py:302
  3.7 0.0 collective-permute-start.2
  3.7 0.5 collective-permute-start.3
  4.2 2.1 %shard_map.103 = f32[640,256]{1,0:T(8,128)} custom-call(f32[128,512]{1,0:T(8,128)} %refs_0_.3, f32[128,512]{1,0:T(8,128)} %refs_1_.3, f32[128,512]{1,0:T(8,128)} %refs_2_.3, f32[128,256]{1,0:T(8,128)} %refs_3_.3, f32[128,256]{1,0:T(8,128)} %refs_4_.3), custom_call_target="tpu_custom_call" | custom-call | flops 1024 | bytes 1024 | tf_op jit(solution)/shard_map/pallas_call | solution.py:58
  6.3 2.6 %collective-permute-start.4 = (f32[640,256]{1,0:T(8,128)}, f32[640,256]{1,0:T(8,128)S(1)}, u32[]{:S(2)}, u32[]{:S(2)}) collective-permute-start(f32[640,256]{1,0:T(8,128)} %shard_map.103), channel_id=1, source_target_pairs={{0,16},{16,24},{24,8},{8,0},{1,17},{17,25},{25,9},{9,1},{2,18},{18... | collective-permute-start | bytes 1966088 | tf_op jit(solution)/shard_map/ppermute | solution.py:284
  8.9 0.5 collective-permute-start.1
  9.4 7.3 %collective-permute-done.refs_4_ = f32[64,4096]{1,0:T(8,128)S(1)} collective-permute-done((f32[64,4096]{1,0:T(8,128)}, f32[64,4096]{1,0:T(8,128)S(1)}, u32[]{:S(2)}, u32[]{:S(2)}) %collective-permute-start) | collective-permute-done | bytes 1048608 | tf_op jit(solution)/shard_map/ppermute | solution.py:302
  16.7 0.0 collective-permute-start.7
  16.7 6.7 %collective-permute-done.4.refs_5_ = f32[640,256]{1,0:T(8,128)S(1)} collective-permute-done((f32[640,256]{1,0:T(8,128)}, f32[640,256]{1,0:T(8,128)S(1)}, u32[]{:S(2)}, u32[]{:S(2)}) %collective-permute-start.4) | collective-permute-done | bytes 655392 | tf_op jit(solution)/shard_map/ppermute | solution.py:284
  23.3 0.0 collective-permute-done.2.refs_2_
  23.3 0.0 collective-permute-done.3.refs_3_
  23.3 1.5 %collective-permute-start.5 = (f32[64,4096]{1,0:T(8,128)}, f32[64,4096]{1,0:T(8,128)S(1)}, u32[]{:S(2)}, u32[]{:S(2)}) collective-permute-start(f32[64,4096]{1,0:T(8,128)} %bitcast.8), channel_id=1, source_target_pairs={{0,2},{1,5},{2,0},{3,7},{4,6},{5,1},{6,4},{7,3},{8,10},{9,13},{10,... | collective-permute-start | bytes 3145736 | tf_op jit(solution)/shard_map/ppermute | solution.py:302
  24.8 3.3 %collective-permute-start.11 = (f32[640,256]{1,0:T(8,128)S(1)}, f32[640,256]{1,0:T(8,128)S(1)}, u32[]{:S(2)}, u32[]{:S(2)}) collective-permute-start(f32[640,256]{1,0:T(8,128)S(1)} %collective-permute-done.4.refs_5_), channel_id=1, source_target_pairs={{0,16},{16,24},{24,8},{8,0},{1,17},{17,25},{25,9},{9,1},{2,18},{18... | collective-permute-start | bytes 1966088 | tf_op jit(solution)/shard_map/ppermute | solution.py:284
  28.1 0.6 collective-permute-start.6
  28.8 1.7 %collective-permute-done.1.refs_5_ = f32[64,4096]{1,0:T(8,128)S(1)} collective-permute-done((f32[64,4096]{1,0:T(8,128)}, f32[64,4096]{1,0:T(8,128)S(1)}, u32[]{:S(2)}, u32[]{:S(2)}) %collective-permute-start.1) | collective-permute-done | bytes 1048608 | tf_op jit(solution)/shard_map/ppermute | solution.py:302
  30.5 0.1 pad_maximum_fusion.1
  30.6 2.7 %collective-permute-start.18 = (f32[128,2048]{1,0:T(8,128)S(1)}, f32[128,2048]{1,0:T(8,128)S(1)}, u32[]{:S(2)}, u32[]{:S(2)}) collective-permute-start(f32[128,2048]{1,0:T(8,128)S(1)} %pad_maximum_fusion.1), channel_id=1, source_target_pairs={{0,2},{1,5},{2,0},{3,7},{4,6},{5,1},{6,4},{7,3},{8,10},{9,13},{10,... | collective-permute-start | bytes 3145736 | tf_op jit(solution)/shard_map/ppermute | solution.py:302
  33.3 8.0 %collective-permute-done.11.refs_6_ = f32[640,256]{1,0:T(8,128)S(1)} collective-permute-done((f32[640,256]{1,0:T(8,128)S(1)}, f32[640,256]{1,0:T(8,128)S(1)}, u32[]{:S(2)}, u32[]{:S(2)}) %collective-permute-start.11) | collective-permute-done | bytes 655392 | tf_op jit(solution)/shard_map/ppermute | solution.py:284
  41.3 0.0 collective-permute-start.8
  41.3 0.1 pad_maximum_fusion.2
  41.4 0.0 collective-permute-done.7.refs_6_
  41.4 0.6 collective-permute-start.13
  41.9 0.0 collective-permute-done.5.refs_8_
  41.9 3.4 %collective-permute-start.12 = (f32[640,256]{1,0:T(8,128)S(1)}, f32[640,256]{1,0:T(8,128)S(1)}, u32[]{:S(2)}, u32[]{:S(2)}) collective-permute-start(f32[640,256]{1,0:T(8,128)S(1)} %collective-permute-done.11.refs_6_), channel_id=1, source_target_pairs={{0,16},{16,24},{24,8},{8,0},{1,17},{17,25},{25,9},{9,1},{2,18},{18... | collective-permute-start | bytes 1966088 | tf_op jit(solution)/shard_map/ppermute | solution.py:284
  45.3 0.1 fusion.2
  45.4 4.2 %collective-permute-done.6.refs_9_ = f32[64,4096]{1,0:T(8,128)S(1)} collective-permute-done((f32[64,4096]{1,0:T(8,128)}, f32[64,4096]{1,0:T(8,128)S(1)}, u32[]{:S(2)}, u32[]{:S(2)}) %collective-permute-start.6) | collective-permute-done | bytes 1048608 | tf_op jit(solution)/shard_map/ppermute | solution.py:302
  49.6 0.9 %collective-permute-start.10 = (f32[32,4096]{1,0:T(8,128)S(1)}, f32[32,4096]{1,0:T(8,128)S(1)}, u32[]{:S(2)}, u32[]{:S(2)}) collective-permute-start(f32[32,4096]{1,0:T(8,128)S(1)} %get-tuple-element.59), channel_id=1, source_target_pairs={{0,1},{1,0},{2,3},{3,2},{4,5},{5,4},{6,7},{7,6},{8,9},{9,8},{10,11... | collective-permute-start | bytes 1572872 | tf_op jit(solution)/shard_map/ppermute | solution.py:279
  50.5 0.0 collective-permute-done.13.refs_8_
  50.5 0.0 collective-permute-start.9
  50.5 0.0 collective-permute-done.8.refs_7_
  50.5 1.5 %collective-permute-done.10.refs_11_ = f32[32,4096]{1,0:T(8,128)S(1)} collective-permute-done((f32[32,4096]{1,0:T(8,128)S(1)}, f32[32,4096]{1,0:T(8,128)S(1)}, u32[]{:S(2)}, u32[]{:S(2)}) %collective-permute-start.10) | collective-permute-done | bytes 524320 | tf_op jit(solution)/shard_map/ppermute | solution.py:279
  52.0 0.7 collective-permute-done.9.refs_10_
  52.8 6.8 %collective-permute-done.12.refs_7_ = f32[640,256]{1,0:T(8,128)S(1)} collective-permute-done((f32[640,256]{1,0:T(8,128)S(1)}, f32[640,256]{1,0:T(8,128)S(1)}, u32[]{:S(2)}, u32[]{:S(2)}) %collective-permute-start.12) | collective-permute-done | bytes 655392 | tf_op jit(solution)/shard_map/ppermute | solution.py:284
  59.6 0.0 copy-start.3
  59.6 0.0 copy-start.4
  59.6 0.0 copy-start.5
  59.6 0.0 copy-start.6
  59.6 0.0 copy-start.7
  59.6 0.1 collective-permute-start.14
  59.8 0.1 pad_maximum_fusion
  59.9 0.0 copy-start
  59.9 0.0 copy-start.1
  59.9 0.0 copy-start.2
  59.9 0.4 collective-permute-start.15
  60.4 0.4 collective-permute-done.18.refs_14_
  60.8 0.6 collective-permute-done.14.refs_9_
  61.4 0.1 fusion
  61.5 0.2 collective-permute-start.19
  61.7 0.4 collective-permute-start.20
  62.1 0.1 fusion.1
  62.2 0.2 collective-permute-start.16
  62.4 0.4 collective-permute-start.17
  62.8 0.0 copy-done.3
  62.8 2.9 %shard_map.104 = (bf16[768,256]{1,0:T(8,128)(2,1)S(1)}, bf16[768,256]{1,0:T(8,128)(2,1)S(1)}, bf16[256,256]{1,0:T(8,128)(2,1)S(1)}, bf16[256,256]{1,0:T(8,128)(2...) custom-call(f32[128,512]{1,0:T(8,128)S(1)} %copy-done.3, f32[128,512]{1,0:T(8,128)S(1)} %copy-done.4, ...), custom_call_target="tpu_custom_call" | custom-call | flops 1024 | bytes 1024 | tf_op jit(solution)/shard_map/pallas_call | solution.py:133
  65.6 0.0 collective-permute-done.19.refs_15_
  65.6 0.0 collective-permute-done.20.refs_16_
  65.7 0.0 collective-permute-done.16.refs_12_
  65.7 0.1 collective-permute-done.17.refs_13_
  65.8 7.4 %shard_map.105 = (f32[4096,256]{1,0:T(8,128)}, f32[2048,256]{1,0:T(8,128)S(1)}) custom-call(f32[64,4096]{1,0:T(8,128)S(1)} %bitcast.9, f32[64,4096]{1,0:T(8,128)S(1)} %bitcast.5, f32[64,4096]{1,0:T(8,128)S(1)} %collective-permute-done.2.refs_2_, f32[64,4096]{1,0:T(8,128)S(1)} %collective-permute-done.3.refs_3_, f32[64,4096]{1,0:T(8,128)S(1)} %collective-permute-done.refs_4_, ...), custom_call_target="tpu_custom_call" | custom-call | flops 1024 | bytes 1024 | tf_op jit(solution)/shard_map/pallas_call | solution.py:204
  73.2 1.6 %collective-permute-done.15.panel = f32[128,2048]{1,0:T(8,128)S(1)} collective-permute-done((f32[128,2048]{1,0:T(8,128)S(1)}, f32[128,2048]{1,0:T(8,128)S(1)}, u32[]{:S(2)}, u32[]{:S(2)}) %collective-permute-start.15) | collective-permute-done | bytes 1048608 | tf_op jit(solution)/shard_map/ppermute | solution.py:302
  74.8 0.0 collective-permute-start.21
  74.8 1.1 %shard_map.106.rest = f32[2048,256]{1,0:T(8,128)S(1)} custom-call(f32[128,2048]{1,0:T(8,128)S(1)} %collective-permute-done.15.panel, bf16[256,256]{1,0:T(8,128)(2,1)S(1)} %get-tuple-element.50.refs_19_.high, bf16[256,256]{1,0:T(8,128)(2,1)S(1)} %get-tuple-element.51.refs_20_.low, ...), custom_call_target="tpu_custom_call", output_to_operand_aliasing={{}: (3, {})} | custom-call | flops 1024 | bytes 1024 | tf_op jit(solution)/shard_map/pallas_call | solution.py:232
  75.9 1.6 %collective-permute-done.21.panel = f32[128,2048]{1,0:T(8,128)S(1)} collective-permute-done((f32[128,2048]{1,0:T(8,128)S(1)}, f32[128,2048]{1,0:T(8,128)S(1)}, u32[]{:S(2)}, u32[]{:S(2)}) %collective-permute-start.21) | collective-permute-done | bytes 1048608 | tf_op jit(solution)/shard_map/ppermute | solution.py:279
  77.5 1.7 %shard_map.107 = f32[4096,256]{1,0:T(8,128)} custom-call(f32[128,2048]{1,0:T(8,128)S(1)} %collective-permute-done.21.panel, bf16[256,256]{1,0:T(8,128)(2,1)S(1)} %get-tuple-element.50.refs_19_.high, bf16[256,256]{1,0:T(8,128)(2,1)S(1)} %get-tuple-element.51.refs_20_.low, f32[2048,256]{1,0:T(8,128)S(1)} %shard_map.106.rest, ...), custom_call_target="tpu_custom_call", output_to_operand_aliasing={{}: (4, {})} | custom-call | flops 1024 | bytes 1024 | tf_op jit(solution)/shard_map/pallas_call | solution.py:263
  (14 shorter events, 0.2 us)
Async XLA Ops:
  0.6 16.0 %collective-permute-start = (f32[64,4096]{1,0:T(8,128)}, f32[64,4096]{1,0:T(8,128)S(1)}, u32[]{:S(2)}, u32[]{:S(2)}) collective-permute-start(f32[64,4096]{1,0:T(8,128)} %bitcast.6), channel_id=1, source_target_pairs={{0,4},{1,3},{2,6},{3,1},{4,0},{5,7},{6,2},{7,5},{8,12},{9,11},{10,... | collective-permute-start | bytes 3145736 | tf_op jit(solution)/shard_map/ppermute | solution.py:302
  3.7 19.7 %collective-permute-start.2 = (f32[64,4096]{1,0:T(8,128)}, f32[64,4096]{1,0:T(8,128)S(1)}, u32[]{:S(2)}, u32[]{:S(2)}) collective-permute-start(f32[64,4096]{1,0:T(8,128)} %bitcast.7), channel_id=1, source_target_pairs={{0,1},{1,0},{2,3},{3,2},{4,5},{5,4},{6,7},{7,6},{8,9},{9,8},{10,11... | collective-permute-start | bytes 3145736 | tf_op jit(solution)/shard_map/ppermute | solution.py:279
  3.7 19.7 %collective-permute-start.3 = (f32[64,4096]{1,0:T(8,128)}, f32[64,4096]{1,0:T(8,128)S(1)}, u32[]{:S(2)}, u32[]{:S(2)}) collective-permute-start(f32[64,4096]{1,0:T(8,128)} %bitcast.2), channel_id=1, source_target_pairs={{0,1},{1,0},{2,3},{3,2},{4,5},{5,4},{6,7},{7,6},{8,9},{9,8},{10,11... | collective-permute-start | bytes 3145736 | tf_op jit(solution)/shard_map/ppermute | solution.py:279
  6.3 17.1 %collective-permute-start.4 = (f32[640,256]{1,0:T(8,128)}, f32[640,256]{1,0:T(8,128)S(1)}, u32[]{:S(2)}, u32[]{:S(2)}) collective-permute-start(f32[640,256]{1,0:T(8,128)} %shard_map.103), channel_id=1, source_target_pairs={{0,16},{16,24},{24,8},{8,0},{1,17},{17,25},{25,9},{9,1},{2,18},{18... | collective-permute-start | bytes 1966088 | tf_op jit(solution)/shard_map/ppermute | solution.py:284
  8.9 21.6 %collective-permute-start.1 = (f32[64,4096]{1,0:T(8,128)}, f32[64,4096]{1,0:T(8,128)S(1)}, u32[]{:S(2)}, u32[]{:S(2)}) collective-permute-start(f32[64,4096]{1,0:T(8,128)} %bitcast.3), channel_id=1, source_target_pairs={{0,4},{1,3},{2,6},{3,1},{4,0},{5,7},{6,2},{7,5},{8,12},{9,11},{10,... | collective-permute-start | bytes 3145736 | tf_op jit(solution)/shard_map/ppermute | solution.py:302
  16.7 24.7 %collective-permute-start.7 = (f32[64,4096]{1,0:T(8,128)S(1)}, f32[64,4096]{1,0:T(8,128)S(1)}, u32[]{:S(2)}, u32[]{:S(2)}) collective-permute-start(f32[64,4096]{1,0:T(8,128)S(1)} %collective-permute-done.refs_4_), channel_id=1, source_target_pairs={{0,1},{1,0},{2,3},{3,2},{4,5},{5,4},{6,7},{7,6},{8,9},{9,8},{10,11... | collective-permute-start | bytes 3145736 | tf_op jit(solution)/shard_map/ppermute | solution.py:279
  23.3 18.6 %collective-permute-start.5 = (f32[64,4096]{1,0:T(8,128)}, f32[64,4096]{1,0:T(8,128)S(1)}, u32[]{:S(2)}, u32[]{:S(2)}) collective-permute-start(f32[64,4096]{1,0:T(8,128)} %bitcast.8), channel_id=1, source_target_pairs={{0,2},{1,5},{2,0},{3,7},{4,6},{5,1},{6,4},{7,3},{8,10},{9,13},{10,... | collective-permute-start | bytes 3145736 | tf_op jit(solution)/shard_map/ppermute | solution.py:302
  24.8 16.4 %collective-permute-start.11 = (f32[640,256]{1,0:T(8,128)S(1)}, f32[640,256]{1,0:T(8,128)S(1)}, u32[]{:S(2)}, u32[]{:S(2)}) collective-permute-start(f32[640,256]{1,0:T(8,128)S(1)} %collective-permute-done.4.refs_5_), channel_id=1, source_target_pairs={{0,16},{16,24},{24,8},{8,0},{1,17},{17,25},{25,9},{9,1},{2,18},{18... | collective-permute-start | bytes 1966088 | tf_op jit(solution)/shard_map/ppermute | solution.py:284
  28.1 21.4 %collective-permute-start.6 = (f32[64,4096]{1,0:T(8,128)}, f32[64,4096]{1,0:T(8,128)S(1)}, u32[]{:S(2)}, u32[]{:S(2)}) collective-permute-start(f32[64,4096]{1,0:T(8,128)} %bitcast.4), channel_id=1, source_target_pairs={{0,2},{1,5},{2,0},{3,7},{4,6},{5,1},{6,4},{7,3},{8,10},{9,13},{10,... | collective-permute-start | bytes 3145736 | tf_op jit(solution)/shard_map/ppermute | solution.py:302
  30.6 30.2 %collective-permute-start.18 = (f32[128,2048]{1,0:T(8,128)S(1)}, f32[128,2048]{1,0:T(8,128)S(1)}, u32[]{:S(2)}, u32[]{:S(2)}) collective-permute-start(f32[128,2048]{1,0:T(8,128)S(1)} %pad_maximum_fusion.1), channel_id=1, source_target_pairs={{0,2},{1,5},{2,0},{3,7},{4,6},{5,1},{6,4},{7,3},{8,10},{9,13},{10,... | collective-permute-start | bytes 3145736 | tf_op jit(solution)/shard_map/ppermute | solution.py:302
  41.3 9.2 %collective-permute-start.8 = (f32[64,4096]{1,0:T(8,128)S(1)}, f32[64,4096]{1,0:T(8,128)S(1)}, u32[]{:S(2)}, u32[]{:S(2)}) collective-permute-start(f32[64,4096]{1,0:T(8,128)S(1)} %collective-permute-done.1.refs_5_), channel_id=1, source_target_pairs={{0,1},{1,0},{2,3},{3,2},{4,5},{5,4},{6,7},{7,6},{8,9},{9,8},{10,11... | collective-permute-start | bytes 3145736 | tf_op jit(solution)/shard_map/ppermute | solution.py:279
  41.4 9.1 %collective-permute-start.13 = (f32[768,256]{1,0:T(8,128)S(1)}, f32[768,256]{1,0:T(8,128)S(1)}, u32[]{:S(2)}, u32[]{:S(2)}) collective-permute-start(f32[768,256]{1,0:T(8,128)S(1)} %pad_maximum_fusion.2), channel_id=1, source_target_pairs={{0,1},{1,0},{2,3},{3,2},{4,5},{5,4},{6,7},{7,6},{8,9},{9,8},{10,11... | collective-permute-start | bytes 2359304 | tf_op jit(solution)/shard_map/ppermute | solution.py:279
  41.9 17.6 %collective-permute-start.12 = (f32[640,256]{1,0:T(8,128)S(1)}, f32[640,256]{1,0:T(8,128)S(1)}, u32[]{:S(2)}, u32[]{:S(2)}) collective-permute-start(f32[640,256]{1,0:T(8,128)S(1)} %collective-permute-done.11.refs_6_), channel_id=1, source_target_pairs={{0,16},{16,24},{24,8},{8,0},{1,17},{17,25},{25,9},{9,1},{2,18},{18... | collective-permute-start | bytes 1966088 | tf_op jit(solution)/shard_map/ppermute | solution.py:284
  49.6 2.4 %collective-permute-start.10 = (f32[32,4096]{1,0:T(8,128)S(1)}, f32[32,4096]{1,0:T(8,128)S(1)}, u32[]{:S(2)}, u32[]{:S(2)}) collective-permute-start(f32[32,4096]{1,0:T(8,128)S(1)} %get-tuple-element.59), channel_id=1, source_target_pairs={{0,1},{1,0},{2,3},{3,2},{4,5},{5,4},{6,7},{7,6},{8,9},{9,8},{10,11... | collective-permute-start | bytes 1572872 | tf_op jit(solution)/shard_map/ppermute | solution.py:279
  50.5 2.3 %collective-permute-start.9 = (f32[32,4096]{1,0:T(8,128)S(1)}, f32[32,4096]{1,0:T(8,128)S(1)}, u32[]{:S(2)}, u32[]{:S(2)}) collective-permute-start(f32[32,4096]{1,0:T(8,128)S(1)} %get-tuple-element.60), channel_id=1, source_target_pairs={{0,1},{1,0},{2,3},{3,2},{4,5},{5,4},{6,7},{7,6},{8,9},{9,8},{10,11... | collective-permute-start | bytes 1572872 | tf_op jit(solution)/shard_map/ppermute | solution.py:279
  59.6 3.2 %copy-start.3 = (f32[128,512]{1,0:T(8,128)S(1)}, f32[128,512]{1,0:T(8,128)}, u32[]{:S(2)}) copy-start(f32[128,512]{1,0:T(8,128)} %refs_0_.3) | copy-start | bytes 786436
  59.6 3.2 %copy-start.4 = (f32[128,512]{1,0:T(8,128)S(1)}, f32[128,512]{1,0:T(8,128)}, u32[]{:S(2)}) copy-start(f32[128,512]{1,0:T(8,128)} %refs_1_.3) | copy-start | bytes 786436
  59.6 3.2 %copy-start.5 = (f32[128,512]{1,0:T(8,128)S(1)}, f32[128,512]{1,0:T(8,128)}, u32[]{:S(2)}) copy-start(f32[128,512]{1,0:T(8,128)} %refs_2_.3) | copy-start | bytes 786436
  59.6 3.1 %copy-start.6 = (f32[128,256]{1,0:T(8,128)S(1)}, f32[128,256]{1,0:T(8,128)}, u32[]{:S(2)}) copy-start(f32[128,256]{1,0:T(8,128)} %refs_3_.3) | copy-start | bytes 393220
  59.6 3.1 %copy-start.7 = (f32[128,256]{1,0:T(8,128)S(1)}, f32[128,256]{1,0:T(8,128)}, u32[]{:S(2)}) copy-start(f32[128,256]{1,0:T(8,128)} %refs_4_.3) | copy-start | bytes 393220
  59.6 1.8 %collective-permute-start.14 = (f32[384,256]{1,0:T(8,128)S(1)}, f32[384,256]{1,0:T(8,128)S(1)}, u32[]{:S(2)}, u32[]{:S(2)}) collective-permute-start(f32[384,256]{1,0:T(8,128)S(1)} %slice.23), channel_id=1, source_target_pairs={{0,1},{1,0},{2,3},{3,2},{4,5},{5,4},{6,7},{7,6},{8,9},{9,8},{10,11... | collective-permute-start | bytes 1179656 | tf_op jit(solution)/shard_map/ppermute | solution.py:279
  59.9 5.8 %copy-start = (f32[4096,256]{1,0:T(8,128)S(1)}, f32[4096,256]{1,0:T(8,128)}, u32[]{:S(2)}) copy-start(f32[4096,256]{1,0:T(8,128)} %refs_21_.1) | copy-start | bytes 12582916
  59.9 5.8 %copy-start.1 = (f32[4096,64]{0,1:T(8,128)S(1)}, f32[4096,64]{0,1:T(8,128)}, u32[]{:S(2)}) copy-start(f32[4096,64]{0,1:T(8,128)} %param.12) | copy-start | bytes 3145732
  59.9 5.8 %copy-start.2 = (f32[4096,64]{0,1:T(8,128)S(1)}, f32[4096,64]{0,1:T(8,128)}, u32[]{:S(2)}) copy-start(f32[4096,64]{0,1:T(8,128)} %param.11) | copy-start | bytes 3145732
  59.9 14.9 %collective-permute-start.15 = (f32[128,2048]{1,0:T(8,128)S(1)}, f32[128,2048]{1,0:T(8,128)S(1)}, u32[]{:S(2)}, u32[]{:S(2)}) collective-permute-start(f32[128,2048]{1,0:T(8,128)S(1)} %pad_maximum_fusion), channel_id=1, source_target_pairs={{0,2},{1,5},{2,0},{3,7},{4,6},{5,1},{6,4},{7,3},{8,10},{9,13},{10,... | collective-permute-start | bytes 3145736 | tf_op jit(solution)/shard_map/ppermute | solution.py:302
  61.5 4.1 %collective-permute-start.19 = (f32[64,2048]{1,0:T(8,128)S(1)}, f32[64,2048]{1,0:T(8,128)S(1)}, u32[]{:S(2)}, u32[]{:S(2)}) collective-permute-start(f32[64,2048]{1,0:T(8,128)S(1)} %get-tuple-element.56), channel_id=1, source_target_pairs={{0,1},{1,0},{2,3},{3,2},{4,5},{5,4},{6,7},{7,6},{8,9},{9,8},{10,11... | collective-permute-start | bytes 1572872 | tf_op jit(solution)/shard_map/ppermute | solution.py:279
  61.7 3.9 %collective-permute-start.20 = (f32[64,2048]{1,0:T(8,128)S(1)}, f32[64,2048]{1,0:T(8,128)S(1)}, u32[]{:S(2)}, u32[]{:S(2)}) collective-permute-start(f32[64,2048]{1,0:T(8,128)S(1)} %get-tuple-element.55), channel_id=1, source_target_pairs={{0,1},{1,0},{2,3},{3,2},{4,5},{5,4},{6,7},{7,6},{8,9},{9,8},{10,11... | collective-permute-start | bytes 1572872 | tf_op jit(solution)/shard_map/ppermute | solution.py:279
  62.2 3.5 %collective-permute-start.16 = (f32[32,4096]{1,0:T(8,128)S(1)}, f32[32,4096]{1,0:T(8,128)S(1)}, u32[]{:S(2)}, u32[]{:S(2)}) collective-permute-start(f32[32,4096]{1,0:T(8,128)S(1)} %get-tuple-element.58), channel_id=1, source_target_pairs={{0,1},{1,0},{2,3},{3,2},{4,5},{5,4},{6,7},{7,6},{8,9},{9,8},{10,11... | collective-permute-start | bytes 1572872 | tf_op jit(solution)/shard_map/ppermute | solution.py:279
  62.4 3.4 %collective-permute-start.17 = (f32[32,4096]{1,0:T(8,128)S(1)}, f32[32,4096]{1,0:T(8,128)S(1)}, u32[]{:S(2)}, u32[]{:S(2)}) collective-permute-start(f32[32,4096]{1,0:T(8,128)S(1)} %get-tuple-element.57), channel_id=1, source_target_pairs={{0,1},{1,0},{2,3},{3,2},{4,5},{5,4},{6,7},{7,6},{8,9},{9,8},{10,11... | collective-permute-start | bytes 1572872 | tf_op jit(solution)/shard_map/ppermute | solution.py:279
  74.8 2.7 %collective-permute-start.21 = (f32[128,2048]{1,0:T(8,128)S(1)}, f32[128,2048]{1,0:T(8,128)S(1)}, u32[]{:S(2)}, u32[]{:S(2)}) collective-permute-start(f32[128,2048]{1,0:T(8,128)S(1)} %collective-permute-done.15.panel), channel_id=1, source_target_pairs={{0,1},{1,0},{2,3},{3,2},{4,5},{5,4},{6,7},{7,6},{8,9},{9,8},{10,11... | collective-permute-start | bytes 3145736 | tf_op jit(solution)/shard_map/ppermute | solution.py:279
